TPU v7x, 256 devices: a whole 4x4x8 slice. The times are simulated.
256 devices in a mesh: rows: 32 (over y_hi, z, core), pairs: 8 (over y_lo, x).
Axes of the slice: x: 4, y: 4 (y_hi: 2, y_lo: 2; y = y_hi * 2 + y_lo), z: 8, core: 2. Of those that a mesh axis runs over, the one named last changes fastest.
Arguments:
- loads: float32 [8192, 4096], P('rows', 'pairs'), may hold values from -6 to 6
- col_weights: float32 [4096], P('pairs'), may hold values from 0.3 to 3
- partner_offsets: int32 [2, 2], replicated, may hold values from 0 to 127
- skip_mask: int32 [2, 16], P(None, 'pairs'), may hold values 0 or 1
Outputs:
- rotated: float32 [8192, 4096], P('rows', 'pairs')
- column_power: float32 [4096], P('pairs')
All inputs are finite; a program needn't handle non-finite values. No bound on the sum of `skip_mask` on one device may be relied on, other than what follows from the above.
Results may differ from a plain program's by a relative error of at most 0.0003.
Values sent between devices are 32-bit elements; how exact they have to be, the bound alone decides.
No kernel may reach another device: no remote copies, remote signals or barrier semaphores. Data moves between devices by JAX's collectives and lax.ppermute only.
A program may use at most 128 MiB of HBM per device.

v0:
```python
import jax
import jax.numpy as jnp
from jax import lax
from jax.sharding import PartitionSpec as P

BLOCK = 128
STEPS = 2


precise = lax.Precision.HIGHEST


def shifted(x, axis, by):
    size = lax.axis_size(axis)
    pairs = [(i, i + by) for i in range(size) if 0 <= i + by < size]
    return lax.ppermute(x, axis, pairs)


def turn_columns(matrix, cosine_values, sine_values, offset):
    half_width = matrix.shape[-1] // 2
    left_part = matrix[..., :half_width]
    right_part = jnp.roll(matrix[..., half_width:], -offset, axis=-1)
    cosine_grid = cosine_values[:, None, :]
    sine_grid = sine_values[:, None, :]
    new_left = cosine_grid * left_part - sine_grid * right_part
    new_right = jnp.roll(sine_grid * left_part + cosine_grid * right_part, offset, axis=-1)
    return jnp.concatenate([new_left, new_right], axis=-1)


def rotate_pair(gram_matrix, offsets_step, skip_step):
    half_width = gram_matrix.shape[-1] // 2
    identity = jnp.broadcast_to(jnp.eye(2 * half_width, dtype=jnp.float32), gram_matrix.shape)
    turned = gram_matrix
    rotation = identity
    for step_round in range(offsets_step.shape[0]):
        offset = offsets_step[step_round]
        diagonal_values = jnp.diagonal(turned, axis1=1, axis2=2)
        first_norms = diagonal_values[:, :half_width]
        second_norms = jnp.roll(diagonal_values[:, half_width:], -offset, axis=1)
        coupling = jnp.diagonal(
            jnp.roll(turned[:, :half_width, half_width:], -offset, axis=2), axis1=1, axis2=2
        )
        half_gap = 0.5 * (second_norms - first_norms)
        gap_sign = jnp.where(half_gap >= 0.0, 1.0, -1.0)
        denominator = jnp.maximum(
            jnp.abs(half_gap) + jnp.sqrt(half_gap * half_gap + coupling * coupling),
            1e-06 * (first_norms + second_norms),
        )
        tangent = gap_sign * coupling / denominator
        cosine_values = 1.0 / jnp.sqrt(1.0 + tangent * tangent)
        sine_values = tangent * cosine_values
        turned = turn_columns(turned, cosine_values, sine_values, offset)
        turned = jnp.swapaxes(
            turn_columns(jnp.swapaxes(turned, 1, 2), cosine_values, sine_values, offset), 1, 2
        )
        rotation = turn_columns(rotation, cosine_values, sine_values, offset)
    unskipped = (skip_step == 0)[:, None, None]
    return (jnp.where(unskipped, rotation, identity), jnp.where(unskipped, turned, gram_matrix))


def whole_gram(joined):
    partial_gram = jnp.einsum(
        "prc,prd->pcd", joined, joined, precision=precise, preferred_element_type=jnp.float32
    )
    return lax.psum(partial_gram, "rows")


def next_gram(joined):
    gram_matrix = whole_gram(joined)
    return gram_matrix


def settle(upper_stack, lower_stack, incoming_upper, incoming_lower, position, last_index):
    head_upper = jnp.concatenate([upper_stack[:1], lower_stack[:1], upper_stack[1:-1]], axis=0)
    rest_upper = jnp.concatenate([incoming_upper[None], upper_stack[:-1]], axis=0)
    new_upper = jnp.where(position == 0, head_upper, rest_upper)
    tail_lower = jnp.concatenate([lower_stack[1:], upper_stack[-1:]], axis=0)
    rest_lower = jnp.concatenate([lower_stack[1:], incoming_lower[None]], axis=0)
    new_lower = jnp.where(position == last_index, tail_lower, rest_lower)
    return (new_upper, new_lower)


def move_all(upper_blocks, lower_blocks, diag_upper, diag_lower, position, last_index):
    incoming_upper = shifted(upper_blocks[-1], "pairs", 1)
    incoming_lower = shifted(lower_blocks[0], "pairs", -1)
    upper_blocks, lower_blocks = settle(
        upper_blocks, lower_blocks, incoming_upper, incoming_lower, position, last_index
    )
    return (upper_blocks, lower_blocks, diag_upper, diag_lower)


def per_device(loads, col_weights, partner_offsets, skip_mask):
    row_count = loads.shape[0]
    half_count = loads.shape[1] // (2 * BLOCK)
    weighted = loads * col_weights[None, :]
    stacked = weighted.reshape(row_count, 2, half_count, BLOCK).transpose(1, 2, 0, 3)
    upper_blocks = stacked[0]
    lower_blocks = stacked[1]
    position = lax.axis_index("pairs")
    last_index = lax.axis_size("pairs") - 1
    diag_upper = jnp.zeros((half_count, BLOCK, BLOCK), jnp.float32)
    diag_lower = jnp.zeros((half_count, BLOCK, BLOCK), jnp.float32)
    turned = jnp.zeros((half_count, 2 * BLOCK, 2 * BLOCK), jnp.float32)
    for step_index in range(STEPS):
        joined = jnp.concatenate([upper_blocks, lower_blocks], axis=-1)
        if step_index == 0:
            gram_matrix = whole_gram(joined)
        else:
            gram_matrix = next_gram(joined)
        rotation, turned = rotate_pair(
            gram_matrix, partner_offsets[step_index], skip_mask[step_index]
        )
        joined = jnp.einsum(
            "prc,pcd->prd", joined, rotation, precision=precise, preferred_element_type=jnp.float32
        )
        upper_blocks = joined[..., :BLOCK]
        lower_blocks = joined[..., BLOCK:]
        diag_upper = turned[:, :BLOCK, :BLOCK]
        diag_lower = turned[:, BLOCK:, BLOCK:]
        if step_index + 1 < STEPS:
            upper_blocks, lower_blocks, diag_upper, diag_lower = move_all(
                upper_blocks, lower_blocks, diag_upper, diag_lower, position, last_index
            )
    total_rows = row_count * lax.axis_size("rows")
    upper_power, lower_power = lax.psum(
        (
            jnp.sum(upper_blocks * upper_blocks, axis=1),
            jnp.sum(lower_blocks * lower_blocks, axis=1),
        ),
        "rows",
    )
    column_power = jnp.concatenate([upper_power.reshape(-1), lower_power.reshape(-1)]) / total_rows
    rotated = (
        jnp.stack([upper_blocks, lower_blocks])
        .transpose(2, 0, 1, 3)
        .reshape(row_count, 2 * half_count * BLOCK)
    )
    return (rotated, column_power)


def solution(mesh):
    in_specs = (P("rows", "pairs"), P("pairs"), P(), P(None, "pairs"))
    out_specs = (P("rows", "pairs"), P("pairs"))
    return jax.shard_map(
        per_device, mesh=mesh, in_specs=in_specs, out_specs=out_specs, check_vma=False
    )
```

profile of v0, /device:TPU:9, one launch (start us, length us, event | category | flops | bytes accessed | tf_op | source)
XLA Modules:
  0.0 742.7 jit_solution(13982182701009204397)
XLA Ops:
  7.2 1.2 copy.132
  8.5 0.8 broadcast_multiply_fusion
  9.3 0.2 copy.133
  9.5 1.9 fusion.7
  11.5 1.5 fusion.85
  17.9 0.8 compare_bitcast_fusion
  18.6 260.9 %all-reduce.4.cloned.1.call-done = f32[2,256,256]{2,1,0:T(8,128)} async-done(((f32[2,256,256]{2,1,0:T(8,128)}), f32[2,256,256]{2,1,0:T(8,128)}) %all-reduce.4.cloned.1.call-update) | async-done | bytes 524304 | tf_op jit(solution)/shard_map/psum | solution.py:65
  279.6 1.0 slice.196
  280.6 0.1 fusion.41
  280.7 4.6 copy.137
  285.3 1.8 gather_fusion.1
  287.2 17.2 %copy.135 = f32[2,256,256]{0,2,1:T(8,128)} copy(f32[2,256,256]{2,1,0:T(8,128)} %all-reduce.4.cloned.1.call-done) | data formatting | bytes 1048576 | tf_op jit(solution)/shard_map/psum | solution.py:65
  304.4 2.3 gather_fusion
  306.9 0.1 add_rsqrt_fusion.3
  307.0 0.1 copy.165
  307.2 0.1 broadcast_multiply_fusion.1
  307.3 0.1 copy.142
  307.4 0.2 multiply_add_fusion.5
  307.6 0.1 copy.140
  307.8 0.2 fusion.32
  307.9 0.1 copy.143
  308.1 0.2 fusion.21
  308.4 0.1 multiply_subtract_fusion.4
  308.5 0.1 fusion.19
  308.6 16.5 %copy.144 = f32[2,256,256]{0,2,1:T(8,128)} copy(f32[2,256,256]{2,1,0:T(8,128)S(1)} %maximum_bitcast_fusion.1) | data formatting | bytes 1048576 | tf_op jit(solution)/shard_map/transpose | solution.py:53
  325.2 2.3 gather_fusion.2
  327.5 0.1 copy.145
  327.6 0.2 fusion.40
  327.7 4.6 copy.146
  332.4 1.8 gather_fusion.3
  334.2 0.1 add_rsqrt_fusion.2
  334.3 0.1 fusion.18
  334.4 0.3 multiply_subtract_fusion.3
  334.7 0.1 fusion.16
  334.8 0.7 fusion
  335.6 3.1 collective-permute-start
  338.7 4.5 collective-permute-start.1
  343.2 0.8 collective-permute-done
  344.0 0.9 collective-permute-done.1
  344.9 1.5 fusion.6
  352.0 260.0 %all-reduce.6.cloned.1.call-done = f32[2,256,256]{1,2,0:T(8,128)} async-done(((f32[2,256,256]{1,2,0:T(8,128)}), f32[2,256,256]{1,2,0:T(8,128)}) %all-reduce.6.cloned.1.call-update) | async-done | bytes 524304 | tf_op jit(solution)/shard_map/psum | solution.py:65
  612.0 17.4 %copy.150 = f32[2,256,256]{0,2,1:T(8,128)} copy(f32[2,256,256]{1,2,0:T(8,128)} %all-reduce.6.cloned.1.call-done) | data formatting | bytes 1048576 | tf_op jit(solution)/shard_map/psum | solution.py:65
  629.3 2.3 gather_fusion.4
  631.8 7.6 %copy.152 = f32[2,128,128]{0,2,1:T(8,128)} copy(f32[2,128,128]{1,2,0:T(8,128)S(1)} %fusion.39) | data formatting | bytes 262144 | tf_op jit(solution)/shard_map/jit(_roll_dynamic)/dynamic_slice | solution.py:41
  639.4 1.8 gather_fusion.5
  641.3 0.1 add_rsqrt_fusion.1
  641.4 0.2 multiply_subtract_fusion.2
  641.7 0.1 fusion.14
  641.8 0.2 copy.154
  642.0 0.1 multiply_subtract_fusion.1
  642.2 0.1 fusion.11
  642.4 16.5 %copy.155 = f32[2,256,256]{0,2,1:T(8,128)} copy(f32[2,256,256]{2,1,0:T(8,128)S(1)} %maximum_bitcast_fusion.2) | data formatting | bytes 1048576 | tf_op jit(solution)/shard_map/transpose | solution.py:53
  658.9 2.3 gather_fusion.6
  661.3 0.2 fusion.38
  661.5 4.6 copy.157
  666.1 1.8 gather_fusion.7
  667.9 0.1 add_rsqrt_fusion
  668.1 0.3 multiply_subtract_fusion
  668.3 0.1 fusion.9
  668.4 0.7 fusion.3
  669.1 0.2 multiply_reduce_fusion.1
  669.3 1.0 copy.160
  670.3 65.0 %all-reduce = (f32[256]{0:T(256)S(1)}, f32[256]{0:T(256)S(1)}) all-reduce(f32[256]{0:T(256)S(1)} %bitcast.119, f32[256]{0:T(256)S(1)} %bitcast.118), channel_id=1, replica_groups=mesh['rows'=32,'pairs'=8] {'rows'}, use_global_device_ids=true, to_apply=%region_5.9 | all-reduce | flops 512 | bytes 4096 | tf_op jit(solution)/shard_map/psum | solution.py:125
  735.3 0.6 maximum_multiply_fusion
  (46 shorter events, 1.2 us)
Async XLA Ops:
  7.2 272.4 %all-reduce.4.cloned.1.call-start = ((), (), s32[]{:S(2)}) async-start(), calls=%async_computation | async-start | bytes 1048576 | tf_op jit(solution)/shard_map/psum | solution.py:65
  11.4 600.5 %all-reduce.6.cloned.1.call-start = ((), (), s32[]{:S(2)}) async-start(), calls=%async_computation.1 | async-start | bytes 1048576 | tf_op jit(solution)/shard_map/psum | solution.py:65
  279.6 27.4 %copy-start = (f32[2,256,256]{2,1,0:T(8,128)S(1)}, f32[2,256,256]{2,1,0:T(8,128)}, u32[]{:S(2)}) copy-start(f32[2,256,256]{2,1,0:T(8,128)} %all-reduce.4.cloned.1.call-done) | copy-start | bytes 1572868
  335.6 8.4 %collective-permute-start = (f32[256,128]{0,1:T(8,128)S(1)}, f32[256,128]{0,1:T(8,128)S(1)}, u32[]{:S(2)}, u32[]{:S(2)}) collective-permute-start(f32[256,128]{0,1:T(8,128)S(1)} %get-tuple-element.41), channel_id=1, source_target_pairs={{0,1},{1,2},{2,3},{3,4},{4,5},{5,6},{6,7},{8,9},{9,10},{10,11},{11... | collective-permute-start | bytes 393224 | tf_op jit(solution)/shard_map/ppermute | solution.py:16
  338.7 6.2 collective-permute-start.1
  612.0 19.8 %copy-start.1 = (f32[2,256,256]{1,2,0:T(8,128)S(1)}, f32[2,256,256]{1,2,0:T(8,128)}, u32[]{:S(2)}) copy-start(f32[2,256,256]{1,2,0:T(8,128)} %all-reduce.6.cloned.1.call-done) | copy-start | bytes 1572868
  612.0 29.4 %slice-start = ((f32[2,256,256]{1,2,0:T(8,128)}), f32[2,256,128]{1,2,0:T(8,128)S(1)}, s32[]{:S(2)}) async-start(f32[2,256,256]{1,2,0:T(8,128)} %all-reduce.6.cloned.1.call-done), calls=%async_computation.2 | async-start | bytes 524288 | tf_op jit(solution)/shard_map/slice | solution.py:22
Sparse Core Ops, SparseCore 0:
  11.5 267.9 all-reduce.3
  346.5 265.3 all-reduce.5
where the time goes:
time: 750 us; the launch traced here: 743 us
  waiting for transfers between devices  523 us (70%)
  local copies, waits for them, and re-layouts  112 us (15%)
  blocking collectives  65 us (9%)
  between operations  24.9 us (3%)
  starting transfers between devices  7.65 us (1%)
    psum x2, waiting for transfers between devices, whole_gram(): return lax.psum(partial_gram, 'rows')  521 us
    psum x1, blocking collectives, per_device(): lax.psum((jnp.sum(upper_blocks * upper_blocks, axis=1), jnp.sum(lower_blo...  65 us
    psum x2, local copies, waits for them, and re-layouts, whole_gram(): return lax.psum(partial_gram, 'rows')  34.6 us
    transpose x2, local copies, waits for them, and re-layouts, rotate_pair(): jnp.swapaxes(turn_columns(jnp.swapaxes(turned, 1, 2), cosine_values, sine...  33 us
    dynamic_slice x4, local copies, waits for them, and re-layouts, rotate_pair(): jnp.roll(turned[:, :half_width, half_width:], -offset, axis=2)  21.5 us
  transfers between devices with their start and end apart: 4, of which 4 were waited for; matrix products, arithmetic and copies ran while one was open for 0% of the time, Pallas kernels for 0%

commit v1 on v0

v1 whole, which is shorter than its diff:
```python
import functools
import jax
import jax.numpy as jnp
from jax import lax
from jax.experimental import pallas as pl
from jax.experimental.pallas import tpu as pltpu
from jax.sharding import PartitionSpec as P

BLOCK = 128
STEPS = 2
GROUP = 8

ENTRIES = 7
PADDED = 8


def left(x, by):
    return pltpu.roll(x, (BLOCK - by) & (BLOCK - 1), 1)


def right(x, by):
    return pltpu.roll(x, by, 1)


def pair_entries(load_pair, rows, first, second):
    gap = (second - first) & (BLOCK - 1)
    sums = [None] * ENTRIES
    for start in range(0, rows, GROUP):
        upper, lower = load_pair(start)
        lower_first = left(lower, first)
        lower_second = left(lower, second)
        upper_gap = left(upper, gap)
        terms = (
            upper * upper,
            lower * lower,
            upper * lower_first,
            upper * lower_second,
            upper_gap * lower_first,
            upper * upper_gap,
            lower_first * lower_second,
        )
        sums = [term if total is None else total + term for total, term in zip(sums, terms)]
    reduced = [jnp.sum(total, axis=0, keepdims=True) for total in sums]
    return jnp.concatenate(reduced + [jnp.zeros_like(reduced[0])], axis=0)


def angle(first_norms, second_norms, coupling):
    half_gap = 0.5 * (second_norms - first_norms)
    gap_sign = jnp.where(half_gap >= 0.0, 1.0, -1.0)
    denominator = jnp.maximum(
        jnp.abs(half_gap) + jnp.sqrt(half_gap * half_gap + coupling * coupling),
        1e-06 * (first_norms + second_norms),
    )
    tangent = gap_sign * coupling / denominator
    cosine = 1.0 / jnp.sqrt(1.0 + tangent * tangent)
    return cosine, tangent * cosine


def turned_norms(first_norms, second_norms, coupling, cosine, sine):
    new_first = cosine * (cosine * first_norms - sine * coupling) - sine * (cosine * coupling - sine * second_norms)
    new_second = sine * (sine * first_norms + cosine * coupling) + cosine * (sine * coupling + cosine * second_norms)
    return new_first, new_second


def pair_angles(entries, first, second, skip):
    gap = (second - first) & (BLOCK - 1)
    uu, ll, ul_first, ul_second, ul_gap, uu_gap, ll_gap = [entries[i : i + 1] for i in range(ENTRIES)]
    ll_first = left(ll, first)
    cosine, sine = angle(uu, ll_first, ul_first)
    upper_norms, lower_norms = turned_norms(uu, ll_first, ul_first, cosine, sine)
    cosine_gap = left(cosine, gap)
    sine_gap = left(sine, gap)
    coupling = cosine * (sine_gap * uu_gap + cosine_gap * ul_second) - sine * (sine_gap * ul_gap + cosine_gap * ll_gap)
    lower_norms = left(lower_norms, gap)
    cosine_last, sine_last = angle(upper_norms, lower_norms, coupling)
    upper_norms, lower_norms = turned_norms(upper_norms, lower_norms, coupling, cosine_last, sine_last)
    keep = skip != 0
    one, zero = jnp.ones_like(cosine), jnp.zeros_like(cosine)
    turns = (
        jnp.where(keep, one, cosine),
        jnp.where(keep, zero, sine),
        jnp.where(keep, one, cosine_last),
        jnp.where(keep, zero, sine_last),
    )
    return turns, jnp.where(keep, uu, upper_norms), jnp.where(keep, ll, right(lower_norms, second))


def turn(upper, lower, turns, first, second):
    gap = (second - first) & (BLOCK - 1)
    cosine, sine, cosine_last, sine_last = turns
    lower = left(lower, first)
    upper, lower = cosine * upper - sine * lower, sine * upper + cosine * lower
    lower = left(lower, gap)
    upper, lower = cosine_last * upper - sine_last * lower, sine_last * upper + cosine_last * lower
    return upper, right(lower, second)


def block_of(loads_ref, weights, block):
    columns = slice(block * BLOCK, (block + 1) * BLOCK)
    weight = weights[:, columns]
    return lambda start: loads_ref[start : start + GROUP, columns] * weight


def entries_kernel(offsets_ref, loads_ref, weights_ref, out_ref):
    rows = loads_ref.shape[0]
    weights = weights_ref[...]
    blocks = [block_of(loads_ref, weights, block) for block in range(4)]
    for pair in range(2):
        upper, lower = blocks[pair], blocks[2 + pair]
        out_ref[pair * PADDED : (pair + 1) * PADDED, :] = pair_entries(
            lambda start: (upper(start), lower(start)), rows, offsets_ref[0, 0], offsets_ref[0, 1]
        )


def first_turn_kernel(offsets_ref, skip_ref, place_ref, parts_ref, loads_ref, weights_ref,
                      even_ref, odd_ref, upper_ref, lower_ref):
    rows = loads_ref.shape[0]
    first, second = offsets_ref[0, 0], offsets_ref[0, 1]
    weights = weights_ref[...]
    blocks = [block_of(loads_ref, weights, block) for block in range(4)]
    total = parts_ref[0]
    for part in range(1, parts_ref.shape[0]):
        total = total + parts_ref[part]
    is_even = (place_ref[0] & 1) == 0
    turns = [
        pair_angles(total[pair * PADDED : (pair + 1) * PADDED], first, second, skip_ref[0, pair])[0]
        for pair in range(2)
    ]
    for start in range(0, rows, GROUP):
        span = slice(start, start + GROUP)
        upper_0, lower_0 = turn(blocks[0](start), blocks[2](start), turns[0], first, second)
        upper_1, lower_1 = turn(blocks[1](start), blocks[3](start), turns[1], first, second)
        upper_ref[span, :] = upper_0
        lower_ref[span, :] = lower_1
        even_ref[span, :] = jnp.where(is_even, upper_1, lower_0)
        odd_ref[span, :] = jnp.where(is_even, lower_0, upper_1)


def moved(place_ref, even_ref, odd_ref, upper_ref, lower_ref):
    is_even = (place_ref[0] & 1) == 0
    is_head = place_ref[0] == 0

    def load(start):
        span = slice(start, start + GROUP)
        even, odd, upper = even_ref[span, :], odd_ref[span, :], upper_ref[span, :]
        coming_upper = jnp.where(is_even, odd, even)
        coming_lower = jnp.where(is_even, even, odd)
        return (
            (jnp.where(is_head, upper, coming_upper), lower_ref[span, :]),
            (jnp.where(is_head, coming_upper, upper), coming_lower),
        )

    return load


def moved_entries_kernel(offsets_ref, place_ref, even_ref, odd_ref, upper_ref, lower_ref, out_ref):
    rows = even_ref.shape[0]
    load = moved(place_ref, even_ref, odd_ref, upper_ref, lower_ref)
    for pair in range(2):
        out_ref[pair * PADDED : (pair + 1) * PADDED, :] = pair_entries(
            lambda start: load(start)[pair], rows, offsets_ref[1, 0], offsets_ref[1, 1]
        )


def last_turn_kernel(total_rows, offsets_ref, skip_ref, place_ref, parts_ref, even_ref, odd_ref, upper_ref, lower_ref,
                     rotated_ref, power_ref):
    rows = even_ref.shape[0]
    first, second = offsets_ref[1, 0], offsets_ref[1, 1]
    load = moved(place_ref, even_ref, odd_ref, upper_ref, lower_ref)
    total = parts_ref[0]
    for part in range(1, parts_ref.shape[0]):
        total = total + parts_ref[part]
    turns = []
    for pair in range(2):
        own, upper_norms, lower_norms = pair_angles(
            total[pair * PADDED : (pair + 1) * PADDED], first, second, skip_ref[1, pair]
        )
        turns.append(own)
        power_ref[:, pair * BLOCK : (pair + 1) * BLOCK] = upper_norms / total_rows
        power_ref[:, (2 + pair) * BLOCK : (3 + pair) * BLOCK] = lower_norms / total_rows
    for start in range(0, rows, GROUP):
        span = slice(start, start + GROUP)
        for pair, (upper, lower) in enumerate(load(start)):
            upper, lower = turn(upper, lower, turns[pair], first, second)
            rotated_ref[span, pair * BLOCK : (pair + 1) * BLOCK] = upper
            rotated_ref[span, (2 + pair) * BLOCK : (3 + pair) * BLOCK] = lower


SMEM = pl.BlockSpec(memory_space=pltpu.SMEM)
VMEM = pl.BlockSpec(memory_space=pltpu.VMEM)


def call(kernel, scalars, arrays, shapes, name):
    several = isinstance(shapes, list)
    outs = [jax.ShapeDtypeStruct(shape, jnp.float32) for shape in (shapes if several else [shapes])]
    return pl.pallas_call(
        kernel,
        out_shape=outs if several else outs[0],
        in_specs=[SMEM] * len(scalars) + [VMEM] * len(arrays),
        out_specs=[VMEM] * len(outs) if several else VMEM,
        name=name,
    )(*scalars, *arrays)


def sum_parts(entries):
    size = lax.axis_size("rows")
    entries = entries + lax.ppermute(entries, "rows", [(row, row ^ 1) for row in range(size)])
    groups = [list(range(core, size, 2)) for core in range(2)]
    copies = jnp.broadcast_to(entries[None], (size // 2,) + entries.shape)
    return lax.all_to_all(copies, "rows", 0, 0, axis_index_groups=groups)


def per_device(loads, col_weights, partner_offsets, skip_mask):
    rows, columns = loads.shape
    pairs = lax.axis_size("pairs")
    place = lax.axis_index("pairs").reshape(1)
    weights = col_weights.reshape(1, columns)
    block = (rows, BLOCK)
    entries = call(entries_kernel, [partner_offsets], [loads, weights], (2 * PADDED, BLOCK), "entries")
    parts = sum_parts(entries)
    even, odd, upper, lower = call(
        first_turn_kernel, [partner_offsets, skip_mask, place], [parts, loads, weights], [block] * 4, "first_turn"
    )
    even = lax.ppermute(even, "pairs", [(at, at ^ 1) for at in range(pairs)])
    odd = lax.ppermute(odd, "pairs", [(at, min(max(((at + 1) ^ 1) - 1, 0), pairs - 1)) for at in range(pairs)])
    held = [even, odd, upper, lower]
    entries = call(moved_entries_kernel, [partner_offsets, place], held, (2 * PADDED, BLOCK), "moved_entries")
    parts = sum_parts(entries)
    total_rows = rows * lax.axis_size("rows")
    rotated, power = call(
        functools.partial(last_turn_kernel, float(total_rows)),
        [partner_offsets, skip_mask, place], [parts] + held, [(rows, columns), (1, columns)], "last_turn",
    )
    return rotated, power.reshape(columns)


def solution(mesh):
    in_specs = (P("rows", "pairs"), P("pairs"), P(), P(None, "pairs"))
    out_specs = (P("rows", "pairs"), P("pairs"))
    return jax.shard_map(
        per_device, mesh=mesh, in_specs=in_specs, out_specs=out_specs, check_vma=False
    )
```

time: 750 us -> 60.9 us (0.08)
  the two profiles are of different devices: /device:TPU:9 before, /device:TPU:6 now
where the time goes in v1:
time: 60.9 us; the launch traced here: 60.5 us
  waiting for transfers between devices  19 us (31%)
  starting transfers between devices  15.2 us (25%)
  blocking collectives  13.5 us (22%)
  Pallas kernels  8.7 us (14%)
  local copies, waits for them, and re-layouts  1.98 us (3%)
  other arithmetic  1.4 us (2%)
  between operations  0.66 us (1%)
    all_to_all x1, blocking collectives, sum_parts(): return lax.all_to_all(copies, 'rows', 0, 0, axis_index_groups=groups)  13.5 us
    all_to_all x1, starting transfers between devices, sum_parts(): return lax.all_to_all(copies, 'rows', 0, 0, axis_index_groups=groups)  11.2 us
    all_to_all x1, waiting for transfers between devices, sum_parts(): return lax.all_to_all(copies, 'rows', 0, 0, axis_index_groups=groups)  10.2 us
    pallas_call x4, Pallas kernels, call(): pl.pallas_call(kernel, out_shape=outs if several else outs[0], in_specs=[...  8.7 us
    ppermute x1, waiting for transfers between devices, per_device(): lax.ppermute(odd, 'pairs', [(at, min(max((at + 1 ^ 1) - 1, 0), pairs - 1)...  4.82 us
    ppermute x1, starting transfers between devices, per_device(): lax.ppermute(odd, 'pairs', [(at, min(max((at + 1 ^ 1) - 1, 0), pairs - 1)...  3.15 us
    ppermute x2, waiting for transfers between devices, sum_parts(): lax.ppermute(entries, 'rows', [(row, row ^ 1) for row in range(size)])  2.76 us
    add x2, other arithmetic, sum_parts(): entries + lax.ppermute(entries, 'rows', [(row, row ^ 1) for row in range(...  1.4 us
  transfers between devices with their start and end apart: 5, of which 5 were waited for; matrix products, arithmetic and copies ran while one was open for 0% of the time, Pallas kernels for 0%

profile of v1, /device:TPU:6, one launch (start us, length us, event | category | flops | bytes accessed | tf_op | source)
XLA Modules:
  0.0 60.5 jit_solution(16748458017888192146)
XLA Ops:
  0.6 1.9 %entries.1 = f32[16,128]{1,0:T(8,128)} custom-call(s32[2,2]{1,0:T(2,128)} %offsets_ref.7, f32[256,512]{1,0:T(8,128)} %loads_ref.3, f32[1,512]{1,0:T(1,128)} %bitcast.3), custom_call_target="tpu_custom_call" | custom-call | tf_op jit(solution)/shard_map/entries/pallas_call | solution.py:196
  2.6 0.0 collective-permute-start
  2.6 1.4 %collective-permute-done = f32[16,128]{1,0:T(8,128)S(1)} collective-permute-done((f32[16,128]{1,0:T(8,128)}, f32[16,128]{1,0:T(8,128)S(1)}, u32[]{:S(2)}, u32[]{:S(2)}) %collective-permute-start) | collective-permute-done | bytes 8224 | tf_op jit(solution)/shard_map/ppermute | solution.py:207
  3.9 0.7 %add.6 = f32[16,128]{1,0:T(8,128)S(1)} add(f32[16,128]{1,0:T(8,128)} %entries.1, f32[16,128]{1,0:T(8,128)S(1)} %collective-permute-done) | non-fusion elementwise | flops 2048 | bytes 24576 | tf_op jit(solution)/shard_map/add | solution.py:207
  4.6 0.7 %broadcast_in_dim.4 = f32[16,16,128]{2,1,0:T(8,128)} broadcast(f32[16,128]{1,0:T(8,128)S(1)} %add.6), dimensions={1,2} | broadcast | bytes 139264 | tf_op jit(solution)/shard_map/broadcast_in_dim | solution.py:209
  5.3 11.2 %all-to-all-start = ((f32[16,16,128]{2,1,0:T(8,128)}), f32[16,16,128]{2,1,0:T(8,128)S(1)}, u32[]{:S(2)}, u32[]{:S(2)}) async-start(f32[16,16,128]{2,1,0:T(8,128)} %broadcast_in_dim.4), calls=%async_computation | async-start | bytes 262144 | tf_op jit(solution)/shard_map/all_to_all | solution.py:210
  16.5 10.2 %all-to-all-done.parts_ref = f32[16,16,128]{2,1,0:T(8,128)S(1)} async-done(((f32[16,16,128]{2,1,0:T(8,128)}), f32[16,16,128]{2,1,0:T(8,128)S(1)}, u32[]{:S(2)}, u32[]{:S(2)}) %all-to-all-start) | async-done | bytes 131104 | tf_op jit(solution)/shard_map/all_to_all | solution.py:210
  26.8 0.0 copy-start.2
  26.8 0.7 %copy-done.2 = f32[16,16,128]{2,1,0:T(8,128)} copy-done((f32[16,16,128]{2,1,0:T(8,128)}, f32[16,16,128]{2,1,0:T(8,128)S(1)}, u32[]{:S(2)}) %copy-start.2) | copy-done | bytes 131096
  27.4 2.3 %first_turn.1 = (f32[256,128]{1,0:T(8,128)}, f32[256,128]{1,0:T(8,128)}, f32[256,128]{1,0:T(8,128)}, f32[256,128]{1,0:T(8,128)}) custom-call(s32[2,2]{1,0:T(2,128)} %offsets_ref.7, s32[2,2]{1,0:T(2,128)} %skip_ref.3, s32[1]{0:T(128)} %bitcast.place_ref, f32[16,16,128]{2,1,0:T(8,128)} %copy-done.2, f32[256,512]{1,0:T(8,128)} %loads_ref.3, f32[1,512]{1,0:T(1,128)} %bitcast.4), custom_call_target="tpu_custom_call" | custom-call | tf_op jit(solution)/shard_map/first_turn/pallas_call | solution.py:196
  29.8 0.8 %collective-permute-start.1 = (f32[256,128]{1,0:T(8,128)}, f32[256,128]{1,0:T(8,128)S(1)}, u32[]{:S(2)}, u32[]{:S(2)}) collective-permute-start(f32[256,128]{1,0:T(8,128)} %get-tuple-element.8), channel_id=1, source_target_pairs={{0,1},{1,0},{2,3},{3,2},{4,5},{5,4},{6,7},{7,6},{8,9},{9,8},{10,11... | collective-permute-start | bytes 393224 | tf_op jit(solution)/shard_map/ppermute | solution.py:224
  30.6 3.2 %collective-permute-start.2 = (f32[256,128]{1,0:T(8,128)}, f32[256,128]{1,0:T(8,128)S(1)}, u32[]{:S(2)}, u32[]{:S(2)}) collective-permute-start(f32[256,128]{1,0:T(8,128)} %get-tuple-element.9), channel_id=1, source_target_pairs={{0,0},{1,2},{2,1},{3,4},{4,3},{5,6},{6,5},{7,7},{8,8},{9,10},{10,9... | collective-permute-start | bytes 393224 | tf_op jit(solution)/shard_map/ppermute | solution.py:225
  33.8 1.2 %collective-permute-done.1.even_ref = f32[256,128]{1,0:T(8,128)S(1)} collective-permute-done((f32[256,128]{1,0:T(8,128)}, f32[256,128]{1,0:T(8,128)S(1)}, u32[]{:S(2)}, u32[]{:S(2)}) %collective-permute-start.1) | collective-permute-done | bytes 131104 | tf_op jit(solution)/shard_map/ppermute | solution.py:224
  35.0 0.0 copy-start
  35.0 4.8 %collective-permute-done.2.odd_ref = f32[256,128]{1,0:T(8,128)S(1)} collective-permute-done((f32[256,128]{1,0:T(8,128)}, f32[256,128]{1,0:T(8,128)S(1)}, u32[]{:S(2)}, u32[]{:S(2)}) %collective-permute-start.2) | collective-permute-done | bytes 131104 | tf_op jit(solution)/shard_map/ppermute | solution.py:225
  39.8 0.0 copy-start.1
  39.8 0.0 copy-done
  39.8 0.6 %copy-done.1 = f32[256,128]{1,0:T(8,128)} copy-done((f32[256,128]{1,0:T(8,128)}, f32[256,128]{1,0:T(8,128)S(1)}, u32[]{:S(2)}) %copy-start.1) | copy-done | bytes 131096
  40.4 2.0 %moved_entries.1 = f32[16,128]{1,0:T(8,128)} custom-call(s32[2,2]{1,0:T(2,128)} %offsets_ref.7, s32[1]{0:T(128)} %bitcast.place_ref, f32[256,128]{1,0:T(8,128)} %copy-done, f32[256,128]{1,0:T(8,128)} %copy-done.1, f32[256,128]{1,0:T(8,128)} %get-tuple-element.10.upper_ref, f32[256,128]{1,0:T(8,128)} %get-tuple-element.11.lower_ref), custom_call_target="tpu_custom_call" | custom-call | tf_op jit(solution)/shard_map/moved_entries/pallas_call | solution.py:196
  42.4 0.0 collective-permute-start.3
  42.4 1.4 %collective-permute-done.3 = f32[16,128]{1,0:T(8,128)S(1)} collective-permute-done((f32[16,128]{1,0:T(8,128)}, f32[16,128]{1,0:T(8,128)S(1)}, u32[]{:S(2)}, u32[]{:S(2)}) %collective-permute-start.3) | collective-permute-done | bytes 8224 | tf_op jit(solution)/shard_map/ppermute | solution.py:207
  43.8 0.7 %add.7 = f32[16,128]{1,0:T(8,128)S(1)} add(f32[16,128]{1,0:T(8,128)} %moved_entries.1, f32[16,128]{1,0:T(8,128)S(1)} %collective-permute-done.3) | non-fusion elementwise | flops 2048 | bytes 24576 | tf_op jit(solution)/shard_map/add | solution.py:207
  44.5 13.5 %all_to_all.10.parts_ref = f32[16,16,128]{2,1,0:T(8,128)} all-to-all(f32[16,16,128]{2,1,0:T(8,128)S(1)} %broadcast_in_dim.5), channel_id=1, replica_groups={{0,16,32,48,64,80,96,112,128,144,160,176,192,208,224,240},{8,24,40,56,7..., dimensions={0} | all-to-all | bytes 262144 | tf_op jit(solution)/shard_map/all_to_all | solution.py:210
  58.0 2.4 %last_turn.1 = (f32[256,512]{1,0:T(8,128)}, f32[1,512]{1,0:T(1,128)}) custom-call(s32[2,2]{1,0:T(2,128)} %offsets_ref.7, s32[2,2]{1,0:T(2,128)} %skip_ref.3, s32[1]{0:T(128)} %bitcast.place_ref, f32[16,16,128]{2,1,0:T(8,128)} %all_to_all.10.parts_ref, f32[256,128]{1,0:T(8,128)} %copy-done, f32[256,128]{1,0:T(8,128)} %copy-done.1, ...), custom_call_target="tpu_custom_call" | custom-call | tf_op jit(solution)/shard_map/last_turn/pallas_call | solution.py:196
  (1 shorter events, 0.0 us)
Async XLA Ops:
  2.6 1.4 %collective-permute-start = (f32[16,128]{1,0:T(8,128)}, f32[16,128]{1,0:T(8,128)S(1)}, u32[]{:S(2)}, u32[]{:S(2)}) collective-permute-start(f32[16,128]{1,0:T(8,128)} %entries.1), channel_id=1, source_target_pairs={{0,8},{8,0},{16,24},{24,16},{32,40},{40,32},{48,56},{56,48},{64,72... | collective-permute-start | bytes 24584 | tf_op jit(solution)/shard_map/ppermute | solution.py:207
  5.3 21.5 %all-to-all-start = ((f32[16,16,128]{2,1,0:T(8,128)}), f32[16,16,128]{2,1,0:T(8,128)S(1)}, u32[]{:S(2)}, u32[]{:S(2)}) async-start(f32[16,16,128]{2,1,0:T(8,128)} %broadcast_in_dim.4), calls=%async_computation | async-start | bytes 262144 | tf_op jit(solution)/shard_map/all_to_all | solution.py:210
  26.8 0.7 %copy-start.2 = (f32[16,16,128]{2,1,0:T(8,128)}, f32[16,16,128]{2,1,0:T(8,128)S(1)}, u32[]{:S(2)}) copy-start(f32[16,16,128]{2,1,0:T(8,128)S(1)} %all-to-all-done.parts_ref) | copy-start | bytes 393220
  29.8 5.2 %collective-permute-start.1 = (f32[256,128]{1,0:T(8,128)}, f32[256,128]{1,0:T(8,128)S(1)}, u32[]{:S(2)}, u32[]{:S(2)}) collective-permute-start(f32[256,128]{1,0:T(8,128)} %get-tuple-element.8), channel_id=1, source_target_pairs={{0,1},{1,0},{2,3},{3,2},{4,5},{5,4},{6,7},{7,6},{8,9},{9,8},{10,11... | collective-permute-start | bytes 393224 | tf_op jit(solution)/shard_map/ppermute | solution.py:224
  30.6 9.2 %collective-permute-start.2 = (f32[256,128]{1,0:T(8,128)}, f32[256,128]{1,0:T(8,128)S(1)}, u32[]{:S(2)}, u32[]{:S(2)}) collective-permute-start(f32[256,128]{1,0:T(8,128)} %get-tuple-element.9), channel_id=1, source_target_pairs={{0,0},{1,2},{2,1},{3,4},{4,3},{5,6},{6,5},{7,7},{8,8},{9,10},{10,9... | collective-permute-start | bytes 393224 | tf_op jit(solution)/shard_map/ppermute | solution.py:225
  35.0 4.8 %copy-start = (f32[256,128]{1,0:T(8,128)}, f32[256,128]{1,0:T(8,128)S(1)}, u32[]{:S(2)}) copy-start(f32[256,128]{1,0:T(8,128)S(1)} %collective-permute-done.1.even_ref) | copy-start | bytes 393220
  39.8 0.6 %copy-start.1 = (f32[256,128]{1,0:T(8,128)}, f32[256,128]{1,0:T(8,128)S(1)}, u32[]{:S(2)}) copy-start(f32[256,128]{1,0:T(8,128)S(1)} %collective-permute-done.2.odd_ref) | copy-start | bytes 393220
  42.4 1.4 %collective-permute-start.3 = (f32[16,128]{1,0:T(8,128)}, f32[16,128]{1,0:T(8,128)S(1)}, u32[]{:S(2)}, u32[]{:S(2)}) collective-permute-start(f32[16,128]{1,0:T(8,128)} %moved_entries.1), channel_id=1, source_target_pairs={{0,8},{8,0},{16,24},{24,16},{32,40},{40,32},{48,56},{56,48},{64,72... | collective-permute-start | bytes 24584 | tf_op jit(solution)/shard_map/ppermute | solution.py:207

commit v2 on v1

--- a/solution.py
+++ b/solution.py
@@ -186,6 +186,7 @@
             rotated_ref[span, (2 + pair) * BLOCK : (3 + pair) * BLOCK] = lower
 
 
+VMEM_LIMIT = 8 * 1024 * 1024
 SMEM = pl.BlockSpec(memory_space=pltpu.SMEM)
 VMEM = pl.BlockSpec(memory_space=pltpu.VMEM)
 
@@ -199,6 +200,7 @@
         in_specs=[SMEM] * len(scalars) + [VMEM] * len(arrays),
         out_specs=[VMEM] * len(outs) if several else VMEM,
         name=name,
+        compiler_params=pltpu.CompilerParams(vmem_limit_bytes=VMEM_LIMIT),
     )(*scalars, *arrays)
 
 

time: 60.9 us -> 55.9 us (0.918)
  Pallas kernels: 8.7 us -> 4.54 us
  other arithmetic: 1.4 us -> 0.01 us
  local copies, waits for them, and re-layouts: 1.98 us -> 3.09 us
  waiting for transfers between devices: 19 us -> 18.3 us
    pallas_call x4, Pallas kernels: 8.7 us -> 4.54 us  [call(): pl.pallas_call(kernel, out_shape=outs if several else outs[0], in_specs=[...]
    add x2, other arithmetic: 1.4 us -> 0.01 us  [sum_parts(): entries + lax.ppermute(entries, 'rows', [(row, row ^ 1) for row in range(...]
    unnamed x6 -> x12, local copies, waits for them, and re-layouts: 1.3 us -> 2.41 us
where the time goes in v2:
time: 55.9 us; the launch traced here: 55.6 us
  waiting for transfers between devices  18.3 us (33%)
  starting transfers between devices  15.5 us (28%)
  blocking collectives  13.5 us (24%)
  Pallas kernels  4.54 us (8%)
  local copies, waits for them, and re-layouts  3.09 us (6%)
  between operations  0.72 us (1%)
    all_to_all x1, blocking collectives, sum_parts(): return lax.all_to_all(copies, 'rows', 0, 0, axis_index_groups=groups)  13.5 us
    all_to_all x1, starting transfers between devices, sum_parts(): return lax.all_to_all(copies, 'rows', 0, 0, axis_index_groups=groups)  11.2 us
    all_to_all x1, waiting for transfers between devices, sum_parts(): return lax.all_to_all(copies, 'rows', 0, 0, axis_index_groups=groups)  10.2 us
    ppermute x1, waiting for transfers between devices, per_device(): lax.ppermute(odd, 'pairs', [(at, min(max((at + 1 ^ 1) - 1, 0), pairs - 1)...  4.82 us
    pallas_call x4, Pallas kernels, call(): pl.pallas_call(kernel, out_shape=outs if several else outs[0], in_specs=[...  4.54 us
    ppermute x1, starting transfers between devices, per_device(): lax.ppermute(odd, 'pairs', [(at, min(max((at + 1 ^ 1) - 1, 0), pairs - 1)...  3.15 us
    unnamed x12, local copies, waits for them, and re-layouts  2.41 us
    ppermute x2, waiting for transfers between devices, sum_parts(): lax.ppermute(entries, 'rows', [(row, row ^ 1) for row in range(size)])  2.32 us
  transfers between devices with their start and end apart: 5, of which 5 were waited for; matrix products, arithmetic and copies ran while one was open for 0% of the time, Pallas kernels for 0%

profile of v2, /device:TPU:6, one launch (start us, length us, event | category | flops | bytes accessed | tf_op | source)
XLA Modules:
  0.0 55.6 jit_solution(14127892472591903322)
XLA Ops:
  0.6 0.0 copy-start.2
  0.6 0.7 %copy-done.2 = s32[2,2]{1,0:T(2,128)S(1)} copy-done((s32[2,2]{1,0:T(2,128)S(1)}, s32[2,2]{1,0:T(2,128)}, u32[]{:S(2)}) %copy-start.2) | copy-done | bytes 40
  1.3 0.0 copy-start
  1.3 1.0 %copy-done = f32[256,512]{1,0:T(8,128)S(1)} copy-done((f32[256,512]{1,0:T(8,128)S(1)}, f32[256,512]{1,0:T(8,128)}, u32[]{:S(2)}) %copy-start) | copy-done | bytes 524312
  2.4 0.0 copy-start.3
  2.4 0.7 %copy-done.3 = f32[512]{0:T(512)S(1)} copy-done((f32[512]{0:T(512)S(1)}, f32[512]{0:T(512)}, u32[]{:S(2)}) %copy-start.3) | copy-done | bytes 2072
  3.0 0.0 copy-start.1
  3.0 0.8 %entries.1 = f32[16,128]{1,0:T(8,128)S(1)} custom-call(s32[2,2]{1,0:T(2,128)S(1)} %copy-done.2, f32[256,512]{1,0:T(8,128)S(1)} %copy-done, f32[1,512]{1,0:T(1,128)S(1)} %bitcast.3), custom_call_target="tpu_custom_call" | custom-call | tf_op jit(solution)/shard_map/entries/pallas_call | solution.py:197
  3.9 0.1 collective-permute-start
  4.0 1.2 %collective-permute-done = f32[16,128]{1,0:T(8,128)S(1)} collective-permute-done((f32[16,128]{1,0:T(8,128)S(1)}, f32[16,128]{1,0:T(8,128)S(1)}, u32[]{:S(2)}, u32[]{:S(2)}) %collective-permute-start) | collective-permute-done | bytes 8224 | tf_op jit(solution)/shard_map/ppermute | solution.py:209
  5.1 0.7 %broadcast_in_dim.4 = f32[16,16,128]{2,1,0:T(8,128)} broadcast(f32[16,128]{1,0:T(8,128)S(1)} %add.6), dimensions={1,2} | broadcast | bytes 139264 | tf_op jit(solution)/shard_map/broadcast_in_dim | solution.py:211
  5.8 11.2 %all-to-all-start = ((f32[16,16,128]{2,1,0:T(8,128)}), f32[16,16,128]{2,1,0:T(8,128)S(1)}, u32[]{:S(2)}, u32[]{:S(2)}) async-start(f32[16,16,128]{2,1,0:T(8,128)} %broadcast_in_dim.4), calls=%async_computation | async-start | bytes 262144 | tf_op jit(solution)/shard_map/all_to_all | solution.py:212
  17.0 0.0 copy-start.4
  17.0 0.0 copy-start.5
  17.0 10.2 %all-to-all-done.parts_ref = f32[16,16,128]{2,1,0:T(8,128)S(1)} async-done(((f32[16,16,128]{2,1,0:T(8,128)}), f32[16,16,128]{2,1,0:T(8,128)S(1)}, u32[]{:S(2)}, u32[]{:S(2)}) %all-to-all-start) | async-done | bytes 131104 | tf_op jit(solution)/shard_map/all_to_all | solution.py:212
  27.3 0.0 copy-done.1
  27.3 0.0 copy-done.4
  27.3 0.0 copy-done.5
  27.3 1.0 %first_turn.1 = (f32[256,128]{1,0:T(8,128)S(1)}, f32[256,128]{1,0:T(8,128)S(1)}, f32[256,128]{1,0:T(8,128)S(1)}, f32[256,128]{1,0:T(8,128)S(1)}) custom-call(s32[2,2]{1,0:T(2,128)S(1)} %copy-done.2, s32[2,2]{1,0:T(2,128)S(1)} %copy-done.5, s32[1]{0:T(128)} %bitcast.place_ref, f32[16,16,128]{2,1,0:T(8,128)S(1)} %all-to-all-done.parts_ref, ...), custom_call_target="tpu_custom_call" | custom-call | tf_op jit(solution)/shard_map/first_turn/pallas_call | solution.py:197
  28.3 0.9 %collective-permute-start.1 = (f32[256,128]{1,0:T(8,128)S(1)}, f32[256,128]{1,0:T(8,128)S(1)}, u32[]{:S(2)}, u32[]{:S(2)}) collective-permute-start(f32[256,128]{1,0:T(8,128)S(1)} %get-tuple-element.8), channel_id=1, source_target_pairs={{0,1},{1,0},{2,3},{3,2},{4,5},{5,4},{6,7},{7,6},{8,9},{9,8},{10,11... | collective-permute-start | bytes 393224 | tf_op jit(solution)/shard_map/ppermute | solution.py:226
  29.2 3.2 %collective-permute-start.2 = (f32[256,128]{1,0:T(8,128)S(1)}, f32[256,128]{1,0:T(8,128)S(1)}, u32[]{:S(2)}, u32[]{:S(2)}) collective-permute-start(f32[256,128]{1,0:T(8,128)S(1)} %get-tuple-element.9), channel_id=1, source_target_pairs={{0,0},{1,2},{2,1},{3,4},{4,3},{5,6},{6,5},{7,7},{8,8},{9,10},{10,9... | collective-permute-start | bytes 393224 | tf_op jit(solution)/shard_map/ppermute | solution.py:227
  32.4 1.0 %collective-permute-done.1.even_ref = f32[256,128]{1,0:T(8,128)S(1)} collective-permute-done((f32[256,128]{1,0:T(8,128)S(1)}, f32[256,128]{1,0:T(8,128)S(1)}, u32[]{:S(2)}, u32[]{:S(2)}) %collective-permute-start.1) | collective-permute-done | bytes 131104 | tf_op jit(solution)/shard_map/ppermute | solution.py:226
  33.4 4.8 %collective-permute-done.2.odd_ref = f32[256,128]{1,0:T(8,128)S(1)} collective-permute-done((f32[256,128]{1,0:T(8,128)S(1)}, f32[256,128]{1,0:T(8,128)S(1)}, u32[]{:S(2)}, u32[]{:S(2)}) %collective-permute-start.2) | collective-permute-done | bytes 131104 | tf_op jit(solution)/shard_map/ppermute | solution.py:227
  38.2 0.8 %moved_entries.1 = f32[16,128]{1,0:T(8,128)S(1)} custom-call(s32[2,2]{1,0:T(2,128)S(1)} %copy-done.2, s32[1]{0:T(128)} %bitcast.place_ref, f32[256,128]{1,0:T(8,128)S(1)} %collective-permute-done.1.even_ref, f32[256,128]{1,0:T(8,128)S(1)} %collective-permute-done.2.odd_ref, f32[256,128]{1,0:T(8,128)S(1)} %get-tuple-element.10.upper_ref, ...), custom_call_target="tpu_custom_call" | custom-call | tf_op jit(solution)/shard_map/moved_entries/pallas_call | solution.py:197
  39.0 0.1 collective-permute-start.3
  39.1 1.2 %collective-permute-done.3 = f32[16,128]{1,0:T(8,128)S(1)} collective-permute-done((f32[16,128]{1,0:T(8,128)S(1)}, f32[16,128]{1,0:T(8,128)S(1)}, u32[]{:S(2)}, u32[]{:S(2)}) %collective-permute-start.3) | collective-permute-done | bytes 8224 | tf_op jit(solution)/shard_map/ppermute | solution.py:209
  40.3 13.5 %all_to_all.10.parts_ref = f32[16,16,128]{2,1,0:T(8,128)S(1)} all-to-all(f32[16,16,128]{2,1,0:T(8,128)S(1)} %broadcast_in_dim.5), channel_id=1, replica_groups={{0,16,32,48,64,80,96,112,128,144,160,176,192,208,224,240},{8,24,40,56,7..., dimensions={0} | all-to-all | bytes 262144 | tf_op jit(solution)/shard_map/all_to_all | solution.py:212
  53.8 1.8 %last_turn.1 = (f32[256,512]{1,0:T(8,128)}, f32[1,512]{1,0:T(1,128)}) custom-call(s32[2,2]{1,0:T(2,128)S(1)} %copy-done.2, s32[2,2]{1,0:T(2,128)S(1)} %copy-done.5, s32[1]{0:T(128)} %bitcast.place_ref, f32[16,16,128]{2,1,0:T(8,128)S(1)} %all_to_all.10.parts_ref, f32[256,128]{1,0:T(8,128)S(1)} %collective-permute-done.1.even_ref, ...), custom_call_target="tpu_custom_call" | custom-call | tf_op jit(solution)/shard_map/last_turn/pallas_call | solution.py:197
  (3 shorter events, 0.0 us)
Async XLA Ops:
  0.6 0.7 %copy-start.2 = (s32[2,2]{1,0:T(2,128)S(1)}, s32[2,2]{1,0:T(2,128)}, u32[]{:S(2)}) copy-start(s32[2,2]{1,0:T(2,128)} %offsets_ref.7) | copy-start | bytes 52
  1.3 1.0 %copy-start = (f32[256,512]{1,0:T(8,128)S(1)}, f32[256,512]{1,0:T(8,128)}, u32[]{:S(2)}) copy-start(f32[256,512]{1,0:T(8,128)} %loads_ref.3) | copy-start | bytes 1572868
  2.4 0.7 %copy-start.3 = (f32[512]{0:T(512)S(1)}, f32[512]{0:T(512)}, u32[]{:S(2)}) copy-start(f32[512]{0:T(512)} %param.5) | copy-start | bytes 6148
  3.0 24.2 %copy-start.1 = (f32[256,512]{1,0:T(8,128)S(1)}, f32[256,512]{1,0:T(8,128)}, u32[]{:S(2)}) copy-start(f32[256,512]{1,0:T(8,128)} %loads_ref.3) | copy-start | bytes 1572868
  3.9 1.3 %collective-permute-start = (f32[16,128]{1,0:T(8,128)S(1)}, f32[16,128]{1,0:T(8,128)S(1)}, u32[]{:S(2)}, u32[]{:S(2)}) collective-permute-start(f32[16,128]{1,0:T(8,128)S(1)} %entries.1), channel_id=1, source_target_pairs={{0,8},{8,0},{16,24},{24,16},{32,40},{40,32},{48,56},{56,48},{64,72... | collective-permute-start | bytes 24584 | tf_op jit(solution)/shard_map/ppermute | solution.py:209
  5.8 21.5 %all-to-all-start = ((f32[16,16,128]{2,1,0:T(8,128)}), f32[16,16,128]{2,1,0:T(8,128)S(1)}, u32[]{:S(2)}, u32[]{:S(2)}) async-start(f32[16,16,128]{2,1,0:T(8,128)} %broadcast_in_dim.4), calls=%async_computation | async-start | bytes 262144 | tf_op jit(solution)/shard_map/all_to_all | solution.py:212
  17.0 10.2 %copy-start.4 = (f32[512]{0:T(512)S(1)}, f32[512]{0:T(512)}, u32[]{:S(2)}) copy-start(f32[512]{0:T(512)} %param.5) | copy-start | bytes 6148
  17.0 10.2 %copy-start.5 = (s32[2,2]{1,0:T(2,128)S(1)}, s32[2,2]{1,0:T(2,128)}, u32[]{:S(2)}) copy-start(s32[2,2]{1,0:T(2,128)} %skip_ref.3) | copy-start | bytes 52
  28.3 5.1 %collective-permute-start.1 = (f32[256,128]{1,0:T(8,128)S(1)}, f32[256,128]{1,0:T(8,128)S(1)}, u32[]{:S(2)}, u32[]{:S(2)}) collective-permute-start(f32[256,128]{1,0:T(8,128)S(1)} %get-tuple-element.8), channel_id=1, source_target_pairs={{0,1},{1,0},{2,3},{3,2},{4,5},{5,4},{6,7},{7,6},{8,9},{9,8},{10,11... | collective-permute-start | bytes 393224 | tf_op jit(solution)/shard_map/ppermute | solution.py:226
  29.2 9.0 %collective-permute-start.2 = (f32[256,128]{1,0:T(8,128)S(1)}, f32[256,128]{1,0:T(8,128)S(1)}, u32[]{:S(2)}, u32[]{:S(2)}) collective-permute-start(f32[256,128]{1,0:T(8,128)S(1)} %get-tuple-element.9), channel_id=1, source_target_pairs={{0,0},{1,2},{2,1},{3,4},{4,3},{5,6},{6,5},{7,7},{8,8},{9,10},{10,9... | collective-permute-start | bytes 393224 | tf_op jit(solution)/shard_map/ppermute | solution.py:227
  39.0 1.3 %collective-permute-start.3 = (f32[16,128]{1,0:T(8,128)S(1)}, f32[16,128]{1,0:T(8,128)S(1)}, u32[]{:S(2)}, u32[]{:S(2)}) collective-permute-start(f32[16,128]{1,0:T(8,128)S(1)} %moved_entries.1), channel_id=1, source_target_pairs={{0,8},{8,0},{16,24},{24,16},{32,40},{40,32},{48,56},{56,48},{64,72... | collective-permute-start | bytes 24584 | tf_op jit(solution)/shard_map/ppermute | solution.py:209

commit v3 on v0

v3 whole, which is shorter than its diff:
```python
import functools
import jax
import jax.numpy as jnp
from jax import lax
from jax.experimental import pallas as pl
from jax.experimental.pallas import tpu as pltpu
from jax.sharding import PartitionSpec as P

BLOCK = 128
GROUP = 8
CHUNKS = 4

STATS = 19
CROSS = 2 * STATS
FLAGS = CROSS + 36
SUMS = 80
NORMS = 12
ANGLES = 16
VMEM_LIMIT = 8 * 1024 * 1024


def left(x, by):
    return pltpu.roll(x, (-by) & (BLOCK - 1), 1)


def right(x, by):
    return pltpu.roll(x, by & (BLOCK - 1), 1)


class Lags:
    def __init__(self, offsets, slot):
        place = lax.axis_index("pairs")
        self.first = offsets[0, 0]
        self.gap = offsets[0, 1] - offsets[0, 0]
        self.turn = offsets[1, 1] - offsets[1, 0]
        self.x_low = (slot == 1) & (place == 0)
        self.y_up = (slot == 1) & (place == lax.axis_size("pairs") - 1)
        self.x_shift = jnp.where(self.x_low, offsets[0, 1], 0)
        y_shift = jnp.where(self.y_up, 0, offsets[0, 1])
        self.lag = offsets[1, 0] - y_shift + self.x_shift
        self.out = self.x_shift + offsets[1, 1]

    def crossed(self):
        return (self.lag, self.lag + self.turn, self.lag - self.turn)


def halves(ref, span):
    return ref[span, :BLOCK], ref[span, BLOCK:]


def sums_over(rows, count, terms):
    def body(step, totals):
        span = pl.ds(pl.multiple_of(step * GROUP, GROUP), GROUP)
        return tuple(total + term for total, term in zip(totals, terms(span)))

    zeros = tuple(jnp.zeros((GROUP, BLOCK), jnp.float32) for _ in range(count))
    totals = lax.fori_loop(0, rows // GROUP, body, zeros, unroll=4)
    return [jnp.sum(total, axis=0, keepdims=True) for total in totals]


def store_rows(out_ref, start, values):
    for index, value in enumerate(values):
        out_ref[start + index : start + index + 1, :] = value


def lagged(x, y, lag, gap):
    terms = []
    for by in (lag - gap, lag, lag + gap):
        moved = [left(half, by) for half in y]
        terms += [a * b for a in x for b in moved]
    return terms


def pair_stats(ref, rows, lags):
    def terms(span):
        upper, lower = halves(ref, span)
        upper_gap, lower_gap = left(upper, lags.gap), left(lower, lags.gap)
        step_0 = [upper * upper, lower * lower, upper * lower, upper * lower_gap, upper_gap * lower, upper * upper_gap, lower * lower_gap]
        return step_0 + lagged((upper, lower), (upper, lower), lags.turn, lags.gap)

    return sums_over(rows, STATS, terms)


def angle(first_norms, second_norms, coupling):
    half_gap = 0.5 * (second_norms - first_norms)
    gap_sign = jnp.where(half_gap >= 0.0, 1.0, -1.0)
    denominator = jnp.maximum(
        jnp.abs(half_gap) + jnp.sqrt(half_gap * half_gap + coupling * coupling),
        1e-06 * (first_norms + second_norms),
    )
    tangent = gap_sign * coupling / denominator
    cosine = 1.0 / jnp.sqrt(1.0 + tangent * tangent)
    return cosine, tangent * cosine


def turned_norms(first_norms, second_norms, coupling, cosine, sine):
    new_first = cosine * (cosine * first_norms - sine * coupling) - sine * (cosine * coupling - sine * second_norms)
    new_second = sine * (sine * first_norms + cosine * coupling) + cosine * (sine * coupling + cosine * second_norms)
    return new_first, new_second


def two_rounds(first_norms, second_norms, couplings, gap, keep):
    same, ahead, behind, firsts, seconds = couplings
    cosine, sine = angle(first_norms, second_norms, same)
    new_first, new_second = turned_norms(first_norms, second_norms, same, cosine, sine)
    cosine_gap, sine_gap = left(cosine, gap), left(sine, gap)
    coupling = cosine * (sine_gap * firsts + cosine_gap * ahead) - sine * (sine_gap * behind + cosine_gap * seconds)
    new_second = left(new_second, gap)
    cosine_last, sine_last = angle(new_first, new_second, coupling)
    new_first, new_second = turned_norms(new_first, new_second, coupling, cosine_last, sine_last)
    one, zero = jnp.ones_like(cosine), jnp.zeros_like(cosine)
    turns = (
        jnp.where(keep, one, cosine),
        jnp.where(keep, zero, sine),
        jnp.where(keep, one, cosine_last),
        jnp.where(keep, zero, sine_last),
    )
    return turns, (jnp.where(keep, first_norms, new_first), jnp.where(keep, left(second_norms, gap), new_second))


def joint(x_weights, y_weights, dots, gap):
    total = None
    for a in range(2):
        for b in range(2):
            (x_here, x_gap), (y_here, y_gap) = x_weights[a], y_weights[b]
            before, at, after = [dots[4 * index + 2 * a + b] for index in range(3)]
            part = x_here * (y_here * at + y_gap * after) + x_gap * (y_here * left(before, gap) + y_gap * left(at, gap))
            total = part if total is None else total + part
    return total


def rolled(weights, by):
    return [[left(value, by) for value in pair] for pair in weights]


def load_kernel(offsets_hbm, skip_hbm, loads_hbm, weights_hbm, first_ref, second_ref, offsets, skip, loads, weights, sems):
    rows = loads.shape[0]
    part = rows // CHUNKS
    small = [
        pltpu.make_async_copy(offsets_hbm, offsets, sems.at[CHUNKS]),
        pltpu.make_async_copy(skip_hbm, skip, sems.at[CHUNKS + 1]),
        pltpu.make_async_copy(weights_hbm, weights, sems.at[CHUNKS + 2]),
    ]
    large = [
        pltpu.make_async_copy(loads_hbm.at[pl.ds(chunk * part, part)], loads.at[pl.ds(chunk * part, part)], sems.at[chunk])
        for chunk in range(CHUNKS)
    ]
    for copy in small + large:
        copy.start()
    for copy in small:
        copy.wait()
    is_even = (lax.axis_index("pairs") & 1) == 0
    first = offsets[0, 0]
    weight = [weights[:, block * BLOCK : (block + 1) * BLOCK] for block in range(4)]
    for chunk in range(CHUNKS):
        large[chunk].wait()

        def body(step, _):
            span = pl.ds(pl.multiple_of(chunk * part + step * GROUP, GROUP), GROUP)
            blocks = [loads[span, block * BLOCK : (block + 1) * BLOCK] * weight[block] for block in range(4)]
            lower_0, lower_1 = left(blocks[2], first), left(blocks[3], first)
            first_ref[span, :BLOCK] = jnp.where(is_even, blocks[1], blocks[0])
            first_ref[span, BLOCK:] = jnp.where(is_even, lower_1, lower_0)
            second_ref[span, :BLOCK] = jnp.where(is_even, blocks[0], blocks[1])
            second_ref[span, BLOCK:] = jnp.where(is_even, lower_0, lower_1)
            return _

        lax.fori_loop(0, part // GROUP, body, 0, unroll=4)
    span = slice(rows, rows + GROUP)
    skips = [skip[0, pair].astype(jnp.float32) for pair in range(2)]
    first_ref[span, :] = jnp.full((GROUP, 2 * BLOCK), jnp.where(is_even, skips[1], skips[0]), jnp.float32)
    second_ref[span, :] = jnp.full((GROUP, 2 * BLOCK), jnp.where(is_even, skips[0], skips[1]), jnp.float32)


def stats_kernel(rows, offsets, first_ref, second_ref, first_out, second_out):
    lags = Lags(offsets, 0)
    for ref, out in ((first_ref, first_out), (second_ref, second_out)):
        store_rows(out, 0, pair_stats(ref, rows, lags))


def cross_kernel(rows, odd_slot, offsets, skip, own_ref, come_ref, stats_ref, out_ref):
    is_even = (lax.axis_index("pairs") & 1) == 0
    slot = jnp.where(is_even, 1 - odd_slot, odd_slot)
    lags = Lags(offsets, slot)
    own_first = slot == 1
    come_stats = pair_stats(come_ref, rows, lags)
    own_flag, come_flag = [ref[rows : rows + 1, :BLOCK] for ref in (own_ref, come_ref)]
    step_flag = jnp.full((1, BLOCK), jnp.where(own_first, skip[1, 1], skip[1, 0]).astype(jnp.float32), jnp.float32)
    own_stats = [stats_ref[index : index + 1, :] for index in range(STATS)]

    def fill(x_ref, y_ref, x_stats, y_stats, flags):
        store_rows(out_ref, 0, x_stats)
        store_rows(out_ref, STATS, y_stats)
        for index, lag in enumerate(lags.crossed()):
            sums = sums_over(rows, 12, lambda span: lagged(halves(x_ref, span), halves(y_ref, span), lag, lags.gap))
            store_rows(out_ref, CROSS + 12 * index, sums)
        store_rows(out_ref, FLAGS, flags + [jnp.zeros((1, BLOCK), jnp.float32)] * (SUMS - FLAGS - 3))

    @pl.when(own_first)
    def _():
        fill(own_ref, come_ref, own_stats, come_stats, [own_flag, come_flag, step_flag])

    @pl.when(jnp.logical_not(own_first))
    def _():
        fill(come_ref, own_ref, come_stats, own_stats, [come_flag, own_flag, step_flag])


def angles_kernel(total_rows, offsets, sums_ref, out_ref):
    lags = Lags(offsets, lax.axis_index("rows") & 1)
    rows = [sums_ref[index : index + 1, :] for index in range(FLAGS + 3)]
    sides = []
    for side, is_low in ((0, lags.x_low), (1, jnp.logical_not(lags.y_up))):
        stats = rows[side * STATS : (side + 1) * STATS]
        (cosine, sine, cosine_last, sine_last), norms = two_rounds(stats[0], stats[1], stats[2:7], lags.gap, rows[FLAGS + side] > 0.5)
        here = jnp.where(is_low, sine_last, cosine_last)
        ahead = jnp.where(is_low, cosine_last, -sine_last)
        weights = [
            [here * cosine, ahead * left(sine, lags.gap)],
            [-here * sine, ahead * left(cosine, lags.gap)],
        ]
        sides.append((jnp.where(is_low, norms[1], norms[0]), weights, stats[7:], [cosine, sine, here, ahead]))
    (x_norms, x_weights, x_dots, x_turns), (y_norms, y_weights, y_dots, y_turns) = sides
    crossed = [
        joint(x_weights, rolled(y_weights, lag), rows[CROSS + 12 * index : CROSS + 12 * (index + 1)], lags.gap)
        for index, lag in enumerate(lags.crossed())
    ]
    firsts = joint(x_weights, rolled(x_weights, lags.turn), x_dots, lags.gap)
    seconds = left(joint(y_weights, rolled(y_weights, lags.turn), y_dots, lags.gap), lags.lag)
    couplings = (crossed[0], crossed[1], left(crossed[2], lags.turn), firsts, seconds)
    turns, (upper, lower) = two_rounds(x_norms, left(y_norms, lags.lag), couplings, lags.turn, rows[FLAGS + 2] > 0.5)
    norms = [right(upper, lags.x_shift) / total_rows, right(lower, lags.out) / total_rows]
    store_rows(out_ref, 0, x_turns + y_turns + list(turns) + norms + [jnp.zeros_like(upper)] * (ANGLES - NORMS - 2))


def last_kernel(offsets, mine_ref, other_ref, first_ref, second_ref, first_come, second_come,
                rotated_hbm, power_ref, rotated, sems):
    rows = rotated.shape[0]
    part = rows // CHUNKS
    is_even = (lax.axis_index("pairs") & 1) == 0
    on_first_core = (lax.axis_index("rows") & 1) == 0
    mine, other = mine_ref[...], other_ref[...]
    angles = [jnp.where(on_first_core, mine, other), jnp.where(on_first_core, other, mine)]
    lags = [Lags(offsets, slot) for slot in range(2)]
    for slot in range(2):
        power_ref[:, slot * BLOCK : (slot + 1) * BLOCK] = angles[slot][NORMS : NORMS + 1]
        power_ref[:, (2 + slot) * BLOCK : (3 + slot) * BLOCK] = angles[slot][NORMS + 1 : NORMS + 2]

    def turn(x, y, cosine, sine):
        return cosine * x - sine * y, sine * x + cosine * y

    def block_after(ref, span, values, gap):
        cosine, sine, here, ahead = values
        upper, lower = turn(*halves(ref, span), cosine, sine)
        return here * upper + ahead * left(lower, gap)

    def fill(sources):
        copies = []
        for chunk in range(CHUNKS):

            def body(step, _):
                span = pl.ds(pl.multiple_of(chunk * part + step * GROUP, GROUP), GROUP)
                for slot, (x_ref, y_ref) in enumerate(sources):
                    lag, values = lags[slot], [angles[slot][index : index + 1] for index in range(NORMS)]
                    upper = block_after(x_ref, span, values[:4], lag.gap)
                    lower = left(block_after(y_ref, span, values[4:8], lag.gap), lag.lag)
                    upper, lower = turn(upper, lower, values[8], values[9])
                    upper, lower = turn(upper, left(lower, lag.turn), values[10], values[11])
                    rotated[span, slot * BLOCK : (slot + 1) * BLOCK] = right(upper, lag.x_shift) if slot else upper
                    rotated[span, (2 + slot) * BLOCK : (3 + slot) * BLOCK] = right(lower, lag.out)
                return _

            lax.fori_loop(0, part // GROUP, body, 0, unroll=2)
            place = pl.ds(chunk * part, part)
            copy = pltpu.make_async_copy(rotated.at[place], rotated_hbm.at[place], sems.at[chunk])
            copy.start()
            copies.append(copy)
        for copy in copies:
            copy.wait()

    @pl.when(is_even)
    def _():
        fill([(second_come, first_ref), (second_ref, first_come)])

    @pl.when(jnp.logical_not(is_even))
    def _():
        fill([(first_come, second_ref), (first_ref, second_come)])


SMEM = pl.BlockSpec(memory_space=pltpu.SMEM)
VMEM = pl.BlockSpec(memory_space=pltpu.VMEM)
HBM = pl.BlockSpec(memory_space=pltpu.HBM)


def call(kernel, operands, outs, name, scratch=(), micros=1):
    return pl.pallas_call(
        kernel,
        out_shape=[jax.ShapeDtypeStruct(shape, jnp.float32) for shape, _ in outs],
        in_specs=[space for _, space in operands],
        out_specs=[space for _, space in outs],
        scratch_shapes=scratch,
        name=name,
        cost_estimate=pl.CostEstimate(flops=micros * 10**9, bytes_accessed=micros * 10**6, transcendentals=0),
        compiler_params=pltpu.CompilerParams(vmem_limit_bytes=VMEM_LIMIT),
    )(*[array for array, _ in operands])


def swap_rows(x, partner):
    size = lax.axis_size("rows")
    depth = size // 4

    def other(row):
        y, z, core = partner(row // (2 * depth), (row // 2) % depth, row % 2)
        return (y * depth + z) * 2 + core

    return lax.ppermute(x, "rows", [(row, other(row)) for row in range(size)])


OPPOSITE = (6, 7, 4, 5, 2, 3, 0, 1)


def per_device(loads, col_weights, partner_offsets, skip_mask):
    rows, columns = loads.shape
    pairs = lax.axis_size("pairs")
    weights = col_weights.reshape(1, columns)
    held = (rows + GROUP, 2 * BLOCK)
    first, second = call(
        load_kernel,
        [(partner_offsets, HBM), (skip_mask, HBM), (loads, HBM), (weights, HBM)],
        [(held, VMEM)] * 2,
        "load",
        [
            pltpu.SMEM(partner_offsets.shape, jnp.int32),
            pltpu.SMEM(skip_mask.shape, jnp.int32),
            pltpu.VMEM((rows, columns), jnp.float32),
            pltpu.VMEM((1, columns), jnp.float32),
            pltpu.SemaphoreType.DMA((CHUNKS + 3,)),
        ],
    )
    first_come = lax.ppermute(first, "pairs", [(at, at ^ 1) for at in range(pairs)])
    second_come = lax.ppermute(second, "pairs", [(at, min(max(((at + 1) ^ 1) - 1, 0), pairs - 1)) for at in range(pairs)])
    offsets, skips = (partner_offsets, SMEM), (skip_mask, SMEM)
    first_stats, second_stats = call(
        functools.partial(stats_kernel, rows), [offsets, (first, VMEM), (second, VMEM)], [((24, BLOCK), VMEM)] * 2, "stats"
    )
    slots = []
    for odd_slot, own, come, stats in ((0, second, first_come, second_stats), (1, first, second_come, first_stats)):
        slots += call(
            functools.partial(cross_kernel, rows, odd_slot),
            [offsets, skips, (own, VMEM), (come, VMEM), (stats, VMEM)],
            [((SUMS, BLOCK), VMEM)],
            "cross",
        )
    keeps_first = (lax.axis_index("pairs") & 1) == (lax.axis_index("rows") & 1)
    sums = jnp.where(keeps_first, slots[1], slots[0])
    sums = sums + swap_rows(jnp.where(keeps_first, slots[0], slots[1]), lambda y, z, core: (y, z, 1 - core))
    sums = sums + swap_rows(sums, lambda y, z, core: (1 - y, z, core))
    sums = sums + swap_rows(sums, lambda y, z, core: (y, z ^ 1, core))
    sums = sums + swap_rows(sums, lambda y, z, core: (y, z ^ 2, core))
    sums = sums + swap_rows(sums, lambda y, z, core: (y, OPPOSITE[z], core))
    total_rows = float(rows * lax.axis_size("rows"))
    (angles,) = call(functools.partial(angles_kernel, total_rows), [offsets, (sums, VMEM)], [((ANGLES, BLOCK), VMEM)], "angles")
    other = swap_rows(angles, lambda y, z, core: (y, z, 1 - core))
    rotated, power = call(
        last_kernel,
        [offsets] + [(array, VMEM) for array in (angles, other, first, second, first_come, second_come)],
        [((rows, columns), HBM), ((1, columns), VMEM)],
        "last",
        [pltpu.VMEM((rows, columns), jnp.float32), pltpu.SemaphoreType.DMA((CHUNKS,))],
    )
    return rotated, power.reshape(columns)


def solution(mesh):
    in_specs = (P("rows", "pairs"), P("pairs"), P(), P(None, "pairs"))
    out_specs = (P("rows", "pairs"), P("pairs"))
    return jax.shard_map(
        per_device, mesh=mesh, in_specs=in_specs, out_specs=out_specs, check_vma=False
    )
```

time: 750 us -> 55.6 us (0.07)
  waiting for transfers between devices: 523 us -> 8.93 us
  local copies, waits for them, and re-layouts: 112 us -> 3.74 us
  blocking collectives: 65 us -> 0 us
  between operations: 24.9 us -> 0.73 us
  Pallas kernels: 0 us -> 18.5 us
  starting transfers between devices: 7.65 us -> 23.5 us
    psum x2 -> x0, waiting for transfers between devices: 521 us -> none  [whole_gram(): return lax.psum(partial_gram, 'rows')]
    psum x1 -> x0, blocking collectives: 65 us -> none  [per_device(): lax.psum((jnp.sum(upper_blocks * upper_blocks, axis=1), jnp.sum(lower_blo...]
    psum x2 -> x0, local copies, waits for them, and re-layouts: 34.6 us -> none  [whole_gram(): return lax.psum(partial_gram, 'rows')]
    transpose x2 -> x0, local copies, waits for them, and re-layouts: 33 us -> none  [rotate_pair(): jnp.swapaxes(turn_columns(jnp.swapaxes(turned, 1, 2), cosine_values, sine...]
    dynamic_slice x5 -> x0, local copies, waits for them, and re-layouts: 21.6 us -> none  [the longest x4 21.5 us: rotate_pair(): jnp.roll(turned[:, :half_width, half_width:], -offset, axis=2)]
    pallas_call x0 -> x6, Pallas kernels: none -> 18.5 us  [call(): pl.pallas_call(kernel, out_shape=[jax.ShapeDtypeStruct(shape, jnp.float32...]
    gather x16 -> x0, local copies, waits for them, and re-layouts: 17 us -> none  [the longest x8 9.6 us: rotate_pair(): diagonal_values = jnp.diagonal(turned, axis1=1, axis2=2)]
    ppermute x2 -> x8, starting transfers between devices: 7.57 us -> 23.5 us  [the longest x6 18.6 us: swap_rows(): return lax.ppermute(x, 'rows', [(row, other(row)) for row in range(size)])]
  transfers between devices with their start and end apart: 4 -> 8, of which waited for: 4 -> 7; matrix products, arithmetic and copies ran while one was open for 0% -> 0% of each run, Pallas kernels for 0% -> 11%
where the time goes in v3:
time: 55.6 us; the launch traced here: 55.4 us
  starting transfers between devices  23.5 us (42%)
  Pallas kernels  18.5 us (33%)
  waiting for transfers between devices  8.93 us (16%)
  local copies, waits for them, and re-layouts  3.74 us (7%)
  between operations  0.73 us (1%)
    ppermute x6, starting transfers between devices, swap_rows(): return lax.ppermute(x, 'rows', [(row, other(row)) for row in range(size)])  18.6 us
    pallas_call x6, Pallas kernels, call(): pl.pallas_call(kernel, out_shape=[jax.ShapeDtypeStruct(shape, jnp.float32...  18.5 us
    ppermute x6, waiting for transfers between devices, swap_rows(): return lax.ppermute(x, 'rows', [(row, other(row)) for row in range(size)])  8.21 us
    unnamed x10, local copies, waits for them, and re-layouts  3.74 us
    ppermute x1, starting transfers between devices, per_device(): lax.ppermute(second, 'pairs', [(at, min(max((at + 1 ^ 1) - 1, 0), pairs -...  3.6 us
    ppermute x1, starting transfers between devices, per_device(): lax.ppermute(first, 'pairs', [(at, at ^ 1) for at in range(pairs)])  1.3 us
  transfers between devices with their start and end apart: 8, of which 7 were waited for; matrix products, arithmetic and copies ran while one was open for 0% of the time, Pallas kernels for 11%

profile of v3, /device:TPU:9, one launch (start us, length us, event | category | flops | bytes accessed | tf_op | source)
XLA Modules:
  0.0 55.4 jit_solution(14919440805519299840)
XLA Ops:
  0.6 0.0 copy-start.2
  0.6 0.7 %copy-done.2 = s32[2,2]{1,0:T(2,128)S(1)} copy-done((s32[2,2]{1,0:T(2,128)S(1)}, s32[2,2]{1,0:T(2,128)}, u32[]{:S(2)}) %copy-start.2) | copy-done | bytes 40
  1.3 0.0 copy-start
  1.3 1.0 %copy-done = f32[256,512]{1,0:T(8,128)S(1)} copy-done((f32[256,512]{1,0:T(8,128)S(1)}, f32[256,512]{1,0:T(8,128)}, u32[]{:S(2)}) %copy-start) | copy-done | bytes 524312
  2.4 0.0 copy-start.1
  2.4 0.7 %copy-done.1 = f32[512]{0:T(512)S(1)} copy-done((f32[512]{0:T(512)S(1)}, f32[512]{0:T(512)}, u32[]{:S(2)}) %copy-start.1) | copy-done | bytes 2072
  3.0 0.0 copy-start.3
  3.0 0.7 %copy-done.3 = s32[2,2]{1,0:T(2,128)S(1)} copy-done((s32[2,2]{1,0:T(2,128)S(1)}, s32[2,2]{1,0:T(2,128)}, u32[]{:S(2)}) %copy-start.3) | copy-done | bytes 40
  3.7 1.4 %load.1 = (f32[264,256]{1,0:T(8,128)S(1)}, f32[264,256]{1,0:T(8,128)S(1)}) custom-call(s32[2,2]{1,0:T(2,128)S(1)} %copy-done.3, s32[2,2]{1,0:T(2,128)S(1)} %copy-done.2, f32[256,512]{1,0:T(8,128)S(1)} %copy-done, f32[1,512]{1,0:T(1,128)S(1)} %bitcast.2), custom_call_target="tpu_custom_call" | custom-call | flops 1000000000 | bytes 1000000 | tf_op jit(solution)/shard_map/load/pallas_call | solution.py:295
  5.1 1.3 %collective-permute-start.1 = (f32[264,256]{1,0:T(8,128)S(1)}, f32[264,256]{1,0:T(8,128)S(1)}, u32[]{:S(2)}, u32[]{:S(2)}) collective-permute-start(f32[264,256]{1,0:T(8,128)S(1)} %get-tuple-element.8.first_ref.own_ref), channel_id=1, source_target_pairs={{0,1},{1,0},{2,3},{3,2},{4,5},{5,4},{6,7},{7,6},{8,9},{9,8},{10,11... | collective-permute-start | bytes 811016 | tf_op jit(solution)/shard_map/ppermute | solution.py:339
  6.4 3.6 %collective-permute-start = (f32[264,256]{1,0:T(8,128)S(1)}, f32[264,256]{1,0:T(8,128)S(1)}, u32[]{:S(2)}, u32[]{:S(2)}) collective-permute-start(f32[264,256]{1,0:T(8,128)S(1)} %get-tuple-element.9.second_ref.own_ref), channel_id=1, source_target_pairs={{0,0},{1,2},{2,1},{3,4},{4,3},{5,6},{6,5},{7,7},{8,8},{9,10},{10,9... | collective-permute-start | bytes 811016 | tf_op jit(solution)/shard_map/ppermute | solution.py:340
  10.0 0.0 copy-start.4
  10.0 0.7 %copy-done.4 = s32[2,2]{1,0:T(2,128)S(1)} copy-done((s32[2,2]{1,0:T(2,128)S(1)}, s32[2,2]{1,0:T(2,128)}, u32[]{:S(2)}) %copy-start.4) | copy-done | bytes 40
  10.7 2.3 %stats.1 = (f32[24,128]{1,0:T(8,128)S(1)}, f32[24,128]{1,0:T(8,128)S(1)}) custom-call(s32[2,2]{1,0:T(2,128)S(1)} %copy-done.4, f32[264,256]{1,0:T(8,128)S(1)} %get-tuple-element.8.first_ref.own_ref, f32[264,256]{1,0:T(8,128)S(1)} %get-tuple-element.9.second_ref.own_ref), custom_call_target="tpu_custom_call" | custom-call | flops 1000000000 | bytes 1000000 | tf_op jit(solution)/shard_map/stats/pallas_call | solution.py:295
  12.9 0.0 collective-permute-done.1.come_ref.first_come
  13.0 3.7 %cross.3 = f32[80,128]{1,0:T(8,128)S(1)} custom-call(s32[2,2]{1,0:T(2,128)S(1)} %copy-done.4, s32[2,2]{1,0:T(2,128)S(1)} %copy-done.2, f32[264,256]{1,0:T(8,128)S(1)} %get-tuple-element.9.second_ref.own_ref, f32[264,256]{1,0:T(8,128)S(1)} %collective-permute-done.1.come_ref.first_come, f32[24,128]{1,0:T(8,128)S(1)} %get-tuple-element.11.stats_ref), custom_call_target="tpu_custom_call" | custom-call | flops 1000000000 | bytes 1000000 | tf_op jit(solution)/shard_map/cross/pallas_call | solution.py:295
  16.7 0.7 %collective-permute-done.come_ref.second_come = f32[264,256]{1,0:T(8,128)S(1)} collective-permute-done((f32[264,256]{1,0:T(8,128)S(1)}, f32[264,256]{1,0:T(8,128)S(1)}, u32[]{:S(2)}, u32[]{:S(2)}) %collective-permute-start) | collective-permute-done | bytes 270368 | tf_op jit(solution)/shard_map/ppermute | solution.py:340
  17.4 3.7 %cross.2 = f32[80,128]{1,0:T(8,128)S(1)} custom-call(s32[2,2]{1,0:T(2,128)S(1)} %copy-done.4, s32[2,2]{1,0:T(2,128)S(1)} %copy-done.2, f32[264,256]{1,0:T(8,128)S(1)} %get-tuple-element.8.first_ref.own_ref, f32[264,256]{1,0:T(8,128)S(1)} %collective-permute-done.come_ref.second_come, f32[24,128]{1,0:T(8,128)S(1)} %get-tuple-element.10.stats_ref), custom_call_target="tpu_custom_call" | custom-call | flops 1000000000 | bytes 1000000 | tf_op jit(solution)/shard_map/cross/pallas_call | solution.py:295
  21.2 2.0 %collective-permute-start.2 = (f32[80,128]{1,0:T(8,128)S(1)}, f32[80,128]{1,0:T(8,128)S(1)}, u32[]{:S(2)}, u32[]{:S(2)}) collective-permute-start(f32[80,128]{1,0:T(8,128)S(1)} %broadcast_select_fusion), channel_id=1, source_target_pairs={{0,8},{8,0},{16,24},{24,16},{32,40},{40,32},{48,56},{56,48},{64,72... | collective-permute-start | bytes 122888 | tf_op jit(solution)/shard_map/ppermute | solution.py:315
  23.1 0.9 %collective-permute-done.2 = f32[80,128]{1,0:T(8,128)S(1)} collective-permute-done((f32[80,128]{1,0:T(8,128)S(1)}, f32[80,128]{1,0:T(8,128)S(1)}, u32[]{:S(2)}, u32[]{:S(2)}) %collective-permute-start.2) | collective-permute-done | bytes 40992 | tf_op jit(solution)/shard_map/ppermute | solution.py:315
  24.0 2.1 %collective-permute-start.3 = (f32[80,128]{1,0:T(8,128)S(1)}, f32[80,128]{1,0:T(8,128)S(1)}, u32[]{:S(2)}, u32[]{:S(2)}) collective-permute-start(f32[80,128]{1,0:T(8,128)S(1)} %select_add_fusion), channel_id=1, source_target_pairs={{0,128},{8,136},{16,144},{24,152},{32,160},{40,168},{48,176},{56,1... | collective-permute-start | bytes 122888 | tf_op jit(solution)/shard_map/ppermute | solution.py:315
  26.1 2.3 %collective-permute-done.3 = f32[80,128]{1,0:T(8,128)S(1)} collective-permute-done((f32[80,128]{1,0:T(8,128)S(1)}, f32[80,128]{1,0:T(8,128)S(1)}, u32[]{:S(2)}, u32[]{:S(2)}) %collective-permute-start.3) | collective-permute-done | bytes 40992 | tf_op jit(solution)/shard_map/ppermute | solution.py:315
  28.4 1.6 %collective-permute-start.4 = (f32[80,128]{1,0:T(8,128)S(1)}, f32[80,128]{1,0:T(8,128)S(1)}, u32[]{:S(2)}, u32[]{:S(2)}) collective-permute-start(f32[80,128]{1,0:T(8,128)S(1)} %add.16), channel_id=1, source_target_pairs={{0,16},{8,24},{16,0},{24,8},{32,48},{40,56},{48,32},{56,40},{64,80... | collective-permute-start | bytes 122888 | tf_op jit(solution)/shard_map/ppermute | solution.py:315
  30.1 1.4 %collective-permute-done.4 = f32[80,128]{1,0:T(8,128)S(1)} collective-permute-done((f32[80,128]{1,0:T(8,128)S(1)}, f32[80,128]{1,0:T(8,128)S(1)}, u32[]{:S(2)}, u32[]{:S(2)}) %collective-permute-start.4) | collective-permute-done | bytes 40992 | tf_op jit(solution)/shard_map/ppermute | solution.py:315
  31.5 3.0 %collective-permute-start.5 = (f32[80,128]{1,0:T(8,128)S(1)}, f32[80,128]{1,0:T(8,128)S(1)}, u32[]{:S(2)}, u32[]{:S(2)}) collective-permute-start(f32[80,128]{1,0:T(8,128)S(1)} %add.17), channel_id=1, source_target_pairs={{0,32},{8,40},{16,48},{24,56},{32,0},{40,8},{48,16},{56,24},{64,96... | collective-permute-start | bytes 122888 | tf_op jit(solution)/shard_map/ppermute | solution.py:315
  34.5 1.4 %collective-permute-done.5 = f32[80,128]{1,0:T(8,128)S(1)} collective-permute-done((f32[80,128]{1,0:T(8,128)S(1)}, f32[80,128]{1,0:T(8,128)S(1)}, u32[]{:S(2)}, u32[]{:S(2)}) %collective-permute-start.5) | collective-permute-done | bytes 40992 | tf_op jit(solution)/shard_map/ppermute | solution.py:315
  35.9 5.2 %collective-permute-start.6 = (f32[80,128]{1,0:T(8,128)S(1)}, f32[80,128]{1,0:T(8,128)S(1)}, u32[]{:S(2)}, u32[]{:S(2)}) collective-permute-start(f32[80,128]{1,0:T(8,128)S(1)} %add.18), channel_id=1, source_target_pairs={{0,96},{8,104},{16,112},{24,120},{32,64},{40,72},{48,80},{56,88},{... | collective-permute-start | bytes 122888 | tf_op jit(solution)/shard_map/ppermute | solution.py:315
  41.1 1.4 %collective-permute-done.6 = f32[80,128]{1,0:T(8,128)S(1)} collective-permute-done((f32[80,128]{1,0:T(8,128)S(1)}, f32[80,128]{1,0:T(8,128)S(1)}, u32[]{:S(2)}, u32[]{:S(2)}) %collective-permute-start.6) | collective-permute-done | bytes 40992 | tf_op jit(solution)/shard_map/ppermute | solution.py:315
  42.5 1.0 %angles.1.mine_ref = f32[16,128]{1,0:T(8,128)S(1)} custom-call(s32[2,2]{1,0:T(2,128)S(1)} %copy-done.4, f32[80,128]{1,0:T(8,128)S(1)} %add.19.sums_ref), custom_call_target="tpu_custom_call" | custom-call | flops 1000000000 | bytes 1000000 | tf_op jit(solution)/shard_map/angles/pallas_call | solution.py:295
  43.5 4.7 %collective-permute-start.7 = (f32[16,128]{1,0:T(8,128)S(1)}, f32[16,128]{1,0:T(8,128)S(1)}, u32[]{:S(2)}, u32[]{:S(2)}) collective-permute-start(f32[16,128]{1,0:T(8,128)S(1)} %angles.1.mine_ref), channel_id=1, source_target_pairs={{0,8},{8,0},{16,24},{24,16},{32,40},{40,32},{48,56},{56,48},{64,72... | collective-permute-start | bytes 24584 | tf_op jit(solution)/shard_map/ppermute | solution.py:315
  48.2 0.8 %collective-permute-done.7.other_ref = f32[16,128]{1,0:T(8,128)S(1)} collective-permute-done((f32[16,128]{1,0:T(8,128)S(1)}, f32[16,128]{1,0:T(8,128)S(1)}, u32[]{:S(2)}, u32[]{:S(2)}) %collective-permute-start.7) | collective-permute-done | bytes 8224 | tf_op jit(solution)/shard_map/ppermute | solution.py:315
  49.0 6.4 %last.1 = (f32[256,512]{1,0:T(8,128)}, f32[1,512]{1,0:T(1,128)}) custom-call(s32[2,2]{1,0:T(2,128)S(1)} %copy-done.4, f32[16,128]{1,0:T(8,128)S(1)} %angles.1.mine_ref, f32[16,128]{1,0:T(8,128)S(1)} %collective-permute-done.7.other_ref, f32[264,256]{1,0:T(8,128)S(1)} %get-tuple-element.8.first_ref.own_ref, ...), custom_call_target="tpu_custom_call" | custom-call | flops 1000000000 | bytes 1000000 | tf_op jit(solution)/shard_map/last/pallas_call | solution.py:295
  (6 shorter events, 0.0 us)
Async XLA Ops:
  0.6 0.7 %copy-start.2 = (s32[2,2]{1,0:T(2,128)S(1)}, s32[2,2]{1,0:T(2,128)}, u32[]{:S(2)}) copy-start(s32[2,2]{1,0:T(2,128)} %skip.3) | copy-start | bytes 52
  1.3 1.0 %copy-start = (f32[256,512]{1,0:T(8,128)S(1)}, f32[256,512]{1,0:T(8,128)}, u32[]{:S(2)}) copy-start(f32[256,512]{1,0:T(8,128)} %loads_hbm.1) | copy-start | bytes 1572868
  2.4 0.7 %copy-start.1 = (f32[512]{0:T(512)S(1)}, f32[512]{0:T(512)}, u32[]{:S(2)}) copy-start(f32[512]{0:T(512)} %param.5) | copy-start | bytes 6148
  3.0 0.7 %copy-start.3 = (s32[2,2]{1,0:T(2,128)S(1)}, s32[2,2]{1,0:T(2,128)}, u32[]{:S(2)}) copy-start(s32[2,2]{1,0:T(2,128)} %offsets.9) | copy-start | bytes 52
  5.1 7.9 %collective-permute-start.1 = (f32[264,256]{1,0:T(8,128)S(1)}, f32[264,256]{1,0:T(8,128)S(1)}, u32[]{:S(2)}, u32[]{:S(2)}) collective-permute-start(f32[264,256]{1,0:T(8,128)S(1)} %get-tuple-element.8.first_ref.own_ref), channel_id=1, source_target_pairs={{0,1},{1,0},{2,3},{3,2},{4,5},{5,4},{6,7},{7,6},{8,9},{9,8},{10,11... | collective-permute-start | bytes 811016 | tf_op jit(solution)/shard_map/ppermute | solution.py:339
  6.4 11.0 %collective-permute-start = (f32[264,256]{1,0:T(8,128)S(1)}, f32[264,256]{1,0:T(8,128)S(1)}, u32[]{:S(2)}, u32[]{:S(2)}) collective-permute-start(f32[264,256]{1,0:T(8,128)S(1)} %get-tuple-element.9.second_ref.own_ref), channel_id=1, source_target_pairs={{0,0},{1,2},{2,1},{3,4},{4,3},{5,6},{6,5},{7,7},{8,8},{9,10},{10,9... | collective-permute-start | bytes 811016 | tf_op jit(solution)/shard_map/ppermute | solution.py:340
  10.0 0.7 %copy-start.4 = (s32[2,2]{1,0:T(2,128)S(1)}, s32[2,2]{1,0:T(2,128)}, u32[]{:S(2)}) copy-start(s32[2,2]{1,0:T(2,128)} %offsets.9) | copy-start | bytes 52
  21.2 2.8 %collective-permute-start.2 = (f32[80,128]{1,0:T(8,128)S(1)}, f32[80,128]{1,0:T(8,128)S(1)}, u32[]{:S(2)}, u32[]{:S(2)}) collective-permute-start(f32[80,128]{1,0:T(8,128)S(1)} %broadcast_select_fusion), channel_id=1, source_target_pairs={{0,8},{8,0},{16,24},{24,16},{32,40},{40,32},{48,56},{56,48},{64,72... | collective-permute-start | bytes 122888 | tf_op jit(solution)/shard_map/ppermute | solution.py:315
  24.0 4.4 %collective-permute-start.3 = (f32[80,128]{1,0:T(8,128)S(1)}, f32[80,128]{1,0:T(8,128)S(1)}, u32[]{:S(2)}, u32[]{:S(2)}) collective-permute-start(f32[80,128]{1,0:T(8,128)S(1)} %select_add_fusion), channel_id=1, source_target_pairs={{0,128},{8,136},{16,144},{24,152},{32,160},{40,168},{48,176},{56,1... | collective-permute-start | bytes 122888 | tf_op jit(solution)/shard_map/ppermute | solution.py:315
  28.4 3.0 %collective-permute-start.4 = (f32[80,128]{1,0:T(8,128)S(1)}, f32[80,128]{1,0:T(8,128)S(1)}, u32[]{:S(2)}, u32[]{:S(2)}) collective-permute-start(f32[80,128]{1,0:T(8,128)S(1)} %add.16), channel_id=1, source_target_pairs={{0,16},{8,24},{16,0},{24,8},{32,48},{40,56},{48,32},{56,40},{64,80... | collective-permute-start | bytes 122888 | tf_op jit(solution)/shard_map/ppermute | solution.py:315
  31.5 4.4 %collective-permute-start.5 = (f32[80,128]{1,0:T(8,128)S(1)}, f32[80,128]{1,0:T(8,128)S(1)}, u32[]{:S(2)}, u32[]{:S(2)}) collective-permute-start(f32[80,128]{1,0:T(8,128)S(1)} %add.17), channel_id=1, source_target_pairs={{0,32},{8,40},{16,48},{24,56},{32,0},{40,8},{48,16},{56,24},{64,96... | collective-permute-start | bytes 122888 | tf_op jit(solution)/shard_map/ppermute | solution.py:315
  35.9 6.6 %collective-permute-start.6 = (f32[80,128]{1,0:T(8,128)S(1)}, f32[80,128]{1,0:T(8,128)S(1)}, u32[]{:S(2)}, u32[]{:S(2)}) collective-permute-start(f32[80,128]{1,0:T(8,128)S(1)} %add.18), channel_id=1, source_target_pairs={{0,96},{8,104},{16,112},{24,120},{32,64},{40,72},{48,80},{56,88},{... | collective-permute-start | bytes 122888 | tf_op jit(solution)/shard_map/ppermute | solution.py:315
  43.5 5.5 %collective-permute-start.7 = (f32[16,128]{1,0:T(8,128)S(1)}, f32[16,128]{1,0:T(8,128)S(1)}, u32[]{:S(2)}, u32[]{:S(2)}) collective-permute-start(f32[16,128]{1,0:T(8,128)S(1)} %angles.1.mine_ref), channel_id=1, source_target_pairs={{0,8},{8,0},{16,24},{24,16},{32,40},{40,32},{48,56},{56,48},{64,72... | collective-permute-start | bytes 24584 | tf_op jit(solution)/shard_map/ppermute | solution.py:315

commit v4 on v3

--- a/solution.py
+++ b/solution.py
@@ -8,7 +8,7 @@
 
 BLOCK = 128
 GROUP = 8
-CHUNKS = 4
+BATCH = 128
 
 STATS = 19
 CROSS = 2 * STATS
@@ -48,13 +48,11 @@
     return ref[span, :BLOCK], ref[span, BLOCK:]
 
 
-def sums_over(rows, count, terms):
-    def body(step, totals):
-        span = pl.ds(pl.multiple_of(step * GROUP, GROUP), GROUP)
-        return tuple(total + term for total, term in zip(totals, terms(span)))
-
-    zeros = tuple(jnp.zeros((GROUP, BLOCK), jnp.float32) for _ in range(count))
-    totals = lax.fori_loop(0, rows // GROUP, body, zeros, unroll=4)
+def sums_over(rows, terms):
+    totals = None
+    for start in range(0, rows, BATCH):
+        parts = [jnp.sum(term.reshape(BATCH // GROUP, GROUP, BLOCK), axis=0) for term in terms(slice(start, start + BATCH))]
+        totals = parts if totals is None else [total + part for total, part in zip(totals, parts)]
     return [jnp.sum(total, axis=0, keepdims=True) for total in totals]
 
 
@@ -78,7 +76,7 @@
         step_0 = [upper * upper, lower * lower, upper * lower, upper * lower_gap, upper_gap * lower, upper * upper_gap, lower * lower_gap]
         return step_0 + lagged((upper, lower), (upper, lower), lags.turn, lags.gap)
 
-    return sums_over(rows, STATS, terms)
+    return sums_over(rows, terms)
 
 
 def angle(first_norms, second_norms, coupling):
@@ -133,43 +131,38 @@
     return [[left(value, by) for value in pair] for pair in weights]
 
 
-def load_kernel(offsets_hbm, skip_hbm, loads_hbm, weights_hbm, first_ref, second_ref, offsets, skip, loads, weights, sems):
+def load_kernel(offsets_hbm, skip_hbm, loads_hbm, weights_hbm, first_hbm, second_hbm,
+                offsets, skip, loads, weights, held, in_sems, out_sems):
     rows = loads.shape[0]
-    part = rows // CHUNKS
-    small = [
-        pltpu.make_async_copy(offsets_hbm, offsets, sems.at[CHUNKS]),
-        pltpu.make_async_copy(skip_hbm, skip, sems.at[CHUNKS + 1]),
-        pltpu.make_async_copy(weights_hbm, weights, sems.at[CHUNKS + 2]),
-    ]
-    large = [
-        pltpu.make_async_copy(loads_hbm.at[pl.ds(chunk * part, part)], loads.at[pl.ds(chunk * part, part)], sems.at[chunk])
-        for chunk in range(CHUNKS)
-    ]
-    for copy in small + large:
+    parts = range(0, rows, BATCH)
+    small = [(offsets_hbm, offsets), (skip_hbm, skip), (weights_hbm, weights)]
+    large = [(loads_hbm.at[pl.ds(start, BATCH)], loads.at[pl.ds(start, BATCH)]) for start in parts]
+    copies = [pltpu.make_async_copy(*ends, in_sems.at[at]) for at, ends in enumerate(small + large)]
+    for copy in copies:
         copy.start()
-    for copy in small:
+    for copy in copies[:3]:
         copy.wait()
     is_even = (lax.axis_index("pairs") & 1) == 0
-    first = offsets[0, 0]
+    skips = [skip[0, pair].astype(jnp.float32) for pair in range(2)]
+    for at, order in enumerate((skips[::-1], skips)):
+        held[at, rows:, :] = jnp.full((GROUP, 2 * BLOCK), jnp.where(is_even, *order), jnp.float32)
     weight = [weights[:, block * BLOCK : (block + 1) * BLOCK] for block in range(4)]
-    for chunk in range(CHUNKS):
-        large[chunk].wait()
-
-        def body(step, _):
-            span = pl.ds(pl.multiple_of(chunk * part + step * GROUP, GROUP), GROUP)
-            blocks = [loads[span, block * BLOCK : (block + 1) * BLOCK] * weight[block] for block in range(4)]
-            lower_0, lower_1 = left(blocks[2], first), left(blocks[3], first)
-            first_ref[span, :BLOCK] = jnp.where(is_even, blocks[1], blocks[0])
-            first_ref[span, BLOCK:] = jnp.where(is_even, lower_1, lower_0)
-            second_ref[span, :BLOCK] = jnp.where(is_even, blocks[0], blocks[1])
-            second_ref[span, BLOCK:] = jnp.where(is_even, lower_0, lower_1)
-            return _
-
-        lax.fori_loop(0, part // GROUP, body, 0, unroll=4)
-    span = slice(rows, rows + GROUP)
-    skips = [skip[0, pair].astype(jnp.float32) for pair in range(2)]
-    first_ref[span, :] = jnp.full((GROUP, 2 * BLOCK), jnp.where(is_even, skips[1], skips[0]), jnp.float32)
-    second_ref[span, :] = jnp.full((GROUP, 2 * BLOCK), jnp.where(is_even, skips[0], skips[1]), jnp.float32)
+    sent = []
+    for part, start in enumerate(parts):
+        copies[3 + part].wait()
+        span = slice(start, start + BATCH)
+        blocks = [loads[span, block * BLOCK : (block + 1) * BLOCK] * weight[block] for block in range(4)]
+        blocks = blocks[:2] + [left(block, offsets[0, 0]) for block in blocks[2:]]
+        last = start + BATCH == rows
+        for at, out in enumerate((first_hbm, second_hbm)):
+            for half in range(2):
+                even, odd = blocks[2 * half + 1 - at], blocks[2 * half + at]
+                held[at, span, half * BLOCK : (half + 1) * BLOCK] = jnp.where(is_even, even, odd)
+            place = pl.ds(start, BATCH + GROUP if last else BATCH)
+            sent.append(pltpu.make_async_copy(held.at[at, place], out.at[place], out_sems.at[at, part]))
+            sent[-1].start()
+    for copy in sent:
+        copy.wait()
 
 
 def stats_kernel(rows, offsets, first_ref, second_ref, first_out, second_out):
@@ -188,21 +181,16 @@
     step_flag = jnp.full((1, BLOCK), jnp.where(own_first, skip[1, 1], skip[1, 0]).astype(jnp.float32), jnp.float32)
     own_stats = [stats_ref[index : index + 1, :] for index in range(STATS)]
 
-    def fill(x_ref, y_ref, x_stats, y_stats, flags):
-        store_rows(out_ref, 0, x_stats)
-        store_rows(out_ref, STATS, y_stats)
-        for index, lag in enumerate(lags.crossed()):
-            sums = sums_over(rows, 12, lambda span: lagged(halves(x_ref, span), halves(y_ref, span), lag, lags.gap))
-            store_rows(out_ref, CROSS + 12 * index, sums)
-        store_rows(out_ref, FLAGS, flags + [jnp.zeros((1, BLOCK), jnp.float32)] * (SUMS - FLAGS - 3))
-
-    @pl.when(own_first)
-    def _():
-        fill(own_ref, come_ref, own_stats, come_stats, [own_flag, come_flag, step_flag])
-
-    @pl.when(jnp.logical_not(own_first))
-    def _():
-        fill(come_ref, own_ref, come_stats, own_stats, [come_flag, own_flag, step_flag])
+    def pick(mine, theirs):
+        return [jnp.where(own_first, a, b) for a, b in zip(mine, theirs)], [jnp.where(own_first, b, a) for a, b in zip(mine, theirs)]
+
+    for start, stats in zip((0, STATS), pick(own_stats, come_stats)):
+        store_rows(out_ref, start, stats)
+    for index, lag in enumerate(lags.crossed()):
+        sums = sums_over(rows, lambda span: lagged(*pick(halves(own_ref, span), halves(come_ref, span)), lag, lags.gap))
+        store_rows(out_ref, CROSS + 12 * index, sums)
+    x_flag, y_flag = pick([own_flag], [come_flag])
+    store_rows(out_ref, FLAGS, x_flag + y_flag + [step_flag] + [jnp.zeros((1, BLOCK), jnp.float32)] * (SUMS - FLAGS - 3))
 
 
 def angles_kernel(total_rows, offsets, sums_ref, out_ref):
@@ -232,66 +220,58 @@
     store_rows(out_ref, 0, x_turns + y_turns + list(turns) + norms + [jnp.zeros_like(upper)] * (ANGLES - NORMS - 2))
 
 
+def turn(x, y, cosine, sine):
+    return cosine * x - sine * y, sine * x + cosine * y
+
+
+def block_after(pair, turns, gap):
+    cosine, sine, here, ahead = turns
+    upper, lower = turn(*pair, cosine, sine)
+    return here * upper + ahead * left(lower, gap)
+
+
 def last_kernel(offsets, mine_ref, other_ref, first_ref, second_ref, first_come, second_come,
-                rotated_hbm, power_ref, rotated, sems):
+                rotated_hbm, power_hbm, rotated, power, sems):
     rows = rotated.shape[0]
-    part = rows // CHUNKS
     is_even = (lax.axis_index("pairs") & 1) == 0
     on_first_core = (lax.axis_index("rows") & 1) == 0
     mine, other = mine_ref[...], other_ref[...]
-    angles = [jnp.where(on_first_core, mine, other), jnp.where(on_first_core, other, mine)]
-    lags = [Lags(offsets, slot) for slot in range(2)]
+    sources = (((second_come, first_come), (first_ref, second_ref)), ((second_ref, first_ref), (first_come, second_come)))
+    slots = [jnp.where(on_first_core, mine, other), jnp.where(on_first_core, other, mine)]
     for slot in range(2):
-        power_ref[:, slot * BLOCK : (slot + 1) * BLOCK] = angles[slot][NORMS : NORMS + 1]
-        power_ref[:, (2 + slot) * BLOCK : (3 + slot) * BLOCK] = angles[slot][NORMS + 1 : NORMS + 2]
-
-    def turn(x, y, cosine, sine):
-        return cosine * x - sine * y, sine * x + cosine * y
-
-    def block_after(ref, span, values, gap):
-        cosine, sine, here, ahead = values
-        upper, lower = turn(*halves(ref, span), cosine, sine)
-        return here * upper + ahead * left(lower, gap)
-
-    def fill(sources):
-        copies = []
-        for chunk in range(CHUNKS):
-
-            def body(step, _):
-                span = pl.ds(pl.multiple_of(chunk * part + step * GROUP, GROUP), GROUP)
-                for slot, (x_ref, y_ref) in enumerate(sources):
-                    lag, values = lags[slot], [angles[slot][index : index + 1] for index in range(NORMS)]
-                    upper = block_after(x_ref, span, values[:4], lag.gap)
-                    lower = left(block_after(y_ref, span, values[4:8], lag.gap), lag.lag)
-                    upper, lower = turn(upper, lower, values[8], values[9])
-                    upper, lower = turn(upper, left(lower, lag.turn), values[10], values[11])
-                    rotated[span, slot * BLOCK : (slot + 1) * BLOCK] = right(upper, lag.x_shift) if slot else upper
-                    rotated[span, (2 + slot) * BLOCK : (3 + slot) * BLOCK] = right(lower, lag.out)
-                return _
-
-            lax.fori_loop(0, part // GROUP, body, 0, unroll=2)
-            place = pl.ds(chunk * part, part)
-            copy = pltpu.make_async_copy(rotated.at[place], rotated_hbm.at[place], sems.at[chunk])
-            copy.start()
-            copies.append(copy)
-        for copy in copies:
-            copy.wait()
-
-    @pl.when(is_even)
-    def _():
-        fill([(second_come, first_ref), (second_ref, first_come)])
-
-    @pl.when(jnp.logical_not(is_even))
-    def _():
-        fill([(first_come, second_ref), (first_ref, second_come)])
-
-
-SMEM = pl.BlockSpec(memory_space=pltpu.SMEM)
+        for half in range(2):
+            at = 2 * half + slot
+            power[:, at * BLOCK : (at + 1) * BLOCK] = slots[slot][NORMS + half : NORMS + half + 1]
+    copies = [pltpu.make_async_copy(power, power_hbm, sems.at[4])]
+    copies[0].start()
+    for slot, angles in enumerate(slots):
+        lags = Lags(offsets, slot)
+        blocks = [slice(at * BLOCK, (at + 1) * BLOCK) for at in (slot, 2 + slot)]
+        turns = [angles[index : index + 1] for index in range(NORMS)]
+        for start in range(0, rows, BATCH):
+            span = slice(start, start + BATCH)
+            x, y = [
+                [jnp.where(is_even, a, b) for a, b in zip(halves(even_ref, span), halves(odd_ref, span))]
+                for even_ref, odd_ref in sources[slot]
+            ]
+            upper = block_after(x, turns[:4], lags.gap)
+            lower = left(block_after(y, turns[4:8], lags.gap), lags.lag)
+            upper, lower = turn(upper, lower, turns[8], turns[9])
+            upper, lower = turn(upper, left(lower, lags.turn), turns[10], turns[11])
+            rotated[span, blocks[0]] = right(upper, lags.x_shift) if slot else upper
+            rotated[span, blocks[1]] = right(lower, lags.out)
+        for half, columns in enumerate(blocks):
+            copies.append(pltpu.make_async_copy(rotated.at[:, columns], rotated_hbm.at[:, columns], sems.at[2 * slot + half]))
+            copies[-1].start()
+    for copy in copies:
+        copy.wait()
+
+
 VMEM = pl.BlockSpec(memory_space=pltpu.VMEM)
 HBM = pl.BlockSpec(memory_space=pltpu.HBM)
 
 
-def call(kernel, operands, outs, name, scratch=(), micros=1):
+def call(kernel, operands, outs, name, scratch=(), micros=1, grant=VMEM_LIMIT):
     return pl.pallas_call(
         kernel,
         out_shape=[jax.ShapeDtypeStruct(shape, jnp.float32) for shape, _ in outs],
@@ -300,7 +280,7 @@
         scratch_shapes=scratch,
         name=name,
         cost_estimate=pl.CostEstimate(flops=micros * 10**9, bytes_accessed=micros * 10**6, transcendentals=0),
-        compiler_params=pltpu.CompilerParams(vmem_limit_bytes=VMEM_LIMIT),
+        compiler_params=pltpu.CompilerParams(vmem_limit_bytes=grant),
     )(*[array for array, _ in operands])
 
 
@@ -326,19 +306,22 @@
     first, second = call(
         load_kernel,
         [(partner_offsets, HBM), (skip_mask, HBM), (loads, HBM), (weights, HBM)],
-        [(held, VMEM)] * 2,
+        [(held, HBM)] * 2,
         "load",
         [
-            pltpu.SMEM(partner_offsets.shape, jnp.int32),
-            pltpu.SMEM(skip_mask.shape, jnp.int32),
+            pltpu.VMEM(partner_offsets.shape, jnp.int32),
+            pltpu.VMEM(skip_mask.shape, jnp.int32),
             pltpu.VMEM((rows, columns), jnp.float32),
             pltpu.VMEM((1, columns), jnp.float32),
-            pltpu.SemaphoreType.DMA((CHUNKS + 3,)),
+            pltpu.VMEM((2,) + held, jnp.float32),
+            pltpu.SemaphoreType.DMA((3 + rows // BATCH,)),
+            pltpu.SemaphoreType.DMA((2, rows // BATCH)),
         ],
+        grant=None,
     )
     first_come = lax.ppermute(first, "pairs", [(at, at ^ 1) for at in range(pairs)])
     second_come = lax.ppermute(second, "pairs", [(at, min(max(((at + 1) ^ 1) - 1, 0), pairs - 1)) for at in range(pairs)])
-    offsets, skips = (partner_offsets, SMEM), (skip_mask, SMEM)
+    offsets, skips = (partner_offsets, VMEM), (skip_mask, VMEM)
     first_stats, second_stats = call(
         functools.partial(stats_kernel, rows), [offsets, (first, VMEM), (second, VMEM)], [((24, BLOCK), VMEM)] * 2, "stats"
     )
@@ -363,9 +346,9 @@
     rotated, power = call(
         last_kernel,
         [offsets] + [(array, VMEM) for array in (angles, other, first, second, first_come, second_come)],
-        [((rows, columns), HBM), ((1, columns), VMEM)],
+        [((rows, columns), HBM), ((1, columns), HBM)],
         "last",
-        [pltpu.VMEM((rows, columns), jnp.float32), pltpu.SemaphoreType.DMA((CHUNKS,))],
+        [pltpu.VMEM((rows, columns), jnp.float32), pltpu.VMEM((1, columns), jnp.float32), pltpu.SemaphoreType.DMA((5,))],
     )
     return rotated, power.reshape(columns)
 

time: 55.6 us -> 45.4 us (0.82)
  Pallas kernels: 18.5 us -> 6.99 us
  waiting for transfers between devices: 8.93 us -> 10.7 us
    pallas_call x6, Pallas kernels: 18.5 us -> 6.99 us  [call(): pl.pallas_call(kernel, out_shape=[jax.ShapeDtypeStruct(shape, jnp.float32...]
    ppermute x1, waiting for transfers between devices: 0.71 us -> 2.44 us  [per_device(): lax.ppermute(second, 'pairs', [(at, min(max((at + 1 ^ 1) - 1, 0), pairs -...]
    unnamed x10 -> x12, local copies, waits for them, and re-layouts: 3.74 us -> 3.26 us
  transfers between devices with their start and end apart: 8 -> 8, of which waited for: 7 -> 7; matrix products, arithmetic and copies ran while one was open for 0% -> 0% of each run, Pallas kernels for 11% -> 4%
where the time goes in v4:
time: 45.4 us; the launch traced here: 45.2 us
  starting transfers between devices  23.5 us (52%)
  waiting for transfers between devices  10.7 us (24%)
  Pallas kernels  6.99 us (15%)
  local copies, waits for them, and re-layouts  3.26 us (7%)
  between operations  0.72 us (2%)
    ppermute x6, starting transfers between devices, swap_rows(): return lax.ppermute(x, 'rows', [(row, other(row)) for row in range(size)])  18.6 us
    ppermute x6, waiting for transfers between devices, swap_rows(): return lax.ppermute(x, 'rows', [(row, other(row)) for row in range(size)])  8.21 us
    pallas_call x6, Pallas kernels, call(): pl.pallas_call(kernel, out_shape=[jax.ShapeDtypeStruct(shape, jnp.float32...  6.99 us
    ppermute x1, starting transfers between devices, per_device(): lax.ppermute(second, 'pairs', [(at, min(max((at + 1 ^ 1) - 1, 0), pairs -...  3.6 us
    unnamed x12, local copies, waits for them, and re-layouts  3.26 us
    ppermute x1, waiting for transfers between devices, per_device(): lax.ppermute(second, 'pairs', [(at, min(max((at + 1 ^ 1) - 1, 0), pairs -...  2.44 us
    ppermute x1, starting transfers between devices, per_device(): lax.ppermute(first, 'pairs', [(at, at ^ 1) for at in range(pairs)])  1.3 us
  transfers between devices with their start and end apart: 8, of which 7 were waited for; matrix products, arithmetic and copies ran while one was open for 0% of the time, Pallas kernels for 4%

profile of v4, /device:TPU:9, one launch (start us, length us, event | category | flops | bytes accessed | tf_op | source)
XLA Modules:
  0.0 45.2 jit_solution(11490041187927529455)
XLA Ops:
  0.6 2.0 %load.1 = (f32[264,256]{1,0:T(8,128)}, f32[264,256]{1,0:T(8,128)}) custom-call(s32[2,2]{1,0:T(2,128)} %offsets.9, s32[2,2]{1,0:T(2,128)} %skip.3, f32[256,512]{1,0:T(8,128)} %loads_hbm.1, f32[1,512]{1,0:T(1,128)} %bitcast.2), custom_call_target="tpu_custom_call" | custom-call | flops 1000000000 | bytes 1000000 | tf_op jit(solution)/shard_map/load/pallas_call | solution.py:275
  2.7 1.3 %collective-permute-start.1 = (f32[264,256]{1,0:T(8,128)}, f32[264,256]{1,0:T(8,128)S(1)}, u32[]{:S(2)}, u32[]{:S(2)}) collective-permute-start(f32[264,256]{1,0:T(8,128)} %get-tuple-element.8.first_ref.own_ref), channel_id=1, source_target_pairs={{0,1},{1,0},{2,3},{3,2},{4,5},{5,4},{6,7},{7,6},{8,9},{9,8},{10,11... | collective-permute-start | bytes 811016 | tf_op jit(solution)/shard_map/ppermute | solution.py:322
  4.0 3.6 %collective-permute-start = (f32[264,256]{1,0:T(8,128)}, f32[264,256]{1,0:T(8,128)S(1)}, u32[]{:S(2)}, u32[]{:S(2)}) collective-permute-start(f32[264,256]{1,0:T(8,128)} %get-tuple-element.9.second_ref.own_ref), channel_id=1, source_target_pairs={{0,0},{1,2},{2,1},{3,4},{4,3},{5,6},{6,5},{7,7},{8,8},{9,10},{10,9... | collective-permute-start | bytes 811016 | tf_op jit(solution)/shard_map/ppermute | solution.py:323
  7.6 0.0 copy-start.5
  7.6 0.7 %copy-done.5 = s32[2,2]{1,0:T(2,128)S(1)} copy-done((s32[2,2]{1,0:T(2,128)S(1)}, s32[2,2]{1,0:T(2,128)}, u32[]{:S(2)}) %copy-start.5) | copy-done | bytes 40
  8.3 0.0 copy-start
  8.3 1.0 %copy-done = f32[264,256]{1,0:T(8,128)S(1)} copy-done((f32[264,256]{1,0:T(8,128)S(1)}, f32[264,256]{1,0:T(8,128)}, u32[]{:S(2)}) %copy-start) | copy-done | bytes 270360
  9.2 0.0 copy-start.2
  9.2 1.0 %copy-done.2 = f32[264,256]{1,0:T(8,128)S(1)} copy-done((f32[264,256]{1,0:T(8,128)S(1)}, f32[264,256]{1,0:T(8,128)}, u32[]{:S(2)}) %copy-start.2) | copy-done | bytes 270360
  10.2 0.0 copy-start.3
  10.2 0.7 %stats.1 = (f32[24,128]{1,0:T(8,128)S(1)}, f32[24,128]{1,0:T(8,128)S(1)}) custom-call(s32[2,2]{1,0:T(2,128)S(1)} %copy-done.5, f32[264,256]{1,0:T(8,128)S(1)} %copy-done, f32[264,256]{1,0:T(8,128)S(1)} %copy-done.2), custom_call_target="tpu_custom_call" | custom-call | flops 1000000000 | bytes 1000000 | tf_op jit(solution)/shard_map/stats/pallas_call | solution.py:275
  10.9 0.0 copy-start.4
  10.9 0.0 collective-permute-done.1.come_ref.first_come
  11.0 0.2 copy-done.3
  11.1 0.5 %copy-done.4 = s32[2,2]{1,0:T(2,128)S(1)} copy-done((s32[2,2]{1,0:T(2,128)S(1)}, s32[2,2]{1,0:T(2,128)}, u32[]{:S(2)}) %copy-start.4) | copy-done | bytes 40
  11.6 0.0 copy-start.1
  11.6 1.1 %cross.3 = f32[80,128]{1,0:T(8,128)S(1)} custom-call(s32[2,2]{1,0:T(2,128)S(1)} %copy-done.5, s32[2,2]{1,0:T(2,128)S(1)} %copy-done.4, f32[264,256]{1,0:T(8,128)S(1)} %copy-done.3, f32[264,256]{1,0:T(8,128)S(1)} %collective-permute-done.1.come_ref.first_come, f32[24,128]{1,0:T(8,128)S(1)} %get-tuple-element.11.stats_ref), custom_call_target="tpu_custom_call" | custom-call | flops 1000000000 | bytes 1000000 | tf_op jit(solution)/shard_map/cross/pallas_call | solution.py:275
  12.8 2.4 %collective-permute-done.come_ref.second_come = f32[264,256]{1,0:T(8,128)S(1)} collective-permute-done((f32[264,256]{1,0:T(8,128)}, f32[264,256]{1,0:T(8,128)S(1)}, u32[]{:S(2)}, u32[]{:S(2)}) %collective-permute-start) | collective-permute-done | bytes 270368 | tf_op jit(solution)/shard_map/ppermute | solution.py:323
  15.2 0.0 copy-done.1
  15.2 1.2 %cross.2 = f32[80,128]{1,0:T(8,128)S(1)} custom-call(s32[2,2]{1,0:T(2,128)S(1)} %copy-done.5, s32[2,2]{1,0:T(2,128)S(1)} %copy-done.4, f32[264,256]{1,0:T(8,128)S(1)} %copy-done.1, f32[264,256]{1,0:T(8,128)S(1)} %collective-permute-done.come_ref.second_come, f32[24,128]{1,0:T(8,128)S(1)} %get-tuple-element.10.stats_ref), custom_call_target="tpu_custom_call" | custom-call | flops 1000000000 | bytes 1000000 | tf_op jit(solution)/shard_map/cross/pallas_call | solution.py:275
  16.4 2.0 %collective-permute-start.2 = (f32[80,128]{1,0:T(8,128)S(1)}, f32[80,128]{1,0:T(8,128)S(1)}, u32[]{:S(2)}, u32[]{:S(2)}) collective-permute-start(f32[80,128]{1,0:T(8,128)S(1)} %broadcast_select_fusion), channel_id=1, source_target_pairs={{0,8},{8,0},{16,24},{24,16},{32,40},{40,32},{48,56},{56,48},{64,72... | collective-permute-start | bytes 122888 | tf_op jit(solution)/shard_map/ppermute | solution.py:295
  18.4 0.9 %collective-permute-done.2 = f32[80,128]{1,0:T(8,128)S(1)} collective-permute-done((f32[80,128]{1,0:T(8,128)S(1)}, f32[80,128]{1,0:T(8,128)S(1)}, u32[]{:S(2)}, u32[]{:S(2)}) %collective-permute-start.2) | collective-permute-done | bytes 40992 | tf_op jit(solution)/shard_map/ppermute | solution.py:295
  19.2 2.1 %collective-permute-start.3 = (f32[80,128]{1,0:T(8,128)S(1)}, f32[80,128]{1,0:T(8,128)S(1)}, u32[]{:S(2)}, u32[]{:S(2)}) collective-permute-start(f32[80,128]{1,0:T(8,128)S(1)} %select_add_fusion), channel_id=1, source_target_pairs={{0,128},{8,136},{16,144},{24,152},{32,160},{40,168},{48,176},{56,1... | collective-permute-start | bytes 122888 | tf_op jit(solution)/shard_map/ppermute | solution.py:295
  21.3 2.3 %collective-permute-done.3 = f32[80,128]{1,0:T(8,128)S(1)} collective-permute-done((f32[80,128]{1,0:T(8,128)S(1)}, f32[80,128]{1,0:T(8,128)S(1)}, u32[]{:S(2)}, u32[]{:S(2)}) %collective-permute-start.3) | collective-permute-done | bytes 40992 | tf_op jit(solution)/shard_map/ppermute | solution.py:295
  23.7 1.6 %collective-permute-start.4 = (f32[80,128]{1,0:T(8,128)S(1)}, f32[80,128]{1,0:T(8,128)S(1)}, u32[]{:S(2)}, u32[]{:S(2)}) collective-permute-start(f32[80,128]{1,0:T(8,128)S(1)} %add.16), channel_id=1, source_target_pairs={{0,16},{8,24},{16,0},{24,8},{32,48},{40,56},{48,32},{56,40},{64,80... | collective-permute-start | bytes 122888 | tf_op jit(solution)/shard_map/ppermute | solution.py:295
  25.3 1.4 %collective-permute-done.4 = f32[80,128]{1,0:T(8,128)S(1)} collective-permute-done((f32[80,128]{1,0:T(8,128)S(1)}, f32[80,128]{1,0:T(8,128)S(1)}, u32[]{:S(2)}, u32[]{:S(2)}) %collective-permute-start.4) | collective-permute-done | bytes 40992 | tf_op jit(solution)/shard_map/ppermute | solution.py:295
  26.7 3.0 %collective-permute-start.5 = (f32[80,128]{1,0:T(8,128)S(1)}, f32[80,128]{1,0:T(8,128)S(1)}, u32[]{:S(2)}, u32[]{:S(2)}) collective-permute-start(f32[80,128]{1,0:T(8,128)S(1)} %add.17), channel_id=1, source_target_pairs={{0,32},{8,40},{16,48},{24,56},{32,0},{40,8},{48,16},{56,24},{64,96... | collective-permute-start | bytes 122888 | tf_op jit(solution)/shard_map/ppermute | solution.py:295
  29.7 1.4 %collective-permute-done.5 = f32[80,128]{1,0:T(8,128)S(1)} collective-permute-done((f32[80,128]{1,0:T(8,128)S(1)}, f32[80,128]{1,0:T(8,128)S(1)}, u32[]{:S(2)}, u32[]{:S(2)}) %collective-permute-start.5) | collective-permute-done | bytes 40992 | tf_op jit(solution)/shard_map/ppermute | solution.py:295
  31.1 5.2 %collective-permute-start.6 = (f32[80,128]{1,0:T(8,128)S(1)}, f32[80,128]{1,0:T(8,128)S(1)}, u32[]{:S(2)}, u32[]{:S(2)}) collective-permute-start(f32[80,128]{1,0:T(8,128)S(1)} %add.18), channel_id=1, source_target_pairs={{0,96},{8,104},{16,112},{24,120},{32,64},{40,72},{48,80},{56,88},{... | collective-permute-start | bytes 122888 | tf_op jit(solution)/shard_map/ppermute | solution.py:295
  36.3 1.4 %collective-permute-done.6 = f32[80,128]{1,0:T(8,128)S(1)} collective-permute-done((f32[80,128]{1,0:T(8,128)S(1)}, f32[80,128]{1,0:T(8,128)S(1)}, u32[]{:S(2)}, u32[]{:S(2)}) %collective-permute-start.6) | collective-permute-done | bytes 40992 | tf_op jit(solution)/shard_map/ppermute | solution.py:295
  37.7 0.5 %angles.1.mine_ref = f32[16,128]{1,0:T(8,128)S(1)} custom-call(s32[2,2]{1,0:T(2,128)S(1)} %copy-done.5, f32[80,128]{1,0:T(8,128)S(1)} %add.19.sums_ref), custom_call_target="tpu_custom_call" | custom-call | flops 1000000000 | bytes 1000000 | tf_op jit(solution)/shard_map/angles/pallas_call | solution.py:275
  38.2 4.7 %collective-permute-start.7 = (f32[16,128]{1,0:T(8,128)S(1)}, f32[16,128]{1,0:T(8,128)S(1)}, u32[]{:S(2)}, u32[]{:S(2)}) collective-permute-start(f32[16,128]{1,0:T(8,128)S(1)} %angles.1.mine_ref), channel_id=1, source_target_pairs={{0,8},{8,0},{16,24},{24,16},{32,40},{40,32},{48,56},{56,48},{64,72... | collective-permute-start | bytes 24584 | tf_op jit(solution)/shard_map/ppermute | solution.py:295
  42.9 0.8 %collective-permute-done.7.other_ref = f32[16,128]{1,0:T(8,128)S(1)} collective-permute-done((f32[16,128]{1,0:T(8,128)S(1)}, f32[16,128]{1,0:T(8,128)S(1)}, u32[]{:S(2)}, u32[]{:S(2)}) %collective-permute-start.7) | collective-permute-done | bytes 8224 | tf_op jit(solution)/shard_map/ppermute | solution.py:295
  43.8 1.4 %last.1 = (f32[256,512]{1,0:T(8,128)}, f32[1,512]{1,0:T(1,128)}) custom-call(s32[2,2]{1,0:T(2,128)S(1)} %copy-done.5, f32[16,128]{1,0:T(8,128)S(1)} %angles.1.mine_ref, f32[16,128]{1,0:T(8,128)S(1)} %collective-permute-done.7.other_ref, f32[264,256]{1,0:T(8,128)S(1)} %copy-done.1, f32[264,256]{1,0:T(8,128)S(1)} %copy-done.3, ...), custom_call_target="tpu_custom_call" | custom-call | flops 1000000000 | bytes 1000000 | tf_op jit(solution)/shard_map/last/pallas_call | solution.py:275
  (6 shorter events, 0.0 us)
Async XLA Ops:
  2.7 8.3 %collective-permute-start.1 = (f32[264,256]{1,0:T(8,128)}, f32[264,256]{1,0:T(8,128)S(1)}, u32[]{:S(2)}, u32[]{:S(2)}) collective-permute-start(f32[264,256]{1,0:T(8,128)} %get-tuple-element.8.first_ref.own_ref), channel_id=1, source_target_pairs={{0,1},{1,0},{2,3},{3,2},{4,5},{5,4},{6,7},{7,6},{8,9},{9,8},{10,11... | collective-permute-start | bytes 811016 | tf_op jit(solution)/shard_map/ppermute | solution.py:322
  4.0 11.2 %collective-permute-start = (f32[264,256]{1,0:T(8,128)}, f32[264,256]{1,0:T(8,128)S(1)}, u32[]{:S(2)}, u32[]{:S(2)}) collective-permute-start(f32[264,256]{1,0:T(8,128)} %get-tuple-element.9.second_ref.own_ref), channel_id=1, source_target_pairs={{0,0},{1,2},{2,1},{3,4},{4,3},{5,6},{6,5},{7,7},{8,8},{9,10},{10,9... | collective-permute-start | bytes 811016 | tf_op jit(solution)/shard_map/ppermute | solution.py:323
  7.6 0.7 %copy-start.5 = (s32[2,2]{1,0:T(2,128)S(1)}, s32[2,2]{1,0:T(2,128)}, u32[]{:S(2)}) copy-start(s32[2,2]{1,0:T(2,128)} %offsets.9) | copy-start | bytes 52
  8.3 1.0 %copy-start = (f32[264,256]{1,0:T(8,128)S(1)}, f32[264,256]{1,0:T(8,128)}, u32[]{:S(2)}) copy-start(f32[264,256]{1,0:T(8,128)} %get-tuple-element.8.first_ref.own_ref) | copy-start | bytes 811012
  9.2 1.0 %copy-start.2 = (f32[264,256]{1,0:T(8,128)S(1)}, f32[264,256]{1,0:T(8,128)}, u32[]{:S(2)}) copy-start(f32[264,256]{1,0:T(8,128)} %get-tuple-element.9.second_ref.own_ref) | copy-start | bytes 811012
  10.2 1.0 %copy-start.3 = (f32[264,256]{1,0:T(8,128)S(1)}, f32[264,256]{1,0:T(8,128)}, u32[]{:S(2)}) copy-start(f32[264,256]{1,0:T(8,128)} %get-tuple-element.9.second_ref.own_ref) | copy-start | bytes 811012
  10.9 0.7 %copy-start.4 = (s32[2,2]{1,0:T(2,128)S(1)}, s32[2,2]{1,0:T(2,128)}, u32[]{:S(2)}) copy-start(s32[2,2]{1,0:T(2,128)} %skip.3) | copy-start | bytes 52
  11.6 3.6 %copy-start.1 = (f32[264,256]{1,0:T(8,128)S(1)}, f32[264,256]{1,0:T(8,128)}, u32[]{:S(2)}) copy-start(f32[264,256]{1,0:T(8,128)} %get-tuple-element.8.first_ref.own_ref) | copy-start | bytes 811012
  16.4 2.8 %collective-permute-start.2 = (f32[80,128]{1,0:T(8,128)S(1)}, f32[80,128]{1,0:T(8,128)S(1)}, u32[]{:S(2)}, u32[]{:S(2)}) collective-permute-start(f32[80,128]{1,0:T(8,128)S(1)} %broadcast_select_fusion), channel_id=1, source_target_pairs={{0,8},{8,0},{16,24},{24,16},{32,40},{40,32},{48,56},{56,48},{64,72... | collective-permute-start | bytes 122888 | tf_op jit(solution)/shard_map/ppermute | solution.py:295
  19.2 4.4 %collective-permute-start.3 = (f32[80,128]{1,0:T(8,128)S(1)}, f32[80,128]{1,0:T(8,128)S(1)}, u32[]{:S(2)}, u32[]{:S(2)}) collective-permute-start(f32[80,128]{1,0:T(8,128)S(1)} %select_add_fusion), channel_id=1, source_target_pairs={{0,128},{8,136},{16,144},{24,152},{32,160},{40,168},{48,176},{56,1... | collective-permute-start | bytes 122888 | tf_op jit(solution)/shard_map/ppermute | solution.py:295
  23.7 3.0 %collective-permute-start.4 = (f32[80,128]{1,0:T(8,128)S(1)}, f32[80,128]{1,0:T(8,128)S(1)}, u32[]{:S(2)}, u32[]{:S(2)}) collective-permute-start(f32[80,128]{1,0:T(8,128)S(1)} %add.16), channel_id=1, source_target_pairs={{0,16},{8,24},{16,0},{24,8},{32,48},{40,56},{48,32},{56,40},{64,80... | collective-permute-start | bytes 122888 | tf_op jit(solution)/shard_map/ppermute | solution.py:295
  26.7 4.4 %collective-permute-start.5 = (f32[80,128]{1,0:T(8,128)S(1)}, f32[80,128]{1,0:T(8,128)S(1)}, u32[]{:S(2)}, u32[]{:S(2)}) collective-permute-start(f32[80,128]{1,0:T(8,128)S(1)} %add.17), channel_id=1, source_target_pairs={{0,32},{8,40},{16,48},{24,56},{32,0},{40,8},{48,16},{56,24},{64,96... | collective-permute-start | bytes 122888 | tf_op jit(solution)/shard_map/ppermute | solution.py:295
  31.1 6.6 %collective-permute-start.6 = (f32[80,128]{1,0:T(8,128)S(1)}, f32[80,128]{1,0:T(8,128)S(1)}, u32[]{:S(2)}, u32[]{:S(2)}) collective-permute-start(f32[80,128]{1,0:T(8,128)S(1)} %add.18), channel_id=1, source_target_pairs={{0,96},{8,104},{16,112},{24,120},{32,64},{40,72},{48,80},{56,88},{... | collective-permute-start | bytes 122888 | tf_op jit(solution)/shard_map/ppermute | solution.py:295
  38.2 5.5 %collective-permute-start.7 = (f32[16,128]{1,0:T(8,128)S(1)}, f32[16,128]{1,0:T(8,128)S(1)}, u32[]{:S(2)}, u32[]{:S(2)}) collective-permute-start(f32[16,128]{1,0:T(8,128)S(1)} %angles.1.mine_ref), channel_id=1, source_target_pairs={{0,8},{8,0},{16,24},{24,16},{32,40},{40,32},{48,56},{56,48},{64,72... | collective-permute-start | bytes 24584 | tf_op jit(solution)/shard_map/ppermute | solution.py:295

commit v5 on v4

--- a/solution.py
+++ b/solution.py
@@ -25,6 +25,11 @@
 
 def right(x, by):
     return pltpu.roll(x, by & (BLOCK - 1), 1)
+
+
+def at_end():
+    place = lax.axis_index("pairs")
+    return (place == 0) | (place == lax.axis_size("pairs") - 1)
 
 
 class Lags:
@@ -69,9 +74,9 @@
     return terms
 
 
-def pair_stats(ref, rows, lags):
+def pair_stats(pair_at, rows, lags):
     def terms(span):
-        upper, lower = halves(ref, span)
+        upper, lower = pair_at(span)
         upper_gap, lower_gap = left(upper, lags.gap), left(lower, lags.gap)
         step_0 = [upper * upper, lower * lower, upper * lower, upper * lower_gap, upper_gap * lower, upper * upper_gap, lower * lower_gap]
         return step_0 + lagged((upper, lower), (upper, lower), lags.turn, lags.gap)
@@ -168,16 +173,23 @@
 def stats_kernel(rows, offsets, first_ref, second_ref, first_out, second_out):
     lags = Lags(offsets, 0)
     for ref, out in ((first_ref, first_out), (second_ref, second_out)):
-        store_rows(out, 0, pair_stats(ref, rows, lags))
-
-
-def cross_kernel(rows, odd_slot, offsets, skip, own_ref, come_ref, stats_ref, out_ref):
+        store_rows(out, 0, pair_stats(functools.partial(halves, ref), rows, lags))
+
+
+def cross_kernel(rows, odd_slot, offsets, skip, own_ref, come_ref, end_ref, stats_ref, out_ref):
     is_even = (lax.axis_index("pairs") & 1) == 0
     slot = jnp.where(is_even, 1 - odd_slot, odd_slot)
     lags = Lags(offsets, slot)
     own_first = slot == 1
-    come_stats = pair_stats(come_ref, rows, lags)
-    own_flag, come_flag = [ref[rows : rows + 1, :BLOCK] for ref in (own_ref, come_ref)]
+    is_end = at_end()
+
+    def come(span):
+        pair = halves(come_ref, span)
+        return pair if odd_slot == 0 else [jnp.where(is_end, a, b) for a, b in zip(halves(end_ref, span), pair)]
+
+    come_stats = pair_stats(come, rows, lags)
+    flag_row = slice(rows, rows + 1)
+    own_flag, come_flag = halves(own_ref, flag_row)[0], come(flag_row)[0]
     step_flag = jnp.full((1, BLOCK), jnp.where(own_first, skip[1, 1], skip[1, 0]).astype(jnp.float32), jnp.float32)
     own_stats = [stats_ref[index : index + 1, :] for index in range(STATS)]
 
@@ -187,7 +199,7 @@
     for start, stats in zip((0, STATS), pick(own_stats, come_stats)):
         store_rows(out_ref, start, stats)
     for index, lag in enumerate(lags.crossed()):
-        sums = sums_over(rows, lambda span: lagged(*pick(halves(own_ref, span), halves(come_ref, span)), lag, lags.gap))
+        sums = sums_over(rows, lambda span: lagged(*pick(halves(own_ref, span), come(span)), lag, lags.gap))
         store_rows(out_ref, CROSS + 12 * index, sums)
     x_flag, y_flag = pick([own_flag], [come_flag])
     store_rows(out_ref, FLAGS, x_flag + y_flag + [step_flag] + [jnp.zeros((1, BLOCK), jnp.float32)] * (SUMS - FLAGS - 3))
@@ -236,6 +248,12 @@
     is_even = (lax.axis_index("pairs") & 1) == 0
     on_first_core = (lax.axis_index("rows") & 1) == 0
     mine, other = mine_ref[...], other_ref[...]
+    is_end = at_end()
+
+    def pair_at(ref, span):
+        pair = halves(ref, span)
+        return [jnp.where(is_end, a, b) for a, b in zip(halves(second_ref, span), pair)] if ref is second_come else pair
+
     sources = (((second_come, first_come), (first_ref, second_ref)), ((second_ref, first_ref), (first_come, second_come)))
     slots = [jnp.where(on_first_core, mine, other), jnp.where(on_first_core, other, mine)]
     for slot in range(2):
@@ -251,7 +269,7 @@
         for start in range(0, rows, BATCH):
             span = slice(start, start + BATCH)
             x, y = [
-                [jnp.where(is_even, a, b) for a, b in zip(halves(even_ref, span), halves(odd_ref, span))]
+                [jnp.where(is_even, a, b) for a, b in zip(pair_at(even_ref, span), pair_at(odd_ref, span))]
                 for even_ref, odd_ref in sources[slot]
             ]
             upper = block_after(x, turns[:4], lags.gap)
@@ -319,8 +337,8 @@
         ],
         grant=None,
     )
+    second_come = lax.ppermute(second, "pairs", [(at, (((at + 1) ^ 1) - 1) % pairs) for at in range(pairs)])
     first_come = lax.ppermute(first, "pairs", [(at, at ^ 1) for at in range(pairs)])
-    second_come = lax.ppermute(second, "pairs", [(at, min(max(((at + 1) ^ 1) - 1, 0), pairs - 1)) for at in range(pairs)])
     offsets, skips = (partner_offsets, VMEM), (skip_mask, VMEM)
     first_stats, second_stats = call(
         functools.partial(stats_kernel, rows), [offsets, (first, VMEM), (second, VMEM)], [((24, BLOCK), VMEM)] * 2, "stats"
@@ -329,7 +347,7 @@
     for odd_slot, own, come, stats in ((0, second, first_come, second_stats), (1, first, second_come, first_stats)):
         slots += call(
             functools.partial(cross_kernel, rows, odd_slot),
-            [offsets, skips, (own, VMEM), (come, VMEM), (stats, VMEM)],
+            [offsets, skips, (own, VMEM), (come, VMEM), (second, VMEM), (stats, VMEM)],
             [((SUMS, BLOCK), VMEM)],
             "cross",
         )
@@ -337,8 +355,8 @@
     sums = jnp.where(keeps_first, slots[1], slots[0])
     sums = sums + swap_rows(jnp.where(keeps_first, slots[0], slots[1]), lambda y, z, core: (y, z, 1 - core))
     sums = sums + swap_rows(sums, lambda y, z, core: (1 - y, z, core))
-    sums = sums + swap_rows(sums, lambda y, z, core: (y, z ^ 1, core))
-    sums = sums + swap_rows(sums, lambda y, z, core: (y, z ^ 2, core))
+    near = [swap_rows(sums, lambda y, z, core, by=by: (y, z ^ by, core)) for by in (1, 2, 3)]
+    sums = (sums + near[0]) + (near[1] + near[2])
     sums = sums + swap_rows(sums, lambda y, z, core: (y, OPPOSITE[z], core))
     total_rows = float(rows * lax.axis_size("rows"))
     (angles,) = call(functools.partial(angles_kernel, total_rows), [offsets, (sums, VMEM)], [((ANGLES, BLOCK), VMEM)], "angles")

time: 45.4 us -> 42.9 us (0.945)
  the two profiles are of different devices: /device:TPU:9 before, /device:TPU:1 now
where the time goes in v5:
time: 42.9 us; the launch traced here: 42.7 us
  starting transfers between devices  22.8 us (53%)
  waiting for transfers between devices  8.91 us (21%)
  Pallas kernels  7.04 us (16%)
  local copies, waits for them, and re-layouts  3.27 us (8%)
  between operations  0.7 us (2%)
    ppermute x7, starting transfers between devices, swap_rows(): return lax.ppermute(x, 'rows', [(row, other(row)) for row in range(size)])  17.8 us
    ppermute x7, waiting for transfers between devices, swap_rows(): return lax.ppermute(x, 'rows', [(row, other(row)) for row in range(size)])  7.92 us
    pallas_call x6, Pallas kernels, call(): pl.pallas_call(kernel, out_shape=[jax.ShapeDtypeStruct(shape, jnp.float32...  7.04 us
    unnamed x12, local copies, waits for them, and re-layouts  3.27 us
    ppermute x1, starting transfers between devices, per_device(): lax.ppermute(second, 'pairs', [(at, ((at + 1 ^ 1) - 1) % pairs) for at in...  2.83 us
    ppermute x1, starting transfers between devices, per_device(): lax.ppermute(first, 'pairs', [(at, at ^ 1) for at in range(pairs)])  2.13 us
    ppermute x1, waiting for transfers between devices, per_device(): lax.ppermute(second, 'pairs', [(at, ((at + 1 ^ 1) - 1) % pairs) for at in...  0.99 us
  transfers between devices with their start and end apart: 9, of which 7 were waited for; matrix products, arithmetic and copies ran while one was open for 0% of the time, Pallas kernels for 4%

profile of v5, /device:TPU:1, one launch (start us, length us, event | category | flops | bytes accessed | tf_op | source)
XLA Modules:
  0.0 42.7 jit_solution(2677218434643129842)
XLA Ops:
  0.6 2.1 %load.1 = (f32[264,256]{1,0:T(8,128)}, f32[264,256]{1,0:T(8,128)}) custom-call(s32[2,2]{1,0:T(2,128)} %offsets.9, s32[2,2]{1,0:T(2,128)} %skip.3, f32[256,512]{1,0:T(8,128)} %loads_hbm.1, f32[1,512]{1,0:T(1,128)} %bitcast.2), custom_call_target="tpu_custom_call" | custom-call | flops 1000000000 | bytes 1000000 | tf_op jit(solution)/shard_map/load/pallas_call | solution.py:293
  2.7 2.1 %collective-permute-start.1 = (f32[264,256]{1,0:T(8,128)}, f32[264,256]{1,0:T(8,128)S(1)}, u32[]{:S(2)}, u32[]{:S(2)}) collective-permute-start(f32[264,256]{1,0:T(8,128)} %get-tuple-element.8.first_ref.own_ref), channel_id=1, source_target_pairs={{0,1},{1,0},{2,3},{3,2},{4,5},{5,4},{6,7},{7,6},{8,9},{9,8},{10,11... | collective-permute-start | bytes 811016 | tf_op jit(solution)/shard_map/ppermute | solution.py:341
  4.8 2.8 %collective-permute-start = (f32[264,256]{1,0:T(8,128)}, f32[264,256]{1,0:T(8,128)S(1)}, u32[]{:S(2)}, u32[]{:S(2)}) collective-permute-start(f32[264,256]{1,0:T(8,128)} %get-tuple-element.9.second_ref.end_ref.own_ref), channel_id=1, source_target_pairs={{0,7},{1,2},{2,1},{3,4},{4,3},{5,6},{6,5},{7,0},{8,15},{9,10},{10,... | collective-permute-start | bytes 811016 | tf_op jit(solution)/shard_map/ppermute | solution.py:340
  7.7 0.0 copy-start.5
  7.7 0.7 %copy-done.5 = s32[2,2]{1,0:T(2,128)S(1)} copy-done((s32[2,2]{1,0:T(2,128)S(1)}, s32[2,2]{1,0:T(2,128)}, u32[]{:S(2)}) %copy-start.5) | copy-done | bytes 40
  8.3 0.0 copy-start
  8.3 1.0 %copy-done = f32[264,256]{1,0:T(8,128)S(1)} copy-done((f32[264,256]{1,0:T(8,128)S(1)}, f32[264,256]{1,0:T(8,128)}, u32[]{:S(2)}) %copy-start) | copy-done | bytes 270360
  9.3 0.0 copy-start.2
  9.3 1.0 %copy-done.2 = f32[264,256]{1,0:T(8,128)S(1)} copy-done((f32[264,256]{1,0:T(8,128)S(1)}, f32[264,256]{1,0:T(8,128)}, u32[]{:S(2)}) %copy-start.2) | copy-done | bytes 270360
  10.2 0.0 copy-start.3
  10.2 0.7 %stats.1 = (f32[24,128]{1,0:T(8,128)S(1)}, f32[24,128]{1,0:T(8,128)S(1)}) custom-call(s32[2,2]{1,0:T(2,128)S(1)} %copy-done.5, f32[264,256]{1,0:T(8,128)S(1)} %copy-done, f32[264,256]{1,0:T(8,128)S(1)} %copy-done.2), custom_call_target="tpu_custom_call" | custom-call | flops 1000000000 | bytes 1000000 | tf_op jit(solution)/shard_map/stats/pallas_call | solution.py:293
  11.0 0.0 copy-start.4
  11.0 0.0 collective-permute-done.1.come_ref.first_come
  11.0 0.2 copy-done.3
  11.2 0.5 %copy-done.4 = s32[2,2]{1,0:T(2,128)S(1)} copy-done((s32[2,2]{1,0:T(2,128)S(1)}, s32[2,2]{1,0:T(2,128)}, u32[]{:S(2)}) %copy-start.4) | copy-done | bytes 40
  11.7 0.0 copy-start.1
  11.7 1.1 %cross.3 = f32[80,128]{1,0:T(8,128)S(1)} custom-call(s32[2,2]{1,0:T(2,128)S(1)} %copy-done.5, s32[2,2]{1,0:T(2,128)S(1)} %copy-done.4, f32[264,256]{1,0:T(8,128)S(1)} %copy-done.3, f32[264,256]{1,0:T(8,128)S(1)} %collective-permute-done.1.come_ref.first_come, f32[264,256]{1,0:T(8,128)S(1)} %copy-done.3, f32[24,128]{1,0:T(8,128)S(1)} %get-tuple-element.11.stats_ref), custom_call_target="tpu_custom_call" | custom-call | flops 1000000000 | bytes 1000000 | tf_op jit(solution)/shard_map/cross/pallas_call | solution.py:293
  12.8 1.0 %collective-permute-done.come_ref.second_come = f32[264,256]{1,0:T(8,128)S(1)} collective-permute-done((f32[264,256]{1,0:T(8,128)}, f32[264,256]{1,0:T(8,128)S(1)}, u32[]{:S(2)}, u32[]{:S(2)}) %collective-permute-start) | collective-permute-done | bytes 270368 | tf_op jit(solution)/shard_map/ppermute | solution.py:340
  13.8 0.0 copy-done.1
  13.8 1.2 %cross.2 = f32[80,128]{1,0:T(8,128)S(1)} custom-call(s32[2,2]{1,0:T(2,128)S(1)} %copy-done.5, s32[2,2]{1,0:T(2,128)S(1)} %copy-done.4, f32[264,256]{1,0:T(8,128)S(1)} %copy-done.1, f32[264,256]{1,0:T(8,128)S(1)} %collective-permute-done.come_ref.second_come, f32[264,256]{1,0:T(8,128)S(1)} %copy-done.3, f32[24,128]{1,0:T(8,128)S(1)} %get-tuple-element.10.stats_ref), custom_call_target="tpu_custom_call" | custom-call | flops 1000000000 | bytes 1000000 | tf_op jit(solution)/shard_map/cross/pallas_call | solution.py:293
  15.0 2.3 %collective-permute-start.2 = (f32[80,128]{1,0:T(8,128)S(1)}, f32[80,128]{1,0:T(8,128)S(1)}, u32[]{:S(2)}, u32[]{:S(2)}) collective-permute-start(f32[80,128]{1,0:T(8,128)S(1)} %broadcast_select_fusion), channel_id=1, source_target_pairs={{0,8},{8,0},{16,24},{24,16},{32,40},{40,32},{48,56},{56,48},{64,72... | collective-permute-start | bytes 122888 | tf_op jit(solution)/shard_map/ppermute | solution.py:313
  17.4 0.9 %collective-permute-done.2 = f32[80,128]{1,0:T(8,128)S(1)} collective-permute-done((f32[80,128]{1,0:T(8,128)S(1)}, f32[80,128]{1,0:T(8,128)S(1)}, u32[]{:S(2)}, u32[]{:S(2)}) %collective-permute-start.2) | collective-permute-done | bytes 40992 | tf_op jit(solution)/shard_map/ppermute | solution.py:313
  18.2 3.0 %collective-permute-start.3 = (f32[80,128]{1,0:T(8,128)S(1)}, f32[80,128]{1,0:T(8,128)S(1)}, u32[]{:S(2)}, u32[]{:S(2)}) collective-permute-start(f32[80,128]{1,0:T(8,128)S(1)} %select_add_fusion), channel_id=1, source_target_pairs={{0,128},{8,136},{16,144},{24,152},{32,160},{40,168},{48,176},{56,1... | collective-permute-start | bytes 122888 | tf_op jit(solution)/shard_map/ppermute | solution.py:313
  21.2 1.4 %collective-permute-done.3 = f32[80,128]{1,0:T(8,128)S(1)} collective-permute-done((f32[80,128]{1,0:T(8,128)S(1)}, f32[80,128]{1,0:T(8,128)S(1)}, u32[]{:S(2)}, u32[]{:S(2)}) %collective-permute-start.3) | collective-permute-done | bytes 40992 | tf_op jit(solution)/shard_map/ppermute | solution.py:313
  22.7 4.3 %collective-permute-start.6 = (f32[80,128]{1,0:T(8,128)S(1)}, f32[80,128]{1,0:T(8,128)S(1)}, u32[]{:S(2)}, u32[]{:S(2)}) collective-permute-start(f32[80,128]{1,0:T(8,128)S(1)} %add.19), channel_id=1, source_target_pairs={{0,48},{8,56},{16,32},{24,40},{32,16},{40,24},{48,0},{56,8},{64,11... | collective-permute-start | bytes 122888 | tf_op jit(solution)/shard_map/ppermute | solution.py:313
  27.0 0.0 collective-permute-start.5
  27.0 0.4 collective-permute-start.4
  27.4 1.0 %collective-permute-done.6 = f32[80,128]{1,0:T(8,128)S(1)} collective-permute-done((f32[80,128]{1,0:T(8,128)S(1)}, f32[80,128]{1,0:T(8,128)S(1)}, u32[]{:S(2)}, u32[]{:S(2)}) %collective-permute-start.6) | collective-permute-done | bytes 40992 | tf_op jit(solution)/shard_map/ppermute | solution.py:313
  28.4 2.4 %collective-permute-done.5 = f32[80,128]{1,0:T(8,128)S(1)} collective-permute-done((f32[80,128]{1,0:T(8,128)S(1)}, f32[80,128]{1,0:T(8,128)S(1)}, u32[]{:S(2)}, u32[]{:S(2)}) %collective-permute-start.5) | collective-permute-done | bytes 40992 | tf_op jit(solution)/shard_map/ppermute | solution.py:313
  30.8 0.0 collective-permute-done.4
  30.8 4.1 %collective-permute-start.7 = (f32[80,128]{1,0:T(8,128)S(1)}, f32[80,128]{1,0:T(8,128)S(1)}, u32[]{:S(2)}, u32[]{:S(2)}) collective-permute-start(f32[80,128]{1,0:T(8,128)S(1)} %add_add_fusion), channel_id=1, source_target_pairs={{0,96},{8,104},{16,112},{24,120},{32,64},{40,72},{48,80},{56,88},{... | collective-permute-start | bytes 122888 | tf_op jit(solution)/shard_map/ppermute | solution.py:313
  34.9 1.4 %collective-permute-done.7 = f32[80,128]{1,0:T(8,128)S(1)} collective-permute-done((f32[80,128]{1,0:T(8,128)S(1)}, f32[80,128]{1,0:T(8,128)S(1)}, u32[]{:S(2)}, u32[]{:S(2)}) %collective-permute-start.7) | collective-permute-done | bytes 40992 | tf_op jit(solution)/shard_map/ppermute | solution.py:313
  36.3 0.5 %angles.1.mine_ref = f32[16,128]{1,0:T(8,128)S(1)} custom-call(s32[2,2]{1,0:T(2,128)S(1)} %copy-done.5, f32[80,128]{1,0:T(8,128)S(1)} %add.23.sums_ref), custom_call_target="tpu_custom_call" | custom-call | flops 1000000000 | bytes 1000000 | tf_op jit(solution)/shard_map/angles/pallas_call | solution.py:293
  36.8 3.7 %collective-permute-start.8 = (f32[16,128]{1,0:T(8,128)S(1)}, f32[16,128]{1,0:T(8,128)S(1)}, u32[]{:S(2)}, u32[]{:S(2)}) collective-permute-start(f32[16,128]{1,0:T(8,128)S(1)} %angles.1.mine_ref), channel_id=1, source_target_pairs={{0,8},{8,0},{16,24},{24,16},{32,40},{40,32},{48,56},{56,48},{64,72... | collective-permute-start | bytes 24584 | tf_op jit(solution)/shard_map/ppermute | solution.py:313
  40.5 0.8 %collective-permute-done.8.other_ref = f32[16,128]{1,0:T(8,128)S(1)} collective-permute-done((f32[16,128]{1,0:T(8,128)S(1)}, f32[16,128]{1,0:T(8,128)S(1)}, u32[]{:S(2)}, u32[]{:S(2)}) %collective-permute-start.8) | collective-permute-done | bytes 8224 | tf_op jit(solution)/shard_map/ppermute | solution.py:313
  41.3 1.4 %last.1 = (f32[256,512]{1,0:T(8,128)}, f32[1,512]{1,0:T(1,128)}) custom-call(s32[2,2]{1,0:T(2,128)S(1)} %copy-done.5, f32[16,128]{1,0:T(8,128)S(1)} %angles.1.mine_ref, f32[16,128]{1,0:T(8,128)S(1)} %collective-permute-done.8.other_ref, f32[264,256]{1,0:T(8,128)S(1)} %copy-done.1, f32[264,256]{1,0:T(8,128)S(1)} %copy-done.3, ...), custom_call_target="tpu_custom_call" | custom-call | flops 1000000000 | bytes 1000000 | tf_op jit(solution)/shard_map/last/pallas_call | solution.py:293
  (5 shorter events, 0.0 us)
Async XLA Ops:
  2.7 8.3 %collective-permute-start.1 = (f32[264,256]{1,0:T(8,128)}, f32[264,256]{1,0:T(8,128)S(1)}, u32[]{:S(2)}, u32[]{:S(2)}) collective-permute-start(f32[264,256]{1,0:T(8,128)} %get-tuple-element.8.first_ref.own_ref), channel_id=1, source_target_pairs={{0,1},{1,0},{2,3},{3,2},{4,5},{5,4},{6,7},{7,6},{8,9},{9,8},{10,11... | collective-permute-start | bytes 811016 | tf_op jit(solution)/shard_map/ppermute | solution.py:341
  4.8 9.0 %collective-permute-start = (f32[264,256]{1,0:T(8,128)}, f32[264,256]{1,0:T(8,128)S(1)}, u32[]{:S(2)}, u32[]{:S(2)}) collective-permute-start(f32[264,256]{1,0:T(8,128)} %get-tuple-element.9.second_ref.end_ref.own_ref), channel_id=1, source_target_pairs={{0,7},{1,2},{2,1},{3,4},{4,3},{5,6},{6,5},{7,0},{8,15},{9,10},{10,... | collective-permute-start | bytes 811016 | tf_op jit(solution)/shard_map/ppermute | solution.py:340
  7.7 0.7 %copy-start.5 = (s32[2,2]{1,0:T(2,128)S(1)}, s32[2,2]{1,0:T(2,128)}, u32[]{:S(2)}) copy-start(s32[2,2]{1,0:T(2,128)} %offsets.9) | copy-start | bytes 52
  8.3 1.0 %copy-start = (f32[264,256]{1,0:T(8,128)S(1)}, f32[264,256]{1,0:T(8,128)}, u32[]{:S(2)}) copy-start(f32[264,256]{1,0:T(8,128)} %get-tuple-element.8.first_ref.own_ref) | copy-start | bytes 811012
  9.3 1.0 %copy-start.2 = (f32[264,256]{1,0:T(8,128)S(1)}, f32[264,256]{1,0:T(8,128)}, u32[]{:S(2)}) copy-start(f32[264,256]{1,0:T(8,128)} %get-tuple-element.9.second_ref.end_ref.own_ref) | copy-start | bytes 811012
  10.2 1.0 %copy-start.3 = (f32[264,256]{1,0:T(8,128)S(1)}, f32[264,256]{1,0:T(8,128)}, u32[]{:S(2)}) copy-start(f32[264,256]{1,0:T(8,128)} %get-tuple-element.9.second_ref.end_ref.own_ref) | copy-start | bytes 811012
  11.0 0.7 %copy-start.4 = (s32[2,2]{1,0:T(2,128)S(1)}, s32[2,2]{1,0:T(2,128)}, u32[]{:S(2)}) copy-start(s32[2,2]{1,0:T(2,128)} %skip.3) | copy-start | bytes 52
  11.7 2.1 %copy-start.1 = (f32[264,256]{1,0:T(8,128)S(1)}, f32[264,256]{1,0:T(8,128)}, u32[]{:S(2)}) copy-start(f32[264,256]{1,0:T(8,128)} %get-tuple-element.8.first_ref.own_ref) | copy-start | bytes 811012
  15.0 3.2 %collective-permute-start.2 = (f32[80,128]{1,0:T(8,128)S(1)}, f32[80,128]{1,0:T(8,128)S(1)}, u32[]{:S(2)}, u32[]{:S(2)}) collective-permute-start(f32[80,128]{1,0:T(8,128)S(1)} %broadcast_select_fusion), channel_id=1, source_target_pairs={{0,8},{8,0},{16,24},{24,16},{32,40},{40,32},{48,56},{56,48},{64,72... | collective-permute-start | bytes 122888 | tf_op jit(solution)/shard_map/ppermute | solution.py:313
  18.2 4.4 %collective-permute-start.3 = (f32[80,128]{1,0:T(8,128)S(1)}, f32[80,128]{1,0:T(8,128)S(1)}, u32[]{:S(2)}, u32[]{:S(2)}) collective-permute-start(f32[80,128]{1,0:T(8,128)S(1)} %select_add_fusion), channel_id=1, source_target_pairs={{0,128},{8,136},{16,144},{24,152},{32,160},{40,168},{48,176},{56,1... | collective-permute-start | bytes 122888 | tf_op jit(solution)/shard_map/ppermute | solution.py:313
  22.7 5.7 %collective-permute-start.6 = (f32[80,128]{1,0:T(8,128)S(1)}, f32[80,128]{1,0:T(8,128)S(1)}, u32[]{:S(2)}, u32[]{:S(2)}) collective-permute-start(f32[80,128]{1,0:T(8,128)S(1)} %add.19), channel_id=1, source_target_pairs={{0,48},{8,56},{16,32},{24,40},{32,16},{40,24},{48,0},{56,8},{64,11... | collective-permute-start | bytes 122888 | tf_op jit(solution)/shard_map/ppermute | solution.py:313
  27.0 3.8 %collective-permute-start.5 = (f32[80,128]{1,0:T(8,128)S(1)}, f32[80,128]{1,0:T(8,128)S(1)}, u32[]{:S(2)}, u32[]{:S(2)}) collective-permute-start(f32[80,128]{1,0:T(8,128)S(1)} %add.19), channel_id=1, source_target_pairs={{0,32},{8,40},{16,48},{24,56},{32,0},{40,8},{48,16},{56,24},{64,96... | collective-permute-start | bytes 122888 | tf_op jit(solution)/shard_map/ppermute | solution.py:313
  27.0 3.8 %collective-permute-start.4 = (f32[80,128]{1,0:T(8,128)S(1)}, f32[80,128]{1,0:T(8,128)S(1)}, u32[]{:S(2)}, u32[]{:S(2)}) collective-permute-start(f32[80,128]{1,0:T(8,128)S(1)} %add.19), channel_id=1, source_target_pairs={{0,16},{8,24},{16,0},{24,8},{32,48},{40,56},{48,32},{56,40},{64,80... | collective-permute-start | bytes 122888 | tf_op jit(solution)/shard_map/ppermute | solution.py:313
  30.8 5.5 %collective-permute-start.7 = (f32[80,128]{1,0:T(8,128)S(1)}, f32[80,128]{1,0:T(8,128)S(1)}, u32[]{:S(2)}, u32[]{:S(2)}) collective-permute-start(f32[80,128]{1,0:T(8,128)S(1)} %add_add_fusion), channel_id=1, source_target_pairs={{0,96},{8,104},{16,112},{24,120},{32,64},{40,72},{48,80},{56,88},{... | collective-permute-start | bytes 122888 | tf_op jit(solution)/shard_map/ppermute | solution.py:313
  36.8 4.5 %collective-permute-start.8 = (f32[16,128]{1,0:T(8,128)S(1)}, f32[16,128]{1,0:T(8,128)S(1)}, u32[]{:S(2)}, u32[]{:S(2)}) collective-permute-start(f32[16,128]{1,0:T(8,128)S(1)} %angles.1.mine_ref), channel_id=1, source_target_pairs={{0,8},{8,0},{16,24},{24,16},{32,40},{40,32},{48,56},{56,48},{64,72... | collective-permute-start | bytes 24584 | tf_op jit(solution)/shard_map/ppermute | solution.py:313

commit v6 on v4

--- a/solution.py
+++ b/solution.py
@@ -14,6 +14,7 @@
 CROSS = 2 * STATS
 FLAGS = CROSS + 36
 SUMS = 80
+SIDE = 24
 NORMS = 12
 ANGLES = 16
 VMEM_LIMIT = 8 * 1024 * 1024
@@ -25,6 +26,16 @@
 
 def right(x, by):
     return pltpu.roll(x, by & (BLOCK - 1), 1)
+
+
+def at_end():
+    place = lax.axis_index("pairs")
+    return (place == 0) | (place == lax.axis_size("pairs") - 1)
+
+
+def kept_slot():
+    row = lax.axis_index("rows")
+    return (row ^ (row >> 1) ^ (row >> 2) ^ (row >> 4)) & 1
 
 
 class Lags:
@@ -69,14 +80,14 @@
     return terms
 
 
-def pair_stats(ref, rows, lags):
+def pair_stats(ref, lags):
     def terms(span):
         upper, lower = halves(ref, span)
         upper_gap, lower_gap = left(upper, lags.gap), left(lower, lags.gap)
         step_0 = [upper * upper, lower * lower, upper * lower, upper * lower_gap, upper_gap * lower, upper * upper_gap, lower * lower_gap]
         return step_0 + lagged((upper, lower), (upper, lower), lags.turn, lags.gap)
 
-    return sums_over(rows, terms)
+    return sums_over(ref.shape[0], terms)
 
 
 def angle(first_norms, second_norms, coupling):
@@ -131,70 +142,64 @@
     return [[left(value, by) for value in pair] for pair in weights]
 
 
-def load_kernel(offsets_hbm, skip_hbm, loads_hbm, weights_hbm, first_hbm, second_hbm,
-                offsets, skip, loads, weights, held, in_sems, out_sems):
-    rows = loads.shape[0]
-    parts = range(0, rows, BATCH)
-    small = [(offsets_hbm, offsets), (skip_hbm, skip), (weights_hbm, weights)]
-    large = [(loads_hbm.at[pl.ds(start, BATCH)], loads.at[pl.ds(start, BATCH)]) for start in parts]
-    copies = [pltpu.make_async_copy(*ends, in_sems.at[at]) for at, ends in enumerate(small + large)]
-    for copy in copies:
-        copy.start()
-    for copy in copies[:3]:
-        copy.wait()
+def align_into(out_ref, raw, weights, lags):
+    for start in range(0, out_ref.shape[0], BATCH):
+        span = slice(start, start + BATCH)
+        upper, lower = raw(span)
+        out_ref[span, :BLOCK] = upper * weights[0]
+        out_ref[span, BLOCK:] = left(lower, lags.first) * weights[1]
+
+
+def own_kernel(offsets, skip, weights_ref, first_raw, second_raw, first_ref, second_ref, first_side, second_side):
+    lags = Lags(offsets, 0)
     is_even = (lax.axis_index("pairs") & 1) == 0
+    weights = [weights_ref[:, block * BLOCK : (block + 1) * BLOCK] for block in range(4)]
     skips = [skip[0, pair].astype(jnp.float32) for pair in range(2)]
-    for at, order in enumerate((skips[::-1], skips)):
-        held[at, rows:, :] = jnp.full((GROUP, 2 * BLOCK), jnp.where(is_even, *order), jnp.float32)
-    weight = [weights[:, block * BLOCK : (block + 1) * BLOCK] for block in range(4)]
-    sent = []
-    for part, start in enumerate(parts):
-        copies[3 + part].wait()
-        span = slice(start, start + BATCH)
-        blocks = [loads[span, block * BLOCK : (block + 1) * BLOCK] * weight[block] for block in range(4)]
-        blocks = blocks[:2] + [left(block, offsets[0, 0]) for block in blocks[2:]]
-        last = start + BATCH == rows
-        for at, out in enumerate((first_hbm, second_hbm)):
-            for half in range(2):
-                even, odd = blocks[2 * half + 1 - at], blocks[2 * half + at]
-                held[at, span, half * BLOCK : (half + 1) * BLOCK] = jnp.where(is_even, even, odd)
-            place = pl.ds(start, BATCH + GROUP if last else BATCH)
-            sent.append(pltpu.make_async_copy(held.at[at, place], out.at[place], out_sems.at[at, part]))
-            sent[-1].start()
-    for copy in sent:
-        copy.wait()
-
-
-def stats_kernel(rows, offsets, first_ref, second_ref, first_out, second_out):
-    lags = Lags(offsets, 0)
-    for ref, out in ((first_ref, first_out), (second_ref, second_out)):
-        store_rows(out, 0, pair_stats(ref, rows, lags))
-
-
-def cross_kernel(rows, odd_slot, offsets, skip, own_ref, come_ref, stats_ref, out_ref):
+    for even, raw_ref, ref, side in ((1, first_raw, first_ref, first_side), (0, second_raw, second_ref, second_side)):
+        odd = 1 - even
+        weight = [jnp.where(is_even, weights[2 * half + even], weights[2 * half + odd]) for half in range(2)]
+        weight[1] = left(weight[1], lags.first)
+        align_into(ref, functools.partial(halves, raw_ref), weight, lags)
+        flag = jnp.full((1, BLOCK), jnp.where(is_even, skips[even], skips[odd]), jnp.float32)
+        rows = pair_stats(ref, lags) + weight + [flag]
+        store_rows(side, 0, rows + [jnp.zeros_like(flag)] * (SIDE - len(rows)))
+
+
+def cross_kernel(odd_slot, offsets, skip, own_ref, own_side, raw_ref, come_side, end_ref, end_side, out_ref, come_ref):
     is_even = (lax.axis_index("pairs") & 1) == 0
     slot = jnp.where(is_even, 1 - odd_slot, odd_slot)
     lags = Lags(offsets, slot)
     own_first = slot == 1
-    come_stats = pair_stats(come_ref, rows, lags)
-    own_flag, come_flag = [ref[rows : rows + 1, :BLOCK] for ref in (own_ref, come_ref)]
+    rows = range(STATS + 3)
+    own = [own_side[row : row + 1, :] for row in rows]
+    come = [come_side[row : row + 1, :] for row in rows]
+    align_into(come_ref, functools.partial(halves, raw_ref), come[STATS : STATS + 2], lags)
+    if odd_slot == 1:
+
+        @pl.when(at_end())
+        def _():
+            come_ref[...] = end_ref[...]
+
+        come = [jnp.where(at_end(), end_side[row : row + 1, :], value) for row, value in zip(rows, come)]
     step_flag = jnp.full((1, BLOCK), jnp.where(own_first, skip[1, 1], skip[1, 0]).astype(jnp.float32), jnp.float32)
-    own_stats = [stats_ref[index : index + 1, :] for index in range(STATS)]
 
     def pick(mine, theirs):
         return [jnp.where(own_first, a, b) for a, b in zip(mine, theirs)], [jnp.where(own_first, b, a) for a, b in zip(mine, theirs)]
 
-    for start, stats in zip((0, STATS), pick(own_stats, come_stats)):
-        store_rows(out_ref, start, stats)
+    x_side, y_side = pick(own, come)
+    store_rows(out_ref, 0, x_side[:STATS] + y_side[:STATS])
     for index, lag in enumerate(lags.crossed()):
-        sums = sums_over(rows, lambda span: lagged(*pick(halves(own_ref, span), halves(come_ref, span)), lag, lags.gap))
-        store_rows(out_ref, CROSS + 12 * index, sums)
-    x_flag, y_flag = pick([own_flag], [come_flag])
-    store_rows(out_ref, FLAGS, x_flag + y_flag + [step_flag] + [jnp.zeros((1, BLOCK), jnp.float32)] * (SUMS - FLAGS - 3))
+
+        def terms(span):
+            x, y = pick(halves(own_ref, span), halves(come_ref, span))
+            return lagged(x, y, lag, lags.gap)
+
+        store_rows(out_ref, CROSS + 12 * index, sums_over(own_ref.shape[0], terms))
+    store_rows(out_ref, FLAGS, x_side[-1:] + y_side[-1:] + [step_flag] + [jnp.zeros_like(step_flag)] * (SUMS - FLAGS - 3))
 
 
 def angles_kernel(total_rows, offsets, sums_ref, out_ref):
-    lags = Lags(offsets, lax.axis_index("rows") & 1)
+    lags = Lags(offsets, kept_slot())
     rows = [sums_ref[index : index + 1, :] for index in range(FLAGS + 3)]
     sides = []
     for side, is_low in ((0, lags.x_low), (1, jnp.logical_not(lags.y_up))):
@@ -234,10 +239,10 @@
                 rotated_hbm, power_hbm, rotated, power, sems):
     rows = rotated.shape[0]
     is_even = (lax.axis_index("pairs") & 1) == 0
-    on_first_core = (lax.axis_index("rows") & 1) == 0
+    keeps_first = kept_slot() == 0
     mine, other = mine_ref[...], other_ref[...]
     sources = (((second_come, first_come), (first_ref, second_ref)), ((second_ref, first_ref), (first_come, second_come)))
-    slots = [jnp.where(on_first_core, mine, other), jnp.where(on_first_core, other, mine)]
+    slots = [jnp.where(keeps_first, mine, other), jnp.where(keeps_first, other, mine)]
     for slot in range(2):
         for half in range(2):
             at = 2 * half + slot
@@ -301,51 +306,53 @@
 def per_device(loads, col_weights, partner_offsets, skip_mask):
     rows, columns = loads.shape
     pairs = lax.axis_size("pairs")
-    weights = col_weights.reshape(1, columns)
-    held = (rows + GROUP, 2 * BLOCK)
-    first, second = call(
-        load_kernel,
-        [(partner_offsets, HBM), (skip_mask, HBM), (loads, HBM), (weights, HBM)],
-        [(held, HBM)] * 2,
-        "load",
-        [
-            pltpu.VMEM(partner_offsets.shape, jnp.int32),
-            pltpu.VMEM(skip_mask.shape, jnp.int32),
-            pltpu.VMEM((rows, columns), jnp.float32),
-            pltpu.VMEM((1, columns), jnp.float32),
-            pltpu.VMEM((2,) + held, jnp.float32),
-            pltpu.SemaphoreType.DMA((3 + rows // BATCH,)),
-            pltpu.SemaphoreType.DMA((2, rows // BATCH)),
-        ],
-        grant=None,
-    )
-    first_come = lax.ppermute(first, "pairs", [(at, at ^ 1) for at in range(pairs)])
-    second_come = lax.ppermute(second, "pairs", [(at, min(max(((at + 1) ^ 1) - 1, 0), pairs - 1)) for at in range(pairs)])
+    weights = (col_weights.reshape(1, columns), VMEM)
     offsets, skips = (partner_offsets, VMEM), (skip_mask, VMEM)
-    first_stats, second_stats = call(
-        functools.partial(stats_kernel, rows), [offsets, (first, VMEM), (second, VMEM)], [((24, BLOCK), VMEM)] * 2, "stats"
-    )
-    slots = []
-    for odd_slot, own, come, stats in ((0, second, first_come, second_stats), (1, first, second_come, first_stats)):
-        slots += call(
-            functools.partial(cross_kernel, rows, odd_slot),
-            [offsets, skips, (own, VMEM), (come, VMEM), (stats, VMEM)],
-            [((SUMS, BLOCK), VMEM)],
+    is_even = (lax.axis_index("pairs") & 1) == 0
+    blocks = [loads[:, at * BLOCK : (at + 1) * BLOCK] for at in range(4)]
+    raw = [
+        jnp.concatenate([jnp.where(is_even, blocks[even + at], blocks[1 - even + at]) for at in (0, 2)], axis=1) for even in (1, 0)
+    ]
+
+    def swap_first(x):
+        return lax.ppermute(x, "pairs", [(at, at ^ 1) for at in range(pairs)])
+
+    def swap_second(x):
+        return lax.ppermute(x, "pairs", [(at, (((at + 1) ^ 1) - 1) % pairs) for at in range(pairs)])
+
+    pair, side = ((rows, 2 * BLOCK), VMEM), ((SIDE, BLOCK), VMEM)
+    second_raw = swap_second(raw[1])
+    first_raw = swap_first(raw[0])
+    first, second, first_side, second_side = [
+        (array, VMEM)
+        for array in call(own_kernel, [offsets, skips, weights] + [(array, VMEM) for array in raw], [pair, pair, side, side], "own")
+    ]
+    slots, come = [], []
+    for odd_slot, own, own_side, raw_come, side_come in (
+        (0, second, second_side, first_raw, swap_first(first_side[0])),
+        (1, first, first_side, second_raw, swap_second(second_side[0])),
+    ):
+        sums, aligned = call(
+            functools.partial(cross_kernel, odd_slot),
+            [offsets, skips, own, own_side, (raw_come, VMEM), (side_come, VMEM), second, second_side],
+            [((SUMS, BLOCK), VMEM), pair],
             "cross",
         )
-    keeps_first = (lax.axis_index("pairs") & 1) == (lax.axis_index("rows") & 1)
+        slots.append(sums)
+        come.append((aligned, VMEM))
+    keeps_first = (lax.axis_index("pairs") & 1) == kept_slot()
     sums = jnp.where(keeps_first, slots[1], slots[0])
     sums = sums + swap_rows(jnp.where(keeps_first, slots[0], slots[1]), lambda y, z, core: (y, z, 1 - core))
-    sums = sums + swap_rows(sums, lambda y, z, core: (1 - y, z, core))
-    sums = sums + swap_rows(sums, lambda y, z, core: (y, z ^ 1, core))
-    sums = sums + swap_rows(sums, lambda y, z, core: (y, z ^ 2, core))
-    sums = sums + swap_rows(sums, lambda y, z, core: (y, OPPOSITE[z], core))
+    sums = sums + swap_rows(sums, lambda y, z, core: (1 - y, z, 1 - core))
+    near = [swap_rows(sums, lambda y, z, core, by=by: (y, z ^ by, core if by == 3 else 1 - core)) for by in (3, 2, 1)]
+    sums = (sums + near[0]) + (near[1] + near[2])
+    sums = sums + swap_rows(sums, lambda y, z, core: (y, OPPOSITE[z], 1 - core))
     total_rows = float(rows * lax.axis_size("rows"))
     (angles,) = call(functools.partial(angles_kernel, total_rows), [offsets, (sums, VMEM)], [((ANGLES, BLOCK), VMEM)], "angles")
     other = swap_rows(angles, lambda y, z, core: (y, z, 1 - core))
     rotated, power = call(
         last_kernel,
-        [offsets] + [(array, VMEM) for array in (angles, other, first, second, first_come, second_come)],
+        [offsets, (angles, VMEM), (other, VMEM), first, second] + come,
         [((rows, columns), HBM), ((1, columns), HBM)],
         "last",
         [pltpu.VMEM((rows, columns), jnp.float32), pltpu.VMEM((1, columns), jnp.float32), pltpu.SemaphoreType.DMA((5,))],

time: 45.4 us -> 40.6 us (0.89)
  the two profiles are of different devices: /device:TPU:9 before, /device:TPU:1 now
where the time goes in v6:
time: 40.6 us; the launch traced here: 40.5 us
  starting transfers between devices  20.9 us (51%)
  waiting for transfers between devices  13.2 us (33%)
  Pallas kernels  4.48 us (11%)
  other arithmetic  1.22 us (3%)
  between operations  0.72 us (2%)
    ppermute x7, starting transfers between devices, swap_rows(): return lax.ppermute(x, 'rows', [(row, other(row)) for row in range(size)])  14.3 us
    ppermute x7, waiting for transfers between devices, swap_rows(): return lax.ppermute(x, 'rows', [(row, other(row)) for row in range(size)])  10.4 us
    pallas_call x5, Pallas kernels, call(): pl.pallas_call(kernel, out_shape=[jax.ShapeDtypeStruct(shape, jnp.float32...  4.48 us
    ppermute x2, starting transfers between devices, swap_second(): lax.ppermute(x, 'pairs', [(at, ((at + 1 ^ 1) - 1) % pairs) for at in rang...  4.4 us
    ppermute x2, starting transfers between devices, swap_first(): return lax.ppermute(x, 'pairs', [(at, at ^ 1) for at in range(pairs)])  2.22 us
    ppermute x2, waiting for transfers between devices, swap_first(): return lax.ppermute(x, 'pairs', [(at, at ^ 1) for at in range(pairs)])  1.54 us
    ppermute x2, waiting for transfers between devices, swap_second(): lax.ppermute(x, 'pairs', [(at, ((at + 1 ^ 1) - 1) % pairs) for at in rang...  1.28 us
    select_n x1, other arithmetic, per_device(): jnp.where(is_even, blocks[even + at], blocks[1 - even + at])  1.14 us
  transfers between devices with their start and end apart: 11, of which 8 were waited for; matrix products, arithmetic and copies ran while one was open for 0% of the time, Pallas kernels for 4%

profile of v6, /device:TPU:1, one launch (start us, length us, event | category | flops | bytes accessed | tf_op | source)
XLA Modules:
  0.0 40.5 jit_solution(11752625620031217812)
XLA Ops:
  0.6 1.1 %slice_select_fusion.2 = (f32[256,128]{1,0:T(8,128)S(1)}, f32[256,128]{1,0:T(8,128)S(1)}, f32[256,128]{1,0:T(8,128)S(1)}, f32[256,128]{1,0:T(8,128)S(1)}) fusion(f32[256,512]{1,0:T(8,128)} %param.4, pred[]{:T(512)S(6)} %eq.7), kind=kLoop, calls=%fused_computation.4 | loop fusion | flops 131072 | bytes 1048577 | tf_op jit(solution)/shard_map/jit(_where)/select_n | solution.py:314
  1.8 2.1 %collective-permute-start.2 = (f32[256,256]{1,0:T(8,128)S(1)}, f32[256,256]{1,0:T(8,128)S(1)}, u32[]{:S(2)}, u32[]{:S(2)}) collective-permute-start(f32[256,256]{1,0:T(8,128)S(1)} %pad_maximum_fusion.first_raw), channel_id=1, source_target_pairs={{0,1},{1,0},{2,3},{3,2},{4,5},{5,4},{6,7},{7,6},{8,9},{9,8},{10,11... | collective-permute-start | bytes 786440 | tf_op jit(solution)/shard_map/ppermute | solution.py:318
  3.9 0.0 copy-start
  3.9 0.0 copy-start.2
  4.0 0.0 copy-start.1
  4.0 2.9 %collective-permute-start = (f32[256,256]{1,0:T(8,128)S(1)}, f32[256,256]{1,0:T(8,128)S(1)}, u32[]{:S(2)}, u32[]{:S(2)}) collective-permute-start(f32[256,256]{1,0:T(8,128)S(1)} %pad_maximum_fusion.1.second_raw), channel_id=1, source_target_pairs={{0,7},{1,2},{2,1},{3,4},{4,3},{5,6},{6,5},{7,0},{8,15},{9,10},{10,... | collective-permute-start | bytes 786440 | tf_op jit(solution)/shard_map/ppermute | solution.py:321
  6.9 0.0 copy-done
  6.9 0.0 copy-done.2
  6.9 0.0 copy-done.1
  6.9 0.8 %own.1 = (f32[256,256]{1,0:T(8,128)S(1)}, f32[256,256]{1,0:T(8,128)S(1)}, f32[24,128]{1,0:T(8,128)S(1)}, f32[24,128]{1,0:T(8,128)S(1)}) custom-call(s32[2,2]{1,0:T(2,128)S(1)} %copy-done.2, s32[2,2]{1,0:T(2,128)S(1)} %copy-done.1, f32[1,512]{1,0:T(1,128)S(1)} %bitcast.2, f32[256,256]{1,0:T(8,128)S(1)} %pad_maximum_fusion.first_raw, ...), custom_call_target="tpu_custom_call" | custom-call | flops 1000000000 | bytes 1000000 | tf_op jit(solution)/shard_map/own/pallas_call | solution.py:280
  7.7 0.1 collective-permute-start.3
  7.8 1.5 %collective-permute-start.1 = (f32[24,128]{1,0:T(8,128)S(1)}, f32[24,128]{1,0:T(8,128)S(1)}, u32[]{:S(2)}, u32[]{:S(2)}) collective-permute-start(f32[24,128]{1,0:T(8,128)S(1)} %get-tuple-element.14.end_side.own_side), channel_id=1, source_target_pairs={{0,7},{1,2},{2,1},{3,4},{4,3},{5,6},{6,5},{7,0},{8,15},{9,10},{10,... | collective-permute-start | bytes 36872 | tf_op jit(solution)/shard_map/ppermute | solution.py:321
  9.3 1.5 %collective-permute-done.3.come_side = f32[24,128]{1,0:T(8,128)S(1)} collective-permute-done((f32[24,128]{1,0:T(8,128)S(1)}, f32[24,128]{1,0:T(8,128)S(1)}, u32[]{:S(2)}, u32[]{:S(2)}) %collective-permute-start.3) | collective-permute-done | bytes 12320 | tf_op jit(solution)/shard_map/ppermute | solution.py:318
  10.8 0.0 collective-permute-done.2.raw_ref
  10.8 0.9 %cross.3 = (f32[80,128]{1,0:T(8,128)S(1)}, f32[256,256]{1,0:T(8,128)S(1)}) custom-call(s32[2,2]{1,0:T(2,128)S(1)} %copy-done.2, s32[2,2]{1,0:T(2,128)S(1)} %copy-done.1, f32[256,256]{1,0:T(8,128)S(1)} %get-tuple-element.15.end_ref.own_ref.second_ref, f32[24,128]{1,0:T(8,128)S(1)} %get-tuple-element.14.end_side.own_side, ...), custom_call_target="tpu_custom_call" | custom-call | flops 1000000000 | bytes 1000000 | tf_op jit(solution)/shard_map/cross/pallas_call | solution.py:280
  11.7 1.3 %collective-permute-done.1.come_side = f32[24,128]{1,0:T(8,128)S(1)} collective-permute-done((f32[24,128]{1,0:T(8,128)S(1)}, f32[24,128]{1,0:T(8,128)S(1)}, u32[]{:S(2)}, u32[]{:S(2)}) %collective-permute-start.1) | collective-permute-done | bytes 12320 | tf_op jit(solution)/shard_map/ppermute | solution.py:321
  13.0 0.0 collective-permute-done.raw_ref
  13.0 0.9 %cross.2 = (f32[80,128]{1,0:T(8,128)S(1)}, f32[256,256]{1,0:T(8,128)S(1)}) custom-call(s32[2,2]{1,0:T(2,128)S(1)} %copy-done.2, s32[2,2]{1,0:T(2,128)S(1)} %copy-done.1, f32[256,256]{1,0:T(8,128)S(1)} %get-tuple-element.12.own_ref.first_ref, f32[24,128]{1,0:T(8,128)S(1)} %get-tuple-element.13.own_side, f32[256,256]{1,0:T(8,128)S(1)} %collective-permute-done.raw_ref, ...), custom_call_target="tpu_custom_call" | custom-call | flops 1000000000 | bytes 1000000 | tf_op jit(solution)/shard_map/cross/pallas_call | solution.py:280
  13.9 2.2 %collective-permute-start.4 = (f32[80,128]{1,0:T(8,128)S(1)}, f32[80,128]{1,0:T(8,128)S(1)}, u32[]{:S(2)}, u32[]{:S(2)}) collective-permute-start(f32[80,128]{1,0:T(8,128)S(1)} %broadcast_select_fusion), channel_id=1, source_target_pairs={{0,8},{8,0},{16,24},{24,16},{32,40},{40,32},{48,56},{56,48},{64,72... | collective-permute-start | bytes 122888 | tf_op jit(solution)/shard_map/ppermute | solution.py:300
  16.2 0.9 %collective-permute-done.4 = f32[80,128]{1,0:T(8,128)S(1)} collective-permute-done((f32[80,128]{1,0:T(8,128)S(1)}, f32[80,128]{1,0:T(8,128)S(1)}, u32[]{:S(2)}, u32[]{:S(2)}) %collective-permute-start.4) | collective-permute-done | bytes 40992 | tf_op jit(solution)/shard_map/ppermute | solution.py:300
  17.1 3.2 %collective-permute-start.5 = (f32[80,128]{1,0:T(8,128)S(1)}, f32[80,128]{1,0:T(8,128)S(1)}, u32[]{:S(2)}, u32[]{:S(2)}) collective-permute-start(f32[80,128]{1,0:T(8,128)S(1)} %select_add_fusion), channel_id=1, source_target_pairs={{0,136},{8,128},{16,152},{24,144},{32,168},{40,160},{48,184},{56,1... | collective-permute-start | bytes 122888 | tf_op jit(solution)/shard_map/ppermute | solution.py:300
  20.3 1.9 %collective-permute-done.5 = f32[80,128]{1,0:T(8,128)S(1)} collective-permute-done((f32[80,128]{1,0:T(8,128)S(1)}, f32[80,128]{1,0:T(8,128)S(1)}, u32[]{:S(2)}, u32[]{:S(2)}) %collective-permute-start.5) | collective-permute-done | bytes 40992 | tf_op jit(solution)/shard_map/ppermute | solution.py:300
  22.2 4.3 %collective-permute-start.6 = (f32[80,128]{1,0:T(8,128)S(1)}, f32[80,128]{1,0:T(8,128)S(1)}, u32[]{:S(2)}, u32[]{:S(2)}) collective-permute-start(f32[80,128]{1,0:T(8,128)S(1)} %add.19), channel_id=1, source_target_pairs={{0,48},{8,56},{16,32},{24,40},{32,16},{40,24},{48,0},{56,8},{64,11... | collective-permute-start | bytes 122888 | tf_op jit(solution)/shard_map/ppermute | solution.py:300
  26.5 0.0 collective-permute-start.7
  26.5 0.7 %collective-permute-start.8 = (f32[80,128]{1,0:T(8,128)S(1)}, f32[80,128]{1,0:T(8,128)S(1)}, u32[]{:S(2)}, u32[]{:S(2)}) collective-permute-start(f32[80,128]{1,0:T(8,128)S(1)} %add.19), channel_id=1, source_target_pairs={{0,24},{8,16},{16,8},{24,0},{32,56},{40,48},{48,40},{56,32},{64,88... | collective-permute-start | bytes 122888 | tf_op jit(solution)/shard_map/ppermute | solution.py:300
  27.2 0.7 %collective-permute-done.6 = f32[80,128]{1,0:T(8,128)S(1)} collective-permute-done((f32[80,128]{1,0:T(8,128)S(1)}, f32[80,128]{1,0:T(8,128)S(1)}, u32[]{:S(2)}, u32[]{:S(2)}) %collective-permute-start.6) | collective-permute-done | bytes 40992 | tf_op jit(solution)/shard_map/ppermute | solution.py:300
  27.9 3.5 %collective-permute-done.7 = f32[80,128]{1,0:T(8,128)S(1)} collective-permute-done((f32[80,128]{1,0:T(8,128)S(1)}, f32[80,128]{1,0:T(8,128)S(1)}, u32[]{:S(2)}, u32[]{:S(2)}) %collective-permute-start.7) | collective-permute-done | bytes 40992 | tf_op jit(solution)/shard_map/ppermute | solution.py:300
  31.5 0.0 collective-permute-done.8
  31.5 3.4 %collective-permute-start.9 = (f32[80,128]{1,0:T(8,128)S(1)}, f32[80,128]{1,0:T(8,128)S(1)}, u32[]{:S(2)}, u32[]{:S(2)}) collective-permute-start(f32[80,128]{1,0:T(8,128)S(1)} %add_add_fusion), channel_id=1, source_target_pairs={{0,104},{8,96},{16,120},{24,112},{32,72},{40,64},{48,88},{56,80},{... | collective-permute-start | bytes 122888 | tf_op jit(solution)/shard_map/ppermute | solution.py:300
  34.8 2.5 %collective-permute-done.9 = f32[80,128]{1,0:T(8,128)S(1)} collective-permute-done((f32[80,128]{1,0:T(8,128)S(1)}, f32[80,128]{1,0:T(8,128)S(1)}, u32[]{:S(2)}, u32[]{:S(2)}) %collective-permute-start.9) | collective-permute-done | bytes 40992 | tf_op jit(solution)/shard_map/ppermute | solution.py:300
  37.4 0.5 %angles.1.mine_ref = f32[16,128]{1,0:T(8,128)S(1)} custom-call(s32[2,2]{1,0:T(2,128)S(1)} %copy-done.2, f32[80,128]{1,0:T(8,128)S(1)} %add.23.sums_ref), custom_call_target="tpu_custom_call" | custom-call | flops 1000000000 | bytes 1000000 | tf_op jit(solution)/shard_map/angles/pallas_call | solution.py:280
  37.9 0.4 %collective-permute-start.10 = (f32[16,128]{1,0:T(8,128)S(1)}, f32[16,128]{1,0:T(8,128)S(1)}, u32[]{:S(2)}, u32[]{:S(2)}) collective-permute-start(f32[16,128]{1,0:T(8,128)S(1)} %angles.1.mine_ref), channel_id=1, source_target_pairs={{0,8},{8,0},{16,24},{24,16},{32,40},{40,32},{48,56},{56,48},{64,72... | collective-permute-start | bytes 24584 | tf_op jit(solution)/shard_map/ppermute | solution.py:300
  38.3 0.8 %collective-permute-done.10.other_ref = f32[16,128]{1,0:T(8,128)S(1)} collective-permute-done((f32[16,128]{1,0:T(8,128)S(1)}, f32[16,128]{1,0:T(8,128)S(1)}, u32[]{:S(2)}, u32[]{:S(2)}) %collective-permute-start.10) | collective-permute-done | bytes 8224 | tf_op jit(solution)/shard_map/ppermute | solution.py:300
  39.1 1.4 %last.1 = (f32[256,512]{1,0:T(8,128)}, f32[1,512]{1,0:T(1,128)}) custom-call(s32[2,2]{1,0:T(2,128)S(1)} %copy-done.2, f32[16,128]{1,0:T(8,128)S(1)} %angles.1.mine_ref, f32[16,128]{1,0:T(8,128)S(1)} %collective-permute-done.10.other_ref, f32[256,256]{1,0:T(8,128)S(1)} %get-tuple-element.12.own_ref.first_ref, ...), custom_call_target="tpu_custom_call" | custom-call | flops 1000000000 | bytes 1000000 | tf_op jit(solution)/shard_map/last/pallas_call | solution.py:280
  (7 shorter events, 0.1 us)
Async XLA Ops:
  1.8 9.0 %collective-permute-start.2 = (f32[256,256]{1,0:T(8,128)S(1)}, f32[256,256]{1,0:T(8,128)S(1)}, u32[]{:S(2)}, u32[]{:S(2)}) collective-permute-start(f32[256,256]{1,0:T(8,128)S(1)} %pad_maximum_fusion.first_raw), channel_id=1, source_target_pairs={{0,1},{1,0},{2,3},{3,2},{4,5},{5,4},{6,7},{7,6},{8,9},{9,8},{10,11... | collective-permute-start | bytes 786440 | tf_op jit(solution)/shard_map/ppermute | solution.py:318
  3.9 3.0 %copy-start = (f32[512]{0:T(512)S(1)}, f32[512]{0:T(512)}, u32[]{:S(2)}) copy-start(f32[512]{0:T(512)} %param.5) | copy-start | bytes 6148
  3.9 3.0 %copy-start.2 = (s32[2,2]{1,0:T(2,128)S(1)}, s32[2,2]{1,0:T(2,128)}, u32[]{:S(2)}) copy-start(s32[2,2]{1,0:T(2,128)} %offsets.9) | copy-start | bytes 52
  4.0 2.9 %copy-start.1 = (s32[2,2]{1,0:T(2,128)S(1)}, s32[2,2]{1,0:T(2,128)}, u32[]{:S(2)}) copy-start(s32[2,2]{1,0:T(2,128)} %skip.5) | copy-start | bytes 52
  4.0 9.0 %collective-permute-start = (f32[256,256]{1,0:T(8,128)S(1)}, f32[256,256]{1,0:T(8,128)S(1)}, u32[]{:S(2)}, u32[]{:S(2)}) collective-permute-start(f32[256,256]{1,0:T(8,128)S(1)} %pad_maximum_fusion.1.second_raw), channel_id=1, source_target_pairs={{0,7},{1,2},{2,1},{3,4},{4,3},{5,6},{6,5},{7,0},{8,15},{9,10},{10,... | collective-permute-start | bytes 786440 | tf_op jit(solution)/shard_map/ppermute | solution.py:321
  7.7 3.1 %collective-permute-start.3 = (f32[24,128]{1,0:T(8,128)S(1)}, f32[24,128]{1,0:T(8,128)S(1)}, u32[]{:S(2)}, u32[]{:S(2)}) collective-permute-start(f32[24,128]{1,0:T(8,128)S(1)} %get-tuple-element.13.own_side), channel_id=1, source_target_pairs={{0,1},{1,0},{2,3},{3,2},{4,5},{5,4},{6,7},{7,6},{8,9},{9,8},{10,11... | collective-permute-start | bytes 36872 | tf_op jit(solution)/shard_map/ppermute | solution.py:318
  7.8 5.2 %collective-permute-start.1 = (f32[24,128]{1,0:T(8,128)S(1)}, f32[24,128]{1,0:T(8,128)S(1)}, u32[]{:S(2)}, u32[]{:S(2)}) collective-permute-start(f32[24,128]{1,0:T(8,128)S(1)} %get-tuple-element.14.end_side.own_side), channel_id=1, source_target_pairs={{0,7},{1,2},{2,1},{3,4},{4,3},{5,6},{6,5},{7,0},{8,15},{9,10},{10,... | collective-permute-start | bytes 36872 | tf_op jit(solution)/shard_map/ppermute | solution.py:321
  13.9 3.1 %collective-permute-start.4 = (f32[80,128]{1,0:T(8,128)S(1)}, f32[80,128]{1,0:T(8,128)S(1)}, u32[]{:S(2)}, u32[]{:S(2)}) collective-permute-start(f32[80,128]{1,0:T(8,128)S(1)} %broadcast_select_fusion), channel_id=1, source_target_pairs={{0,8},{8,0},{16,24},{24,16},{32,40},{40,32},{48,56},{56,48},{64,72... | collective-permute-start | bytes 122888 | tf_op jit(solution)/shard_map/ppermute | solution.py:300
  17.1 5.1 %collective-permute-start.5 = (f32[80,128]{1,0:T(8,128)S(1)}, f32[80,128]{1,0:T(8,128)S(1)}, u32[]{:S(2)}, u32[]{:S(2)}) collective-permute-start(f32[80,128]{1,0:T(8,128)S(1)} %select_add_fusion), channel_id=1, source_target_pairs={{0,136},{8,128},{16,152},{24,144},{32,168},{40,160},{48,184},{56,1... | collective-permute-start | bytes 122888 | tf_op jit(solution)/shard_map/ppermute | solution.py:300
  22.2 5.7 %collective-permute-start.6 = (f32[80,128]{1,0:T(8,128)S(1)}, f32[80,128]{1,0:T(8,128)S(1)}, u32[]{:S(2)}, u32[]{:S(2)}) collective-permute-start(f32[80,128]{1,0:T(8,128)S(1)} %add.19), channel_id=1, source_target_pairs={{0,48},{8,56},{16,32},{24,40},{32,16},{40,24},{48,0},{56,8},{64,11... | collective-permute-start | bytes 122888 | tf_op jit(solution)/shard_map/ppermute | solution.py:300
  26.5 4.9 %collective-permute-start.7 = (f32[80,128]{1,0:T(8,128)S(1)}, f32[80,128]{1,0:T(8,128)S(1)}, u32[]{:S(2)}, u32[]{:S(2)}) collective-permute-start(f32[80,128]{1,0:T(8,128)S(1)} %add.19), channel_id=1, source_target_pairs={{0,40},{8,32},{16,56},{24,48},{32,8},{40,0},{48,24},{56,16},{64,10... | collective-permute-start | bytes 122888 | tf_op jit(solution)/shard_map/ppermute | solution.py:300
  26.5 4.9 %collective-permute-start.8 = (f32[80,128]{1,0:T(8,128)S(1)}, f32[80,128]{1,0:T(8,128)S(1)}, u32[]{:S(2)}, u32[]{:S(2)}) collective-permute-start(f32[80,128]{1,0:T(8,128)S(1)} %add.19), channel_id=1, source_target_pairs={{0,24},{8,16},{16,8},{24,0},{32,56},{40,48},{48,40},{56,32},{64,88... | collective-permute-start | bytes 122888 | tf_op jit(solution)/shard_map/ppermute | solution.py:300
  31.5 5.9 %collective-permute-start.9 = (f32[80,128]{1,0:T(8,128)S(1)}, f32[80,128]{1,0:T(8,128)S(1)}, u32[]{:S(2)}, u32[]{:S(2)}) collective-permute-start(f32[80,128]{1,0:T(8,128)S(1)} %add_add_fusion), channel_id=1, source_target_pairs={{0,104},{8,96},{16,120},{24,112},{32,72},{40,64},{48,88},{56,80},{... | collective-permute-start | bytes 122888 | tf_op jit(solution)/shard_map/ppermute | solution.py:300
  37.9 1.3 %collective-permute-start.10 = (f32[16,128]{1,0:T(8,128)S(1)}, f32[16,128]{1,0:T(8,128)S(1)}, u32[]{:S(2)}, u32[]{:S(2)}) collective-permute-start(f32[16,128]{1,0:T(8,128)S(1)} %angles.1.mine_ref), channel_id=1, source_target_pairs={{0,8},{8,0},{16,24},{24,16},{32,40},{40,32},{48,56},{56,48},{64,72... | collective-permute-start | bytes 24584 | tf_op jit(solution)/shard_map/ppermute | solution.py:300

commit v7 on v6

--- a/solution.py
+++ b/solution.py
@@ -72,20 +72,22 @@
         out_ref[start + index : start + index + 1, :] = value
 
 
-def lagged(x, y, lag, gap):
-    terms = []
-    for by in (lag - gap, lag, lag + gap):
-        moved = [left(half, by) for half in y]
-        terms += [a * b for a in x for b in moved]
-    return terms
+def moved_by_gap(x, lags):
+    return [left(half, lags.gap) for half in x], x, [right(half, lags.gap) for half in x]
+
+
+def lagged(x_moved, y, lag):
+    ahead = [left(half, lag) for half in y]
+    return [a * b for x in x_moved for a in x for b in ahead]
 
 
 def pair_stats(ref, lags):
     def terms(span):
-        upper, lower = halves(ref, span)
-        upper_gap, lower_gap = left(upper, lags.gap), left(lower, lags.gap)
+        pair = halves(ref, span)
+        moved = moved_by_gap(pair, lags)
+        (upper, lower), (upper_gap, lower_gap) = pair, moved[0]
         step_0 = [upper * upper, lower * lower, upper * lower, upper * lower_gap, upper_gap * lower, upper * upper_gap, lower * lower_gap]
-        return step_0 + lagged((upper, lower), (upper, lower), lags.turn, lags.gap)
+        return step_0 + lagged(moved, pair, lags.turn)
 
     return sums_over(ref.shape[0], terms)
 
@@ -133,7 +135,7 @@
         for b in range(2):
             (x_here, x_gap), (y_here, y_gap) = x_weights[a], y_weights[b]
             before, at, after = [dots[4 * index + 2 * a + b] for index in range(3)]
-            part = x_here * (y_here * at + y_gap * after) + x_gap * (y_here * left(before, gap) + y_gap * left(at, gap))
+            part = x_here * (y_here * at + y_gap * left(after, gap)) + x_gap * (y_here * before + y_gap * left(at, gap))
             total = part if total is None else total + part
     return total
 
@@ -165,7 +167,7 @@
         store_rows(side, 0, rows + [jnp.zeros_like(flag)] * (SIDE - len(rows)))
 
 
-def cross_kernel(odd_slot, offsets, skip, own_ref, own_side, raw_ref, come_side, end_ref, end_side, out_ref, come_ref):
+def cross_kernel(odd_slot, offsets, skip, own_ref, own_side, raw_ref, come_side, end_ref, end_side, _, out_ref, come_ref, moved_ref):
     is_even = (lax.axis_index("pairs") & 1) == 0
     slot = jnp.where(is_even, 1 - odd_slot, odd_slot)
     lags = Lags(offsets, slot)
@@ -188,11 +190,17 @@
 
     x_side, y_side = pick(own, come)
     store_rows(out_ref, 0, x_side[:STATS] + y_side[:STATS])
+    for start in range(0, own_ref.shape[0], BATCH):
+        span = slice(start, start + BATCH)
+        x, _ = pick(halves(own_ref, span), halves(come_ref, span))
+        for at, half in enumerate(half for pair in moved_by_gap(x, lags) for half in pair):
+            moved_ref[span, at * BLOCK : (at + 1) * BLOCK] = half
     for index, lag in enumerate(lags.crossed()):
 
         def terms(span):
-            x, y = pick(halves(own_ref, span), halves(come_ref, span))
-            return lagged(x, y, lag, lags.gap)
+            _, y = pick(halves(own_ref, span), halves(come_ref, span))
+            moved = [[moved_ref[span, at * BLOCK : (at + 1) * BLOCK] for at in (two, two + 1)] for two in (0, 2, 4)]
+            return lagged(moved, y, lag)
 
         store_rows(out_ref, CROSS + 12 * index, sums_over(own_ref.shape[0], terms))
     store_rows(out_ref, FLAGS, x_side[-1:] + y_side[-1:] + [step_flag] + [jnp.zeros_like(step_flag)] * (SUMS - FLAGS - 3))
@@ -318,7 +326,14 @@
         return lax.ppermute(x, "pairs", [(at, at ^ 1) for at in range(pairs)])
 
     def swap_second(x):
-        return lax.ppermute(x, "pairs", [(at, (((at + 1) ^ 1) - 1) % pairs) for at in range(pairs)])
+        size = lax.axis_size("rows")
+
+        def other(row, at):
+            to = (row, ((at + 1) ^ 1) - 1) if 0 < at < pairs - 1 else (row ^ 1, at)
+            return to[0] * pairs + to[1]
+
+        places = [(row, at) for row in range(size) for at in range(pairs)]
+        return lax.ppermute(x, ("rows", "pairs"), [(row * pairs + at, other(row, at)) for row, at in places])
 
     pair, side = ((rows, 2 * BLOCK), VMEM), ((SIDE, BLOCK), VMEM)
     second_raw = swap_second(raw[1])
@@ -329,17 +344,19 @@
     ]
     slots, come = [], []
     for odd_slot, own, own_side, raw_come, side_come in (
+        (1, first, first_side, second_raw, swap_second(second_side[0])),
         (0, second, second_side, first_raw, swap_first(first_side[0])),
-        (1, first, first_side, second_raw, swap_second(second_side[0])),
     ):
         sums, aligned = call(
             functools.partial(cross_kernel, odd_slot),
-            [offsets, skips, own, own_side, (raw_come, VMEM), (side_come, VMEM), second, second_side],
+            [offsets, skips, own, own_side, (raw_come, VMEM), (side_come, VMEM), second, second_side, (slots[-1] if slots else second_side[0], VMEM)],
             [((SUMS, BLOCK), VMEM), pair],
             "cross",
+            [pltpu.VMEM((rows, 6 * BLOCK), jnp.float32)],
         )
         slots.append(sums)
         come.append((aligned, VMEM))
+    slots, come = slots[::-1], come[::-1]
     keeps_first = (lax.axis_index("pairs") & 1) == kept_slot()
     sums = jnp.where(keeps_first, slots[1], slots[0])
     sums = sums + swap_rows(jnp.where(keeps_first, slots[0], slots[1]), lambda y, z, core: (y, z, 1 - core))

time: 40.6 us -> 39.4 us (0.970)
  the two profiles are of different devices: /device:TPU:1 before, /device:TPU:9 now
where the time goes in v7:
time: 39.4 us; the launch traced here: 38.9 us
  starting transfers between devices  16.6 us (42%)
  waiting for transfers between devices  15.7 us (40%)
  Pallas kernels  4.05 us (10%)
  other arithmetic  1.22 us (3%)
  between operations  0.72 us (2%)
  local copies, waits for them, and re-layouts  0.53 us (1%)
    ppermute x7, starting transfers between devices, swap_rows(): return lax.ppermute(x, 'rows', [(row, other(row)) for row in range(size)])  12.7 us
    ppermute x7, waiting for transfers between devices, swap_rows(): return lax.ppermute(x, 'rows', [(row, other(row)) for row in range(size)])  11.3 us
    ppermute x2, waiting for transfers between devices, swap_second(): lax.ppermute(x, ('rows', 'pairs'), [(row * pairs + at, other(row, at)) fo...  4.46 us
    pallas_call x5, Pallas kernels, call(): pl.pallas_call(kernel, out_shape=[jax.ShapeDtypeStruct(shape, jnp.float32...  4.05 us
    ppermute x2, starting transfers between devices, swap_second(): lax.ppermute(x, ('rows', 'pairs'), [(row * pairs + at, other(row, at)) fo...  3.75 us
    select_n x1, other arithmetic, per_device(): jnp.where(is_even, blocks[even + at], blocks[1 - even + at])  1.14 us
  transfers between devices with their start and end apart: 11, of which 7 were waited for; matrix products, arithmetic and copies ran while one was open for 0% of the time, Pallas kernels for 4%

profile of v7, /device:TPU:9, one launch (start us, length us, event | category | flops | bytes accessed | tf_op | source)
XLA Modules:
  0.0 38.9 jit_solution(8109065174224984878)
XLA Ops:
  0.6 1.1 %slice_select_fusion.2 = (f32[256,128]{1,0:T(8,128)S(1)}, f32[256,128]{1,0:T(8,128)S(1)}, f32[256,128]{1,0:T(8,128)S(1)}, f32[256,128]{1,0:T(8,128)S(1)}) fusion(f32[256,512]{1,0:T(8,128)} %param.4, pred[]{:T(512)S(6)} %eq.7), kind=kLoop, calls=%fused_computation.4 | loop fusion | flops 131072 | bytes 1048577 | tf_op jit(solution)/shard_map/jit(_where)/select_n | solution.py:322
  1.8 2.5 %collective-permute-start = (f32[256,256]{1,0:T(8,128)S(1)}, f32[256,256]{1,0:T(8,128)S(1)}, u32[]{:S(2)}, u32[]{:S(2)}) collective-permute-start(f32[256,256]{1,0:T(8,128)S(1)} %pad_maximum_fusion.1.second_raw), channel_id=1, source_target_pairs={{0,8},{1,2},{2,1},{3,4},{4,3},{5,6},{6,5},{7,15},{8,0},{9,10},{10,... | collective-permute-start | bytes 786440 | tf_op jit(solution)/shard_map/ppermute | solution.py:336
  4.3 0.0 copy-start
  4.3 0.0 copy-start.2
  4.3 0.0 copy-start.1
  4.3 0.1 collective-permute-start.2
  4.4 0.5 %copy-done = f32[512]{0:T(512)S(1)} copy-done((f32[512]{0:T(512)S(1)}, f32[512]{0:T(512)}, u32[]{:S(2)}) %copy-start) | copy-done | bytes 2072
  4.9 0.0 copy-done.2
  5.0 0.0 copy-done.1
  5.0 0.7 %own.1 = (f32[256,256]{1,0:T(8,128)S(1)}, f32[256,256]{1,0:T(8,128)S(1)}, f32[24,128]{1,0:T(8,128)S(1)}, f32[24,128]{1,0:T(8,128)S(1)}) custom-call(s32[2,2]{1,0:T(2,128)S(1)} %copy-done.2, s32[2,2]{1,0:T(2,128)S(1)} %copy-done.1, f32[1,512]{1,0:T(1,128)S(1)} %bitcast.2, f32[256,256]{1,0:T(8,128)S(1)} %pad_maximum_fusion.first_raw, ...), custom_call_target="tpu_custom_call" | custom-call | flops 1000000000 | bytes 1000000 | tf_op jit(solution)/shard_map/own/pallas_call | solution.py:288
  5.7 1.3 %collective-permute-start.1 = (f32[24,128]{1,0:T(8,128)S(1)}, f32[24,128]{1,0:T(8,128)S(1)}, u32[]{:S(2)}, u32[]{:S(2)}) collective-permute-start(f32[24,128]{1,0:T(8,128)S(1)} %get-tuple-element.14.end_side._.own_side), channel_id=1, source_target_pairs={{0,8},{1,2},{2,1},{3,4},{4,3},{5,6},{6,5},{7,15},{8,0},{9,10},{10,... | collective-permute-start | bytes 36872 | tf_op jit(solution)/shard_map/ppermute | solution.py:336
  7.0 0.0 collective-permute-start.3
  7.0 4.5 %collective-permute-done.1.come_side = f32[24,128]{1,0:T(8,128)S(1)} collective-permute-done((f32[24,128]{1,0:T(8,128)S(1)}, f32[24,128]{1,0:T(8,128)S(1)}, u32[]{:S(2)}, u32[]{:S(2)}) %collective-permute-start.1) | collective-permute-done | bytes 12320 | tf_op jit(solution)/shard_map/ppermute | solution.py:336
  11.4 0.0 collective-permute-done.raw_ref
  11.4 0.8 %cross.2 = (f32[80,128]{1,0:T(8,128)S(1)}, f32[256,256]{1,0:T(8,128)S(1)}) custom-call(s32[2,2]{1,0:T(2,128)S(1)} %copy-done.2, s32[2,2]{1,0:T(2,128)S(1)} %copy-done.1, f32[256,256]{1,0:T(8,128)S(1)} %get-tuple-element.12.own_ref.first_ref, f32[24,128]{1,0:T(8,128)S(1)} %get-tuple-element.13.own_side, f32[256,256]{1,0:T(8,128)S(1)} %collective-permute-done.raw_ref, ...), custom_call_target="tpu_custom_call" | custom-call | flops 1000000000 | bytes 1000000 | tf_op jit(solution)/shard_map/cross/pallas_call | solution.py:288
  12.2 0.0 collective-permute-done.3.come_side
  12.2 0.0 collective-permute-done.2.raw_ref
  12.2 0.7 %cross.3 = (f32[80,128]{1,0:T(8,128)S(1)}, f32[256,256]{1,0:T(8,128)S(1)}) custom-call(s32[2,2]{1,0:T(2,128)S(1)} %copy-done.2, s32[2,2]{1,0:T(2,128)S(1)} %copy-done.1, f32[256,256]{1,0:T(8,128)S(1)} %get-tuple-element.15.end_ref.own_ref.second_ref, f32[24,128]{1,0:T(8,128)S(1)} %get-tuple-element.14.end_side._.own_side, ...), custom_call_target="tpu_custom_call" | custom-call | flops 1000000000 | bytes 1000000 | tf_op jit(solution)/shard_map/cross/pallas_call | solution.py:288
  13.0 1.6 %collective-permute-start.4 = (f32[80,128]{1,0:T(8,128)S(1)}, f32[80,128]{1,0:T(8,128)S(1)}, u32[]{:S(2)}, u32[]{:S(2)}) collective-permute-start(f32[80,128]{1,0:T(8,128)S(1)} %broadcast_select_fusion), channel_id=1, source_target_pairs={{0,8},{8,0},{16,24},{24,16},{32,40},{40,32},{48,56},{56,48},{64,72... | collective-permute-start | bytes 122888 | tf_op jit(solution)/shard_map/ppermute | solution.py:308
  14.6 0.9 %collective-permute-done.4 = f32[80,128]{1,0:T(8,128)S(1)} collective-permute-done((f32[80,128]{1,0:T(8,128)S(1)}, f32[80,128]{1,0:T(8,128)S(1)}, u32[]{:S(2)}, u32[]{:S(2)}) %collective-permute-start.4) | collective-permute-done | bytes 40992 | tf_op jit(solution)/shard_map/ppermute | solution.py:308
  15.5 2.3 %collective-permute-start.5 = (f32[80,128]{1,0:T(8,128)S(1)}, f32[80,128]{1,0:T(8,128)S(1)}, u32[]{:S(2)}, u32[]{:S(2)}) collective-permute-start(f32[80,128]{1,0:T(8,128)S(1)} %select_add_fusion), channel_id=1, source_target_pairs={{0,136},{8,128},{16,152},{24,144},{32,168},{40,160},{48,184},{56,1... | collective-permute-start | bytes 122888 | tf_op jit(solution)/shard_map/ppermute | solution.py:308
  17.8 2.8 %collective-permute-done.5 = f32[80,128]{1,0:T(8,128)S(1)} collective-permute-done((f32[80,128]{1,0:T(8,128)S(1)}, f32[80,128]{1,0:T(8,128)S(1)}, u32[]{:S(2)}, u32[]{:S(2)}) %collective-permute-start.5) | collective-permute-done | bytes 40992 | tf_op jit(solution)/shard_map/ppermute | solution.py:308
  20.6 4.3 %collective-permute-start.6 = (f32[80,128]{1,0:T(8,128)S(1)}, f32[80,128]{1,0:T(8,128)S(1)}, u32[]{:S(2)}, u32[]{:S(2)}) collective-permute-start(f32[80,128]{1,0:T(8,128)S(1)} %add.19), channel_id=1, source_target_pairs={{0,48},{8,56},{16,32},{24,40},{32,16},{40,24},{48,0},{56,8},{64,11... | collective-permute-start | bytes 122888 | tf_op jit(solution)/shard_map/ppermute | solution.py:308
  24.9 0.0 collective-permute-start.7
  24.9 0.7 %collective-permute-start.8 = (f32[80,128]{1,0:T(8,128)S(1)}, f32[80,128]{1,0:T(8,128)S(1)}, u32[]{:S(2)}, u32[]{:S(2)}) collective-permute-start(f32[80,128]{1,0:T(8,128)S(1)} %add.19), channel_id=1, source_target_pairs={{0,24},{8,16},{16,8},{24,0},{32,56},{40,48},{48,40},{56,32},{64,88... | collective-permute-start | bytes 122888 | tf_op jit(solution)/shard_map/ppermute | solution.py:308
  25.6 0.7 %collective-permute-done.6 = f32[80,128]{1,0:T(8,128)S(1)} collective-permute-done((f32[80,128]{1,0:T(8,128)S(1)}, f32[80,128]{1,0:T(8,128)S(1)}, u32[]{:S(2)}, u32[]{:S(2)}) %collective-permute-start.6) | collective-permute-done | bytes 40992 | tf_op jit(solution)/shard_map/ppermute | solution.py:308
  26.3 3.5 %collective-permute-done.7 = f32[80,128]{1,0:T(8,128)S(1)} collective-permute-done((f32[80,128]{1,0:T(8,128)S(1)}, f32[80,128]{1,0:T(8,128)S(1)}, u32[]{:S(2)}, u32[]{:S(2)}) %collective-permute-start.7) | collective-permute-done | bytes 40992 | tf_op jit(solution)/shard_map/ppermute | solution.py:308
  29.9 0.0 collective-permute-done.8
  29.9 3.4 %collective-permute-start.9 = (f32[80,128]{1,0:T(8,128)S(1)}, f32[80,128]{1,0:T(8,128)S(1)}, u32[]{:S(2)}, u32[]{:S(2)}) collective-permute-start(f32[80,128]{1,0:T(8,128)S(1)} %add_add_fusion), channel_id=1, source_target_pairs={{0,104},{8,96},{16,120},{24,112},{32,72},{40,64},{48,88},{56,80},{... | collective-permute-start | bytes 122888 | tf_op jit(solution)/shard_map/ppermute | solution.py:308
  33.2 2.5 %collective-permute-done.9 = f32[80,128]{1,0:T(8,128)S(1)} collective-permute-done((f32[80,128]{1,0:T(8,128)S(1)}, f32[80,128]{1,0:T(8,128)S(1)}, u32[]{:S(2)}, u32[]{:S(2)}) %collective-permute-start.9) | collective-permute-done | bytes 40992 | tf_op jit(solution)/shard_map/ppermute | solution.py:308
  35.8 0.5 %angles.1.mine_ref = f32[16,128]{1,0:T(8,128)S(1)} custom-call(s32[2,2]{1,0:T(2,128)S(1)} %copy-done.2, f32[80,128]{1,0:T(8,128)S(1)} %add.23.sums_ref), custom_call_target="tpu_custom_call" | custom-call | flops 1000000000 | bytes 1000000 | tf_op jit(solution)/shard_map/angles/pallas_call | solution.py:288
  36.3 0.4 %collective-permute-start.10 = (f32[16,128]{1,0:T(8,128)S(1)}, f32[16,128]{1,0:T(8,128)S(1)}, u32[]{:S(2)}, u32[]{:S(2)}) collective-permute-start(f32[16,128]{1,0:T(8,128)S(1)} %angles.1.mine_ref), channel_id=1, source_target_pairs={{0,8},{8,0},{16,24},{24,16},{32,40},{40,32},{48,56},{56,48},{64,72... | collective-permute-start | bytes 24584 | tf_op jit(solution)/shard_map/ppermute | solution.py:308
  36.7 0.8 %collective-permute-done.10.other_ref = f32[16,128]{1,0:T(8,128)S(1)} collective-permute-done((f32[16,128]{1,0:T(8,128)S(1)}, f32[16,128]{1,0:T(8,128)S(1)}, u32[]{:S(2)}, u32[]{:S(2)}) %collective-permute-start.10) | collective-permute-done | bytes 8224 | tf_op jit(solution)/shard_map/ppermute | solution.py:308
  37.5 1.4 %last.1 = (f32[256,512]{1,0:T(8,128)}, f32[1,512]{1,0:T(1,128)}) custom-call(s32[2,2]{1,0:T(2,128)S(1)} %copy-done.2, f32[16,128]{1,0:T(8,128)S(1)} %angles.1.mine_ref, f32[16,128]{1,0:T(8,128)S(1)} %collective-permute-done.10.other_ref, f32[256,256]{1,0:T(8,128)S(1)} %get-tuple-element.12.own_ref.first_ref, ...), custom_call_target="tpu_custom_call" | custom-call | flops 1000000000 | bytes 1000000 | tf_op jit(solution)/shard_map/last/pallas_call | solution.py:288
  (7 shorter events, 0.1 us)
Async XLA Ops:
  1.8 9.6 %collective-permute-start = (f32[256,256]{1,0:T(8,128)S(1)}, f32[256,256]{1,0:T(8,128)S(1)}, u32[]{:S(2)}, u32[]{:S(2)}) collective-permute-start(f32[256,256]{1,0:T(8,128)S(1)} %pad_maximum_fusion.1.second_raw), channel_id=1, source_target_pairs={{0,8},{1,2},{2,1},{3,4},{4,3},{5,6},{6,5},{7,15},{8,0},{9,10},{10,... | collective-permute-start | bytes 786440 | tf_op jit(solution)/shard_map/ppermute | solution.py:336
  4.3 0.7 %copy-start = (f32[512]{0:T(512)S(1)}, f32[512]{0:T(512)}, u32[]{:S(2)}) copy-start(f32[512]{0:T(512)} %param.5) | copy-start | bytes 6148
  4.3 0.7 %copy-start.2 = (s32[2,2]{1,0:T(2,128)S(1)}, s32[2,2]{1,0:T(2,128)}, u32[]{:S(2)}) copy-start(s32[2,2]{1,0:T(2,128)} %offsets.9) | copy-start | bytes 52
  4.3 0.7 %copy-start.1 = (s32[2,2]{1,0:T(2,128)S(1)}, s32[2,2]{1,0:T(2,128)}, u32[]{:S(2)}) copy-start(s32[2,2]{1,0:T(2,128)} %skip.5) | copy-start | bytes 52
  4.3 7.9 %collective-permute-start.2 = (f32[256,256]{1,0:T(8,128)S(1)}, f32[256,256]{1,0:T(8,128)S(1)}, u32[]{:S(2)}, u32[]{:S(2)}) collective-permute-start(f32[256,256]{1,0:T(8,128)S(1)} %pad_maximum_fusion.first_raw), channel_id=1, source_target_pairs={{0,1},{1,0},{2,3},{3,2},{4,5},{5,4},{6,7},{7,6},{8,9},{9,8},{10,11... | collective-permute-start | bytes 786440 | tf_op jit(solution)/shard_map/ppermute | solution.py:326
  5.7 5.8 %collective-permute-start.1 = (f32[24,128]{1,0:T(8,128)S(1)}, f32[24,128]{1,0:T(8,128)S(1)}, u32[]{:S(2)}, u32[]{:S(2)}) collective-permute-start(f32[24,128]{1,0:T(8,128)S(1)} %get-tuple-element.14.end_side._.own_side), channel_id=1, source_target_pairs={{0,8},{1,2},{2,1},{3,4},{4,3},{5,6},{6,5},{7,15},{8,0},{9,10},{10,... | collective-permute-start | bytes 36872 | tf_op jit(solution)/shard_map/ppermute | solution.py:336
  7.0 5.2 %collective-permute-start.3 = (f32[24,128]{1,0:T(8,128)S(1)}, f32[24,128]{1,0:T(8,128)S(1)}, u32[]{:S(2)}, u32[]{:S(2)}) collective-permute-start(f32[24,128]{1,0:T(8,128)S(1)} %get-tuple-element.13.own_side), channel_id=1, source_target_pairs={{0,1},{1,0},{2,3},{3,2},{4,5},{5,4},{6,7},{7,6},{8,9},{9,8},{10,11... | collective-permute-start | bytes 36872 | tf_op jit(solution)/shard_map/ppermute | solution.py:326
  13.0 2.5 %collective-permute-start.4 = (f32[80,128]{1,0:T(8,128)S(1)}, f32[80,128]{1,0:T(8,128)S(1)}, u32[]{:S(2)}, u32[]{:S(2)}) collective-permute-start(f32[80,128]{1,0:T(8,128)S(1)} %broadcast_select_fusion), channel_id=1, source_target_pairs={{0,8},{8,0},{16,24},{24,16},{32,40},{40,32},{48,56},{56,48},{64,72... | collective-permute-start | bytes 122888 | tf_op jit(solution)/shard_map/ppermute | solution.py:308
  15.5 5.1 %collective-permute-start.5 = (f32[80,128]{1,0:T(8,128)S(1)}, f32[80,128]{1,0:T(8,128)S(1)}, u32[]{:S(2)}, u32[]{:S(2)}) collective-permute-start(f32[80,128]{1,0:T(8,128)S(1)} %select_add_fusion), channel_id=1, source_target_pairs={{0,136},{8,128},{16,152},{24,144},{32,168},{40,160},{48,184},{56,1... | collective-permute-start | bytes 122888 | tf_op jit(solution)/shard_map/ppermute | solution.py:308
  20.6 5.7 %collective-permute-start.6 = (f32[80,128]{1,0:T(8,128)S(1)}, f32[80,128]{1,0:T(8,128)S(1)}, u32[]{:S(2)}, u32[]{:S(2)}) collective-permute-start(f32[80,128]{1,0:T(8,128)S(1)} %add.19), channel_id=1, source_target_pairs={{0,48},{8,56},{16,32},{24,40},{32,16},{40,24},{48,0},{56,8},{64,11... | collective-permute-start | bytes 122888 | tf_op jit(solution)/shard_map/ppermute | solution.py:308
  24.9 4.9 %collective-permute-start.7 = (f32[80,128]{1,0:T(8,128)S(1)}, f32[80,128]{1,0:T(8,128)S(1)}, u32[]{:S(2)}, u32[]{:S(2)}) collective-permute-start(f32[80,128]{1,0:T(8,128)S(1)} %add.19), channel_id=1, source_target_pairs={{0,40},{8,32},{16,56},{24,48},{32,8},{40,0},{48,24},{56,16},{64,10... | collective-permute-start | bytes 122888 | tf_op jit(solution)/shard_map/ppermute | solution.py:308
  24.9 4.9 %collective-permute-start.8 = (f32[80,128]{1,0:T(8,128)S(1)}, f32[80,128]{1,0:T(8,128)S(1)}, u32[]{:S(2)}, u32[]{:S(2)}) collective-permute-start(f32[80,128]{1,0:T(8,128)S(1)} %add.19), channel_id=1, source_target_pairs={{0,24},{8,16},{16,8},{24,0},{32,56},{40,48},{48,40},{56,32},{64,88... | collective-permute-start | bytes 122888 | tf_op jit(solution)/shard_map/ppermute | solution.py:308
  29.9 5.9 %collective-permute-start.9 = (f32[80,128]{1,0:T(8,128)S(1)}, f32[80,128]{1,0:T(8,128)S(1)}, u32[]{:S(2)}, u32[]{:S(2)}) collective-permute-start(f32[80,128]{1,0:T(8,128)S(1)} %add_add_fusion), channel_id=1, source_target_pairs={{0,104},{8,96},{16,120},{24,112},{32,72},{40,64},{48,88},{56,80},{... | collective-permute-start | bytes 122888 | tf_op jit(solution)/shard_map/ppermute | solution.py:308
  36.3 1.3 %collective-permute-start.10 = (f32[16,128]{1,0:T(8,128)S(1)}, f32[16,128]{1,0:T(8,128)S(1)}, u32[]{:S(2)}, u32[]{:S(2)}) collective-permute-start(f32[16,128]{1,0:T(8,128)S(1)} %angles.1.mine_ref), channel_id=1, source_target_pairs={{0,8},{8,0},{16,24},{24,16},{32,40},{40,32},{48,56},{56,48},{64,72... | collective-permute-start | bytes 24584 | tf_op jit(solution)/shard_map/ppermute | solution.py:308

commit v8 on v7

--- a/solution.py
+++ b/solution.py
@@ -9,6 +9,7 @@
 BLOCK = 128
 GROUP = 8
 BATCH = 128
+LAST_BATCH = 64
 
 STATS = 19
 CROSS = 2 * STATS
@@ -261,8 +262,8 @@
         lags = Lags(offsets, slot)
         blocks = [slice(at * BLOCK, (at + 1) * BLOCK) for at in (slot, 2 + slot)]
         turns = [angles[index : index + 1] for index in range(NORMS)]
-        for start in range(0, rows, BATCH):
-            span = slice(start, start + BATCH)
+        for start in range(0, rows, LAST_BATCH):
+            span = slice(start, start + LAST_BATCH)
             x, y = [
                 [jnp.where(is_even, a, b) for a, b in zip(halves(even_ref, span), halves(odd_ref, span))]
                 for even_ref, odd_ref in sources[slot]
@@ -317,10 +318,12 @@
     weights = (col_weights.reshape(1, columns), VMEM)
     offsets, skips = (partner_offsets, VMEM), (skip_mask, VMEM)
     is_even = (lax.axis_index("pairs") & 1) == 0
-    blocks = [loads[:, at * BLOCK : (at + 1) * BLOCK] for at in range(4)]
-    raw = [
-        jnp.concatenate([jnp.where(is_even, blocks[even + at], blocks[1 - even + at]) for at in (0, 2)], axis=1) for even in (1, 0)
-    ]
+
+    def selected(even):
+        at = jnp.where(is_even, even, 1 - even) * BLOCK
+        return jnp.concatenate([lax.dynamic_slice(loads, (0, at + half * 2 * BLOCK), (rows, BLOCK)) for half in range(2)], axis=1)
+
+    raw = [selected(1), selected(0)]
 
     def swap_first(x):
         return lax.ppermute(x, "pairs", [(at, at ^ 1) for at in range(pairs)])

time: 39.4 us -> 39.4 us (level)
  local copies, waits for them, and re-layouts: 0.53 us -> 1.68 us
  other arithmetic: 1.22 us -> 0.08 us
    dynamic_slice x0 -> x1, local copies, waits for them, and re-layouts: none -> 1.15 us  [selected(): lax.dynamic_slice(loads, (0, at + half * 2 * BLOCK), (rows, BLOCK))]
    select_n x1 -> x0, other arithmetic: 1.14 us -> none  [per_device(): jnp.where(is_even, blocks[even + at], blocks[1 - even + at])]
where the time goes in v8:
time: 39.4 us; the launch traced here: 38.9 us
  starting transfers between devices  16.6 us (42%)
  waiting for transfers between devices  15.7 us (40%)
  Pallas kernels  4.02 us (10%)
  local copies, waits for them, and re-layouts  1.68 us (4%)
  between operations  0.73 us (2%)
    ppermute x7, starting transfers between devices, swap_rows(): return lax.ppermute(x, 'rows', [(row, other(row)) for row in range(size)])  12.7 us
    ppermute x7, waiting for transfers between devices, swap_rows(): return lax.ppermute(x, 'rows', [(row, other(row)) for row in range(size)])  11.3 us
    ppermute x2, waiting for transfers between devices, swap_second(): lax.ppermute(x, ('rows', 'pairs'), [(row * pairs + at, other(row, at)) fo...  4.46 us
    pallas_call x5, Pallas kernels, call(): pl.pallas_call(kernel, out_shape=[jax.ShapeDtypeStruct(shape, jnp.float32...  4.02 us
    ppermute x2, starting transfers between devices, swap_second(): lax.ppermute(x, ('rows', 'pairs'), [(row * pairs + at, other(row, at)) fo...  3.75 us
    dynamic_slice x1, local copies, waits for them, and re-layouts, selected(): lax.dynamic_slice(loads, (0, at + half * 2 * BLOCK), (rows, BLOCK))  1.15 us
  transfers between devices with their start and end apart: 11, of which 7 were waited for; matrix products, arithmetic and copies ran while one was open for 0% of the time, Pallas kernels for 4%

profile of v8, /device:TPU:9, one launch (start us, length us, event | category | flops | bytes accessed | tf_op | source)
XLA Modules:
  0.0 38.9 jit_solution(251828015055439368)
XLA Ops:
  0.6 1.1 %constant_dynamic-slice_fusion.1 = (f32[256,128]{1,0:T(8,128)S(1)}, f32[256,128]{1,0:T(8,128)S(1)}, f32[256,128]{1,0:T(8,128)S(1)}, f32[256,128]{1,0:T(8,128)S(1)}) fusion(f32[256,512]{1,0:T(8,128)} %param.4, s32[]{:T(128)S(6)} %select_n.36, s32[]{:T(128)S(6)} %select_n.34, s32[]{:T(128)S(6)} %select_n.33, s32[]{:T(128)S(6)} %select_n.37), kind=kLoop, calls=%fused_computation.6 | loop fusion | bytes 1048592 | tf_op jit(solution)/shard_map/dynamic_slice | solution.py:324
  1.8 2.5 %collective-permute-start = (f32[256,256]{1,0:T(8,128)S(1)}, f32[256,256]{1,0:T(8,128)S(1)}, u32[]{:S(2)}, u32[]{:S(2)}) collective-permute-start(f32[256,256]{1,0:T(8,128)S(1)} %pad_maximum_fusion.1.second_raw), channel_id=1, source_target_pairs={{0,8},{1,2},{2,1},{3,4},{4,3},{5,6},{6,5},{7,15},{8,0},{9,10},{10,... | collective-permute-start | bytes 786440 | tf_op jit(solution)/shard_map/ppermute | solution.py:339
  4.3 0.0 copy-start
  4.3 0.0 copy-start.2
  4.3 0.0 copy-start.1
  4.3 0.1 collective-permute-start.2
  4.5 0.5 %copy-done = f32[512]{0:T(512)S(1)} copy-done((f32[512]{0:T(512)S(1)}, f32[512]{0:T(512)}, u32[]{:S(2)}) %copy-start) | copy-done | bytes 2072
  5.0 0.0 copy-done.2
  5.0 0.0 copy-done.1
  5.0 0.7 %own.1 = (f32[256,256]{1,0:T(8,128)S(1)}, f32[256,256]{1,0:T(8,128)S(1)}, f32[24,128]{1,0:T(8,128)S(1)}, f32[24,128]{1,0:T(8,128)S(1)}) custom-call(s32[2,2]{1,0:T(2,128)S(1)} %copy-done.2, s32[2,2]{1,0:T(2,128)S(1)} %copy-done.1, f32[1,512]{1,0:T(1,128)S(1)} %bitcast.2, f32[256,256]{1,0:T(8,128)S(1)} %pad_maximum_fusion.first_raw, ...), custom_call_target="tpu_custom_call" | custom-call | flops 1000000000 | bytes 1000000 | tf_op jit(solution)/shard_map/own/pallas_call | solution.py:289
  5.7 1.3 %collective-permute-start.1 = (f32[24,128]{1,0:T(8,128)S(1)}, f32[24,128]{1,0:T(8,128)S(1)}, u32[]{:S(2)}, u32[]{:S(2)}) collective-permute-start(f32[24,128]{1,0:T(8,128)S(1)} %get-tuple-element.14.end_side._.own_side), channel_id=1, source_target_pairs={{0,8},{1,2},{2,1},{3,4},{4,3},{5,6},{6,5},{7,15},{8,0},{9,10},{10,... | collective-permute-start | bytes 36872 | tf_op jit(solution)/shard_map/ppermute | solution.py:339
  7.0 0.0 collective-permute-start.3
  7.0 4.5 %collective-permute-done.1.come_side = f32[24,128]{1,0:T(8,128)S(1)} collective-permute-done((f32[24,128]{1,0:T(8,128)S(1)}, f32[24,128]{1,0:T(8,128)S(1)}, u32[]{:S(2)}, u32[]{:S(2)}) %collective-permute-start.1) | collective-permute-done | bytes 12320 | tf_op jit(solution)/shard_map/ppermute | solution.py:339
  11.5 0.0 collective-permute-done.raw_ref
  11.5 0.8 %cross.2 = (f32[80,128]{1,0:T(8,128)S(1)}, f32[256,256]{1,0:T(8,128)S(1)}) custom-call(s32[2,2]{1,0:T(2,128)S(1)} %copy-done.2, s32[2,2]{1,0:T(2,128)S(1)} %copy-done.1, f32[256,256]{1,0:T(8,128)S(1)} %get-tuple-element.12.own_ref.first_ref, f32[24,128]{1,0:T(8,128)S(1)} %get-tuple-element.13.own_side, f32[256,256]{1,0:T(8,128)S(1)} %collective-permute-done.raw_ref, ...), custom_call_target="tpu_custom_call" | custom-call | flops 1000000000 | bytes 1000000 | tf_op jit(solution)/shard_map/cross/pallas_call | solution.py:289
  12.2 0.0 collective-permute-done.3.come_side
  12.2 0.0 collective-permute-done.2.raw_ref
  12.2 0.7 %cross.3 = (f32[80,128]{1,0:T(8,128)S(1)}, f32[256,256]{1,0:T(8,128)S(1)}) custom-call(s32[2,2]{1,0:T(2,128)S(1)} %copy-done.2, s32[2,2]{1,0:T(2,128)S(1)} %copy-done.1, f32[256,256]{1,0:T(8,128)S(1)} %get-tuple-element.15.end_ref.own_ref.second_ref, f32[24,128]{1,0:T(8,128)S(1)} %get-tuple-element.14.end_side._.own_side, ...), custom_call_target="tpu_custom_call" | custom-call | flops 1000000000 | bytes 1000000 | tf_op jit(solution)/shard_map/cross/pallas_call | solution.py:289
  13.0 1.6 %collective-permute-start.4 = (f32[80,128]{1,0:T(8,128)S(1)}, f32[80,128]{1,0:T(8,128)S(1)}, u32[]{:S(2)}, u32[]{:S(2)}) collective-permute-start(f32[80,128]{1,0:T(8,128)S(1)} %broadcast_select_fusion), channel_id=1, source_target_pairs={{0,8},{8,0},{16,24},{24,16},{32,40},{40,32},{48,56},{56,48},{64,72... | collective-permute-start | bytes 122888 | tf_op jit(solution)/shard_map/ppermute | solution.py:309
  14.6 0.9 %collective-permute-done.4 = f32[80,128]{1,0:T(8,128)S(1)} collective-permute-done((f32[80,128]{1,0:T(8,128)S(1)}, f32[80,128]{1,0:T(8,128)S(1)}, u32[]{:S(2)}, u32[]{:S(2)}) %collective-permute-start.4) | collective-permute-done | bytes 40992 | tf_op jit(solution)/shard_map/ppermute | solution.py:309
  15.5 2.3 %collective-permute-start.5 = (f32[80,128]{1,0:T(8,128)S(1)}, f32[80,128]{1,0:T(8,128)S(1)}, u32[]{:S(2)}, u32[]{:S(2)}) collective-permute-start(f32[80,128]{1,0:T(8,128)S(1)} %select_add_fusion), channel_id=1, source_target_pairs={{0,136},{8,128},{16,152},{24,144},{32,168},{40,160},{48,184},{56,1... | collective-permute-start | bytes 122888 | tf_op jit(solution)/shard_map/ppermute | solution.py:309
  17.8 2.8 %collective-permute-done.5 = f32[80,128]{1,0:T(8,128)S(1)} collective-permute-done((f32[80,128]{1,0:T(8,128)S(1)}, f32[80,128]{1,0:T(8,128)S(1)}, u32[]{:S(2)}, u32[]{:S(2)}) %collective-permute-start.5) | collective-permute-done | bytes 40992 | tf_op jit(solution)/shard_map/ppermute | solution.py:309
  20.6 4.3 %collective-permute-start.6 = (f32[80,128]{1,0:T(8,128)S(1)}, f32[80,128]{1,0:T(8,128)S(1)}, u32[]{:S(2)}, u32[]{:S(2)}) collective-permute-start(f32[80,128]{1,0:T(8,128)S(1)} %add.47), channel_id=1, source_target_pairs={{0,48},{8,56},{16,32},{24,40},{32,16},{40,24},{48,0},{56,8},{64,11... | collective-permute-start | bytes 122888 | tf_op jit(solution)/shard_map/ppermute | solution.py:309
  25.0 0.0 collective-permute-start.7
  25.0 0.7 %collective-permute-start.8 = (f32[80,128]{1,0:T(8,128)S(1)}, f32[80,128]{1,0:T(8,128)S(1)}, u32[]{:S(2)}, u32[]{:S(2)}) collective-permute-start(f32[80,128]{1,0:T(8,128)S(1)} %add.47), channel_id=1, source_target_pairs={{0,24},{8,16},{16,8},{24,0},{32,56},{40,48},{48,40},{56,32},{64,88... | collective-permute-start | bytes 122888 | tf_op jit(solution)/shard_map/ppermute | solution.py:309
  25.6 0.7 %collective-permute-done.6 = f32[80,128]{1,0:T(8,128)S(1)} collective-permute-done((f32[80,128]{1,0:T(8,128)S(1)}, f32[80,128]{1,0:T(8,128)S(1)}, u32[]{:S(2)}, u32[]{:S(2)}) %collective-permute-start.6) | collective-permute-done | bytes 40992 | tf_op jit(solution)/shard_map/ppermute | solution.py:309
  26.3 3.5 %collective-permute-done.7 = f32[80,128]{1,0:T(8,128)S(1)} collective-permute-done((f32[80,128]{1,0:T(8,128)S(1)}, f32[80,128]{1,0:T(8,128)S(1)}, u32[]{:S(2)}, u32[]{:S(2)}) %collective-permute-start.7) | collective-permute-done | bytes 40992 | tf_op jit(solution)/shard_map/ppermute | solution.py:309
  29.9 0.0 collective-permute-done.8
  29.9 3.4 %collective-permute-start.9 = (f32[80,128]{1,0:T(8,128)S(1)}, f32[80,128]{1,0:T(8,128)S(1)}, u32[]{:S(2)}, u32[]{:S(2)}) collective-permute-start(f32[80,128]{1,0:T(8,128)S(1)} %add_add_fusion), channel_id=1, source_target_pairs={{0,104},{8,96},{16,120},{24,112},{32,72},{40,64},{48,88},{56,80},{... | collective-permute-start | bytes 122888 | tf_op jit(solution)/shard_map/ppermute | solution.py:309
  33.3 2.5 %collective-permute-done.9 = f32[80,128]{1,0:T(8,128)S(1)} collective-permute-done((f32[80,128]{1,0:T(8,128)S(1)}, f32[80,128]{1,0:T(8,128)S(1)}, u32[]{:S(2)}, u32[]{:S(2)}) %collective-permute-start.9) | collective-permute-done | bytes 40992 | tf_op jit(solution)/shard_map/ppermute | solution.py:309
  35.8 0.5 %angles.1.mine_ref = f32[16,128]{1,0:T(8,128)S(1)} custom-call(s32[2,2]{1,0:T(2,128)S(1)} %copy-done.2, f32[80,128]{1,0:T(8,128)S(1)} %add.51.sums_ref), custom_call_target="tpu_custom_call" | custom-call | flops 1000000000 | bytes 1000000 | tf_op jit(solution)/shard_map/angles/pallas_call | solution.py:289
  36.3 0.4 %collective-permute-start.10 = (f32[16,128]{1,0:T(8,128)S(1)}, f32[16,128]{1,0:T(8,128)S(1)}, u32[]{:S(2)}, u32[]{:S(2)}) collective-permute-start(f32[16,128]{1,0:T(8,128)S(1)} %angles.1.mine_ref), channel_id=1, source_target_pairs={{0,8},{8,0},{16,24},{24,16},{32,40},{40,32},{48,56},{56,48},{64,72... | collective-permute-start | bytes 24584 | tf_op jit(solution)/shard_map/ppermute | solution.py:309
  36.7 0.8 %collective-permute-done.10.other_ref = f32[16,128]{1,0:T(8,128)S(1)} collective-permute-done((f32[16,128]{1,0:T(8,128)S(1)}, f32[16,128]{1,0:T(8,128)S(1)}, u32[]{:S(2)}, u32[]{:S(2)}) %collective-permute-start.10) | collective-permute-done | bytes 8224 | tf_op jit(solution)/shard_map/ppermute | solution.py:309
  37.5 1.4 %last.1 = (f32[256,512]{1,0:T(8,128)}, f32[1,512]{1,0:T(1,128)}) custom-call(s32[2,2]{1,0:T(2,128)S(1)} %copy-done.2, f32[16,128]{1,0:T(8,128)S(1)} %angles.1.mine_ref, f32[16,128]{1,0:T(8,128)S(1)} %collective-permute-done.10.other_ref, f32[256,256]{1,0:T(8,128)S(1)} %get-tuple-element.12.own_ref.first_ref, ...), custom_call_target="tpu_custom_call" | custom-call | flops 1000000000 | bytes 1000000 | tf_op jit(solution)/shard_map/last/pallas_call | solution.py:289
  (7 shorter events, 0.1 us)
Async XLA Ops:
  1.8 9.6 %collective-permute-start = (f32[256,256]{1,0:T(8,128)S(1)}, f32[256,256]{1,0:T(8,128)S(1)}, u32[]{:S(2)}, u32[]{:S(2)}) collective-permute-start(f32[256,256]{1,0:T(8,128)S(1)} %pad_maximum_fusion.1.second_raw), channel_id=1, source_target_pairs={{0,8},{1,2},{2,1},{3,4},{4,3},{5,6},{6,5},{7,15},{8,0},{9,10},{10,... | collective-permute-start | bytes 786440 | tf_op jit(solution)/shard_map/ppermute | solution.py:339
  4.3 0.7 %copy-start = (f32[512]{0:T(512)S(1)}, f32[512]{0:T(512)}, u32[]{:S(2)}) copy-start(f32[512]{0:T(512)} %param.5) | copy-start | bytes 6148
  4.3 0.7 %copy-start.2 = (s32[2,2]{1,0:T(2,128)S(1)}, s32[2,2]{1,0:T(2,128)}, u32[]{:S(2)}) copy-start(s32[2,2]{1,0:T(2,128)} %offsets.9) | copy-start | bytes 52
  4.3 0.7 %copy-start.1 = (s32[2,2]{1,0:T(2,128)S(1)}, s32[2,2]{1,0:T(2,128)}, u32[]{:S(2)}) copy-start(s32[2,2]{1,0:T(2,128)} %skip.5) | copy-start | bytes 52
  4.3 7.9 %collective-permute-start.2 = (f32[256,256]{1,0:T(8,128)S(1)}, f32[256,256]{1,0:T(8,128)S(1)}, u32[]{:S(2)}, u32[]{:S(2)}) collective-permute-start(f32[256,256]{1,0:T(8,128)S(1)} %pad_maximum_fusion.first_raw), channel_id=1, source_target_pairs={{0,1},{1,0},{2,3},{3,2},{4,5},{5,4},{6,7},{7,6},{8,9},{9,8},{10,11... | collective-permute-start | bytes 786440 | tf_op jit(solution)/shard_map/ppermute | solution.py:329
  5.7 5.8 %collective-permute-start.1 = (f32[24,128]{1,0:T(8,128)S(1)}, f32[24,128]{1,0:T(8,128)S(1)}, u32[]{:S(2)}, u32[]{:S(2)}) collective-permute-start(f32[24,128]{1,0:T(8,128)S(1)} %get-tuple-element.14.end_side._.own_side), channel_id=1, source_target_pairs={{0,8},{1,2},{2,1},{3,4},{4,3},{5,6},{6,5},{7,15},{8,0},{9,10},{10,... | collective-permute-start | bytes 36872 | tf_op jit(solution)/shard_map/ppermute | solution.py:339
  7.0 5.2 %collective-permute-start.3 = (f32[24,128]{1,0:T(8,128)S(1)}, f32[24,128]{1,0:T(8,128)S(1)}, u32[]{:S(2)}, u32[]{:S(2)}) collective-permute-start(f32[24,128]{1,0:T(8,128)S(1)} %get-tuple-element.13.own_side), channel_id=1, source_target_pairs={{0,1},{1,0},{2,3},{3,2},{4,5},{5,4},{6,7},{7,6},{8,9},{9,8},{10,11... | collective-permute-start | bytes 36872 | tf_op jit(solution)/shard_map/ppermute | solution.py:329
  13.0 2.5 %collective-permute-start.4 = (f32[80,128]{1,0:T(8,128)S(1)}, f32[80,128]{1,0:T(8,128)S(1)}, u32[]{:S(2)}, u32[]{:S(2)}) collective-permute-start(f32[80,128]{1,0:T(8,128)S(1)} %broadcast_select_fusion), channel_id=1, source_target_pairs={{0,8},{8,0},{16,24},{24,16},{32,40},{40,32},{48,56},{56,48},{64,72... | collective-permute-start | bytes 122888 | tf_op jit(solution)/shard_map/ppermute | solution.py:309
  15.5 5.1 %collective-permute-start.5 = (f32[80,128]{1,0:T(8,128)S(1)}, f32[80,128]{1,0:T(8,128)S(1)}, u32[]{:S(2)}, u32[]{:S(2)}) collective-permute-start(f32[80,128]{1,0:T(8,128)S(1)} %select_add_fusion), channel_id=1, source_target_pairs={{0,136},{8,128},{16,152},{24,144},{32,168},{40,160},{48,184},{56,1... | collective-permute-start | bytes 122888 | tf_op jit(solution)/shard_map/ppermute | solution.py:309
  20.6 5.7 %collective-permute-start.6 = (f32[80,128]{1,0:T(8,128)S(1)}, f32[80,128]{1,0:T(8,128)S(1)}, u32[]{:S(2)}, u32[]{:S(2)}) collective-permute-start(f32[80,128]{1,0:T(8,128)S(1)} %add.47), channel_id=1, source_target_pairs={{0,48},{8,56},{16,32},{24,40},{32,16},{40,24},{48,0},{56,8},{64,11... | collective-permute-start | bytes 122888 | tf_op jit(solution)/shard_map/ppermute | solution.py:309
  25.0 4.9 %collective-permute-start.7 = (f32[80,128]{1,0:T(8,128)S(1)}, f32[80,128]{1,0:T(8,128)S(1)}, u32[]{:S(2)}, u32[]{:S(2)}) collective-permute-start(f32[80,128]{1,0:T(8,128)S(1)} %add.47), channel_id=1, source_target_pairs={{0,40},{8,32},{16,56},{24,48},{32,8},{40,0},{48,24},{56,16},{64,10... | collective-permute-start | bytes 122888 | tf_op jit(solution)/shard_map/ppermute | solution.py:309
  25.0 4.9 %collective-permute-start.8 = (f32[80,128]{1,0:T(8,128)S(1)}, f32[80,128]{1,0:T(8,128)S(1)}, u32[]{:S(2)}, u32[]{:S(2)}) collective-permute-start(f32[80,128]{1,0:T(8,128)S(1)} %add.47), channel_id=1, source_target_pairs={{0,24},{8,16},{16,8},{24,0},{32,56},{40,48},{48,40},{56,32},{64,88... | collective-permute-start | bytes 122888 | tf_op jit(solution)/shard_map/ppermute | solution.py:309
  29.9 5.9 %collective-permute-start.9 = (f32[80,128]{1,0:T(8,128)S(1)}, f32[80,128]{1,0:T(8,128)S(1)}, u32[]{:S(2)}, u32[]{:S(2)}) collective-permute-start(f32[80,128]{1,0:T(8,128)S(1)} %add_add_fusion), channel_id=1, source_target_pairs={{0,104},{8,96},{16,120},{24,112},{32,72},{40,64},{48,88},{56,80},{... | collective-permute-start | bytes 122888 | tf_op jit(solution)/shard_map/ppermute | solution.py:309
  36.3 1.3 %collective-permute-start.10 = (f32[16,128]{1,0:T(8,128)S(1)}, f32[16,128]{1,0:T(8,128)S(1)}, u32[]{:S(2)}, u32[]{:S(2)}) collective-permute-start(f32[16,128]{1,0:T(8,128)S(1)} %angles.1.mine_ref), channel_id=1, source_target_pairs={{0,8},{8,0},{16,24},{24,16},{32,40},{40,32},{48,56},{56,48},{64,72... | collective-permute-start | bytes 24584 | tf_op jit(solution)/shard_map/ppermute | solution.py:309

commit v9 on v8

--- a/solution.py
+++ b/solution.py
@@ -101,7 +101,7 @@
         1e-06 * (first_norms + second_norms),
     )
     tangent = gap_sign * coupling / denominator
-    cosine = 1.0 / jnp.sqrt(1.0 + tangent * tangent)
+    cosine = lax.rsqrt(1.0 + tangent * tangent)
     return cosine, tangent * cosine
 
 

time: 39.4 us -> 39.4 us (level)
  no operation moved by 1% of the time
where the time goes in v9:
time: 39.4 us; the launch traced here: 38.9 us
  starting transfers between devices  16.6 us (42%)
  waiting for transfers between devices  15.7 us (40%)
  Pallas kernels  3.99 us (10%)
  local copies, waits for them, and re-layouts  1.68 us (4%)
  between operations  0.73 us (2%)
    ppermute x7, starting transfers between devices, swap_rows(): return lax.ppermute(x, 'rows', [(row, other(row)) for row in range(size)])  12.7 us
    ppermute x7, waiting for transfers between devices, swap_rows(): return lax.ppermute(x, 'rows', [(row, other(row)) for row in range(size)])  11.3 us
    ppermute x2, waiting for transfers between devices, swap_second(): lax.ppermute(x, ('rows', 'pairs'), [(row * pairs + at, other(row, at)) fo...  4.46 us
    pallas_call x5, Pallas kernels, call(): pl.pallas_call(kernel, out_shape=[jax.ShapeDtypeStruct(shape, jnp.float32...  3.99 us
    ppermute x2, starting transfers between devices, swap_second(): lax.ppermute(x, ('rows', 'pairs'), [(row * pairs + at, other(row, at)) fo...  3.75 us
    dynamic_slice x1, local copies, waits for them, and re-layouts, selected(): lax.dynamic_slice(loads, (0, at + half * 2 * BLOCK), (rows, BLOCK))  1.15 us
  transfers between devices with their start and end apart: 11, of which 7 were waited for; matrix products, arithmetic and copies ran while one was open for 0% of the time, Pallas kernels for 4%

profile of v9, /device:TPU:9, one launch (start us, length us, event | category | flops | bytes accessed | tf_op | source)
XLA Modules:
  0.0 38.9 jit_solution(6557330239831186102)
XLA Ops:
  0.6 1.1 %constant_dynamic-slice_fusion.1 = (f32[256,128]{1,0:T(8,128)S(1)}, f32[256,128]{1,0:T(8,128)S(1)}, f32[256,128]{1,0:T(8,128)S(1)}, f32[256,128]{1,0:T(8,128)S(1)}) fusion(f32[256,512]{1,0:T(8,128)} %param.4, s32[]{:T(128)S(6)} %select_n.36, s32[]{:T(128)S(6)} %select_n.34, s32[]{:T(128)S(6)} %select_n.33, s32[]{:T(128)S(6)} %select_n.37), kind=kLoop, calls=%fused_computation.6 | loop fusion | bytes 1048592 | tf_op jit(solution)/shard_map/dynamic_slice | solution.py:324
  1.8 2.5 %collective-permute-start = (f32[256,256]{1,0:T(8,128)S(1)}, f32[256,256]{1,0:T(8,128)S(1)}, u32[]{:S(2)}, u32[]{:S(2)}) collective-permute-start(f32[256,256]{1,0:T(8,128)S(1)} %pad_maximum_fusion.1.second_raw), channel_id=1, source_target_pairs={{0,8},{1,2},{2,1},{3,4},{4,3},{5,6},{6,5},{7,15},{8,0},{9,10},{10,... | collective-permute-start | bytes 786440 | tf_op jit(solution)/shard_map/ppermute | solution.py:339
  4.3 0.0 copy-start
  4.3 0.0 copy-start.2
  4.3 0.0 copy-start.1
  4.3 0.1 collective-permute-start.2
  4.5 0.5 %copy-done = f32[512]{0:T(512)S(1)} copy-done((f32[512]{0:T(512)S(1)}, f32[512]{0:T(512)}, u32[]{:S(2)}) %copy-start) | copy-done | bytes 2072
  5.0 0.0 copy-done.2
  5.0 0.0 copy-done.1
  5.0 0.7 %own.1 = (f32[256,256]{1,0:T(8,128)S(1)}, f32[256,256]{1,0:T(8,128)S(1)}, f32[24,128]{1,0:T(8,128)S(1)}, f32[24,128]{1,0:T(8,128)S(1)}) custom-call(s32[2,2]{1,0:T(2,128)S(1)} %copy-done.2, s32[2,2]{1,0:T(2,128)S(1)} %copy-done.1, f32[1,512]{1,0:T(1,128)S(1)} %bitcast.2, f32[256,256]{1,0:T(8,128)S(1)} %pad_maximum_fusion.first_raw, ...), custom_call_target="tpu_custom_call" | custom-call | flops 1000000000 | bytes 1000000 | tf_op jit(solution)/shard_map/own/pallas_call | solution.py:289
  5.7 1.3 %collective-permute-start.1 = (f32[24,128]{1,0:T(8,128)S(1)}, f32[24,128]{1,0:T(8,128)S(1)}, u32[]{:S(2)}, u32[]{:S(2)}) collective-permute-start(f32[24,128]{1,0:T(8,128)S(1)} %get-tuple-element.14.end_side._.own_side), channel_id=1, source_target_pairs={{0,8},{1,2},{2,1},{3,4},{4,3},{5,6},{6,5},{7,15},{8,0},{9,10},{10,... | collective-permute-start | bytes 36872 | tf_op jit(solution)/shard_map/ppermute | solution.py:339
  7.0 0.0 collective-permute-start.3
  7.0 4.5 %collective-permute-done.1.come_side = f32[24,128]{1,0:T(8,128)S(1)} collective-permute-done((f32[24,128]{1,0:T(8,128)S(1)}, f32[24,128]{1,0:T(8,128)S(1)}, u32[]{:S(2)}, u32[]{:S(2)}) %collective-permute-start.1) | collective-permute-done | bytes 12320 | tf_op jit(solution)/shard_map/ppermute | solution.py:339
  11.5 0.0 collective-permute-done.raw_ref
  11.5 0.8 %cross.2 = (f32[80,128]{1,0:T(8,128)S(1)}, f32[256,256]{1,0:T(8,128)S(1)}) custom-call(s32[2,2]{1,0:T(2,128)S(1)} %copy-done.2, s32[2,2]{1,0:T(2,128)S(1)} %copy-done.1, f32[256,256]{1,0:T(8,128)S(1)} %get-tuple-element.12.own_ref.first_ref, f32[24,128]{1,0:T(8,128)S(1)} %get-tuple-element.13.own_side, f32[256,256]{1,0:T(8,128)S(1)} %collective-permute-done.raw_ref, ...), custom_call_target="tpu_custom_call" | custom-call | flops 1000000000 | bytes 1000000 | tf_op jit(solution)/shard_map/cross/pallas_call | solution.py:289
  12.2 0.0 collective-permute-done.3.come_side
  12.2 0.0 collective-permute-done.2.raw_ref
  12.2 0.7 %cross.3 = (f32[80,128]{1,0:T(8,128)S(1)}, f32[256,256]{1,0:T(8,128)S(1)}) custom-call(s32[2,2]{1,0:T(2,128)S(1)} %copy-done.2, s32[2,2]{1,0:T(2,128)S(1)} %copy-done.1, f32[256,256]{1,0:T(8,128)S(1)} %get-tuple-element.15.end_ref.own_ref.second_ref, f32[24,128]{1,0:T(8,128)S(1)} %get-tuple-element.14.end_side._.own_side, ...), custom_call_target="tpu_custom_call" | custom-call | flops 1000000000 | bytes 1000000 | tf_op jit(solution)/shard_map/cross/pallas_call | solution.py:289
  13.0 1.6 %collective-permute-start.4 = (f32[80,128]{1,0:T(8,128)S(1)}, f32[80,128]{1,0:T(8,128)S(1)}, u32[]{:S(2)}, u32[]{:S(2)}) collective-permute-start(f32[80,128]{1,0:T(8,128)S(1)} %broadcast_select_fusion), channel_id=1, source_target_pairs={{0,8},{8,0},{16,24},{24,16},{32,40},{40,32},{48,56},{56,48},{64,72... | collective-permute-start | bytes 122888 | tf_op jit(solution)/shard_map/ppermute | solution.py:309
  14.6 0.9 %collective-permute-done.4 = f32[80,128]{1,0:T(8,128)S(1)} collective-permute-done((f32[80,128]{1,0:T(8,128)S(1)}, f32[80,128]{1,0:T(8,128)S(1)}, u32[]{:S(2)}, u32[]{:S(2)}) %collective-permute-start.4) | collective-permute-done | bytes 40992 | tf_op jit(solution)/shard_map/ppermute | solution.py:309
  15.5 2.3 %collective-permute-start.5 = (f32[80,128]{1,0:T(8,128)S(1)}, f32[80,128]{1,0:T(8,128)S(1)}, u32[]{:S(2)}, u32[]{:S(2)}) collective-permute-start(f32[80,128]{1,0:T(8,128)S(1)} %select_add_fusion), channel_id=1, source_target_pairs={{0,136},{8,128},{16,152},{24,144},{32,168},{40,160},{48,184},{56,1... | collective-permute-start | bytes 122888 | tf_op jit(solution)/shard_map/ppermute | solution.py:309
  17.8 2.8 %collective-permute-done.5 = f32[80,128]{1,0:T(8,128)S(1)} collective-permute-done((f32[80,128]{1,0:T(8,128)S(1)}, f32[80,128]{1,0:T(8,128)S(1)}, u32[]{:S(2)}, u32[]{:S(2)}) %collective-permute-start.5) | collective-permute-done | bytes 40992 | tf_op jit(solution)/shard_map/ppermute | solution.py:309
  20.6 4.3 %collective-permute-start.6 = (f32[80,128]{1,0:T(8,128)S(1)}, f32[80,128]{1,0:T(8,128)S(1)}, u32[]{:S(2)}, u32[]{:S(2)}) collective-permute-start(f32[80,128]{1,0:T(8,128)S(1)} %add.47), channel_id=1, source_target_pairs={{0,48},{8,56},{16,32},{24,40},{32,16},{40,24},{48,0},{56,8},{64,11... | collective-permute-start | bytes 122888 | tf_op jit(solution)/shard_map/ppermute | solution.py:309
  25.0 0.0 collective-permute-start.7
  25.0 0.7 %collective-permute-start.8 = (f32[80,128]{1,0:T(8,128)S(1)}, f32[80,128]{1,0:T(8,128)S(1)}, u32[]{:S(2)}, u32[]{:S(2)}) collective-permute-start(f32[80,128]{1,0:T(8,128)S(1)} %add.47), channel_id=1, source_target_pairs={{0,24},{8,16},{16,8},{24,0},{32,56},{40,48},{48,40},{56,32},{64,88... | collective-permute-start | bytes 122888 | tf_op jit(solution)/shard_map/ppermute | solution.py:309
  25.6 0.7 %collective-permute-done.6 = f32[80,128]{1,0:T(8,128)S(1)} collective-permute-done((f32[80,128]{1,0:T(8,128)S(1)}, f32[80,128]{1,0:T(8,128)S(1)}, u32[]{:S(2)}, u32[]{:S(2)}) %collective-permute-start.6) | collective-permute-done | bytes 40992 | tf_op jit(solution)/shard_map/ppermute | solution.py:309
  26.3 3.5 %collective-permute-done.7 = f32[80,128]{1,0:T(8,128)S(1)} collective-permute-done((f32[80,128]{1,0:T(8,128)S(1)}, f32[80,128]{1,0:T(8,128)S(1)}, u32[]{:S(2)}, u32[]{:S(2)}) %collective-permute-start.7) | collective-permute-done | bytes 40992 | tf_op jit(solution)/shard_map/ppermute | solution.py:309
  29.9 0.0 collective-permute-done.8
  29.9 3.4 %collective-permute-start.9 = (f32[80,128]{1,0:T(8,128)S(1)}, f32[80,128]{1,0:T(8,128)S(1)}, u32[]{:S(2)}, u32[]{:S(2)}) collective-permute-start(f32[80,128]{1,0:T(8,128)S(1)} %add_add_fusion), channel_id=1, source_target_pairs={{0,104},{8,96},{16,120},{24,112},{32,72},{40,64},{48,88},{56,80},{... | collective-permute-start | bytes 122888 | tf_op jit(solution)/shard_map/ppermute | solution.py:309
  33.3 2.5 %collective-permute-done.9 = f32[80,128]{1,0:T(8,128)S(1)} collective-permute-done((f32[80,128]{1,0:T(8,128)S(1)}, f32[80,128]{1,0:T(8,128)S(1)}, u32[]{:S(2)}, u32[]{:S(2)}) %collective-permute-start.9) | collective-permute-done | bytes 40992 | tf_op jit(solution)/shard_map/ppermute | solution.py:309
  35.8 0.5 %angles.1.mine_ref = f32[16,128]{1,0:T(8,128)S(1)} custom-call(s32[2,2]{1,0:T(2,128)S(1)} %copy-done.2, f32[80,128]{1,0:T(8,128)S(1)} %add.51.sums_ref), custom_call_target="tpu_custom_call" | custom-call | flops 1000000000 | bytes 1000000 | tf_op jit(solution)/shard_map/angles/pallas_call | solution.py:289
  36.3 0.4 %collective-permute-start.10 = (f32[16,128]{1,0:T(8,128)S(1)}, f32[16,128]{1,0:T(8,128)S(1)}, u32[]{:S(2)}, u32[]{:S(2)}) collective-permute-start(f32[16,128]{1,0:T(8,128)S(1)} %angles.1.mine_ref), channel_id=1, source_target_pairs={{0,8},{8,0},{16,24},{24,16},{32,40},{40,32},{48,56},{56,48},{64,72... | collective-permute-start | bytes 24584 | tf_op jit(solution)/shard_map/ppermute | solution.py:309
  36.7 0.8 %collective-permute-done.10.other_ref = f32[16,128]{1,0:T(8,128)S(1)} collective-permute-done((f32[16,128]{1,0:T(8,128)S(1)}, f32[16,128]{1,0:T(8,128)S(1)}, u32[]{:S(2)}, u32[]{:S(2)}) %collective-permute-start.10) | collective-permute-done | bytes 8224 | tf_op jit(solution)/shard_map/ppermute | solution.py:309
  37.5 1.4 %last.1 = (f32[256,512]{1,0:T(8,128)}, f32[1,512]{1,0:T(1,128)}) custom-call(s32[2,2]{1,0:T(2,128)S(1)} %copy-done.2, f32[16,128]{1,0:T(8,128)S(1)} %angles.1.mine_ref, f32[16,128]{1,0:T(8,128)S(1)} %collective-permute-done.10.other_ref, f32[256,256]{1,0:T(8,128)S(1)} %get-tuple-element.12.own_ref.first_ref, ...), custom_call_target="tpu_custom_call" | custom-call | flops 1000000000 | bytes 1000000 | tf_op jit(solution)/shard_map/last/pallas_call | solution.py:289
  (7 shorter events, 0.1 us)
Async XLA Ops:
  1.8 9.6 %collective-permute-start = (f32[256,256]{1,0:T(8,128)S(1)}, f32[256,256]{1,0:T(8,128)S(1)}, u32[]{:S(2)}, u32[]{:S(2)}) collective-permute-start(f32[256,256]{1,0:T(8,128)S(1)} %pad_maximum_fusion.1.second_raw), channel_id=1, source_target_pairs={{0,8},{1,2},{2,1},{3,4},{4,3},{5,6},{6,5},{7,15},{8,0},{9,10},{10,... | collective-permute-start | bytes 786440 | tf_op jit(solution)/shard_map/ppermute | solution.py:339
  4.3 0.7 %copy-start = (f32[512]{0:T(512)S(1)}, f32[512]{0:T(512)}, u32[]{:S(2)}) copy-start(f32[512]{0:T(512)} %param.5) | copy-start | bytes 6148
  4.3 0.7 %copy-start.2 = (s32[2,2]{1,0:T(2,128)S(1)}, s32[2,2]{1,0:T(2,128)}, u32[]{:S(2)}) copy-start(s32[2,2]{1,0:T(2,128)} %offsets.9) | copy-start | bytes 52
  4.3 0.7 %copy-start.1 = (s32[2,2]{1,0:T(2,128)S(1)}, s32[2,2]{1,0:T(2,128)}, u32[]{:S(2)}) copy-start(s32[2,2]{1,0:T(2,128)} %skip.5) | copy-start | bytes 52
  4.3 7.9 %collective-permute-start.2 = (f32[256,256]{1,0:T(8,128)S(1)}, f32[256,256]{1,0:T(8,128)S(1)}, u32[]{:S(2)}, u32[]{:S(2)}) collective-permute-start(f32[256,256]{1,0:T(8,128)S(1)} %pad_maximum_fusion.first_raw), channel_id=1, source_target_pairs={{0,1},{1,0},{2,3},{3,2},{4,5},{5,4},{6,7},{7,6},{8,9},{9,8},{10,11... | collective-permute-start | bytes 786440 | tf_op jit(solution)/shard_map/ppermute | solution.py:329
  5.7 5.8 %collective-permute-start.1 = (f32[24,128]{1,0:T(8,128)S(1)}, f32[24,128]{1,0:T(8,128)S(1)}, u32[]{:S(2)}, u32[]{:S(2)}) collective-permute-start(f32[24,128]{1,0:T(8,128)S(1)} %get-tuple-element.14.end_side._.own_side), channel_id=1, source_target_pairs={{0,8},{1,2},{2,1},{3,4},{4,3},{5,6},{6,5},{7,15},{8,0},{9,10},{10,... | collective-permute-start | bytes 36872 | tf_op jit(solution)/shard_map/ppermute | solution.py:339
  7.0 5.2 %collective-permute-start.3 = (f32[24,128]{1,0:T(8,128)S(1)}, f32[24,128]{1,0:T(8,128)S(1)}, u32[]{:S(2)}, u32[]{:S(2)}) collective-permute-start(f32[24,128]{1,0:T(8,128)S(1)} %get-tuple-element.13.own_side), channel_id=1, source_target_pairs={{0,1},{1,0},{2,3},{3,2},{4,5},{5,4},{6,7},{7,6},{8,9},{9,8},{10,11... | collective-permute-start | bytes 36872 | tf_op jit(solution)/shard_map/ppermute | solution.py:329
  13.0 2.5 %collective-permute-start.4 = (f32[80,128]{1,0:T(8,128)S(1)}, f32[80,128]{1,0:T(8,128)S(1)}, u32[]{:S(2)}, u32[]{:S(2)}) collective-permute-start(f32[80,128]{1,0:T(8,128)S(1)} %broadcast_select_fusion), channel_id=1, source_target_pairs={{0,8},{8,0},{16,24},{24,16},{32,40},{40,32},{48,56},{56,48},{64,72... | collective-permute-start | bytes 122888 | tf_op jit(solution)/shard_map/ppermute | solution.py:309
  15.5 5.1 %collective-permute-start.5 = (f32[80,128]{1,0:T(8,128)S(1)}, f32[80,128]{1,0:T(8,128)S(1)}, u32[]{:S(2)}, u32[]{:S(2)}) collective-permute-start(f32[80,128]{1,0:T(8,128)S(1)} %select_add_fusion), channel_id=1, source_target_pairs={{0,136},{8,128},{16,152},{24,144},{32,168},{40,160},{48,184},{56,1... | collective-permute-start | bytes 122888 | tf_op jit(solution)/shard_map/ppermute | solution.py:309
  20.6 5.7 %collective-permute-start.6 = (f32[80,128]{1,0:T(8,128)S(1)}, f32[80,128]{1,0:T(8,128)S(1)}, u32[]{:S(2)}, u32[]{:S(2)}) collective-permute-start(f32[80,128]{1,0:T(8,128)S(1)} %add.47), channel_id=1, source_target_pairs={{0,48},{8,56},{16,32},{24,40},{32,16},{40,24},{48,0},{56,8},{64,11... | collective-permute-start | bytes 122888 | tf_op jit(solution)/shard_map/ppermute | solution.py:309
  25.0 4.9 %collective-permute-start.7 = (f32[80,128]{1,0:T(8,128)S(1)}, f32[80,128]{1,0:T(8,128)S(1)}, u32[]{:S(2)}, u32[]{:S(2)}) collective-permute-start(f32[80,128]{1,0:T(8,128)S(1)} %add.47), channel_id=1, source_target_pairs={{0,40},{8,32},{16,56},{24,48},{32,8},{40,0},{48,24},{56,16},{64,10... | collective-permute-start | bytes 122888 | tf_op jit(solution)/shard_map/ppermute | solution.py:309
  25.0 4.9 %collective-permute-start.8 = (f32[80,128]{1,0:T(8,128)S(1)}, f32[80,128]{1,0:T(8,128)S(1)}, u32[]{:S(2)}, u32[]{:S(2)}) collective-permute-start(f32[80,128]{1,0:T(8,128)S(1)} %add.47), channel_id=1, source_target_pairs={{0,24},{8,16},{16,8},{24,0},{32,56},{40,48},{48,40},{56,32},{64,88... | collective-permute-start | bytes 122888 | tf_op jit(solution)/shard_map/ppermute | solution.py:309
  29.9 5.9 %collective-permute-start.9 = (f32[80,128]{1,0:T(8,128)S(1)}, f32[80,128]{1,0:T(8,128)S(1)}, u32[]{:S(2)}, u32[]{:S(2)}) collective-permute-start(f32[80,128]{1,0:T(8,128)S(1)} %add_add_fusion), channel_id=1, source_target_pairs={{0,104},{8,96},{16,120},{24,112},{32,72},{40,64},{48,88},{56,80},{... | collective-permute-start | bytes 122888 | tf_op jit(solution)/shard_map/ppermute | solution.py:309
  36.3 1.3 %collective-permute-start.10 = (f32[16,128]{1,0:T(8,128)S(1)}, f32[16,128]{1,0:T(8,128)S(1)}, u32[]{:S(2)}, u32[]{:S(2)}) collective-permute-start(f32[16,128]{1,0:T(8,128)S(1)} %angles.1.mine_ref), channel_id=1, source_target_pairs={{0,8},{8,0},{16,24},{24,16},{32,40},{40,32},{48,56},{56,48},{64,72... | collective-permute-start | bytes 24584 | tf_op jit(solution)/shard_map/ppermute | solution.py:309
